TPU v7x, 512 devices: a whole 4x8x8 slice. The times are simulated.
512 devices in a mesh: bx: 32 (over z_hi, y, core), by: 16 (over x, z_lo).
Axes of the slice: x: 4, y: 8, z: 8 (z_hi: 2, z_lo: 4; z = z_hi * 4 + z_lo), core: 2. Of those that a mesh axis runs over, the one named last changes fastest.
Arguments:
- interface_velocity: float32 [3, 2048, 2048], P(None, 'bx', 'by'), may hold values from -6 to 6
- history: float32 [6, 2, 3, 64, 32, 16, 128], P(None, None, None, 'by', 'bx'), may hold values from -6 to 6
- kernel: float32 [7, 64, 32, 16, 128], P(None, 'by', 'bx'), may hold values from -6 to 6
- velocity: float32 [3, 4, 2048, 2048], P(None, None, 'bx', 'by'), may hold values from -6 to 6
- stress: float32 [6, 4, 2048, 2048], P(None, None, 'bx', 'by'), may hold values from -6 to 6
- cohesion: float32 [4, 2048, 2048], P(None, 'bx', 'by'), may hold values from 0.5 to 4
Outputs:
- velocity_new: float32 [3, 4, 2048, 2048], P(None, None, 'bx', 'by')
- stress_new: float32 [6, 4, 2048, 2048], P(None, None, 'bx', 'by')
All inputs are finite; a program needn't handle non-finite values.
Results may differ from a plain program's by a relative error of at most 0.00005.
Values sent between devices are 32-bit elements; how exact they have to be, the bound alone decides.
No kernel may reach another device: no remote copies, remote signals or barrier semaphores. Data moves between devices by JAX's collectives and lax.ppermute only.
A program may use at most 64 MiB of HBM per device.

v0:
```python
from functools import partial
import math

import jax
import jax.numpy as jnp
from jax import lax
from jax.sharding import PartitionSpec as P

COURANT = 0.3
FRICTION = 0.6
HIGHEST = lax.Precision.HIGHEST


def extended(block, sides, width):
    for axis, dim in sides:
        count = lax.axis_size(axis)
        forward = [(i, i + 1) for i in range(count - 1)]
        forward.append((count - 1, 0))
        backward = [(target, source) for source, target in forward]
        low = lax.ppermute(
            lax.slice_in_dim(block, block.shape[dim] - width, None, axis=dim), axis, forward
        )
        high = lax.ppermute(lax.slice_in_dim(block, 0, width, axis=dim), axis, backward)
        block = jnp.concatenate([low, block, high], axis=dim)
    return block


def counting(count):
    return jnp.arange(count, dtype=jnp.int32)


def phase_table(row_index, col_index, length, sign):
    product = row_index[:, None] * col_index[None, :] % length
    angle = 2.0 * math.pi / length * product.astype(jnp.float32)
    return (jnp.cos(angle), sign * jnp.sin(angle))


def conjugate(table):
    return (table[0], -table[1])


def complex_apply(pattern, real_part, imag_part, table):
    contract = partial(jnp.einsum, pattern, precision=HIGHEST)
    return (
        contract(real_part, table[0]) - contract(imag_part, table[1]),
        contract(real_part, table[1]) + contract(imag_part, table[0]),
    )


def twist(real_part, imag_part, table_real, table_imag):
    return (
        real_part * table_real - imag_part * table_imag,
        real_part * table_imag + imag_part * table_real,
    )


def dip_blocks(block):
    return lax.all_to_all(block, "by", split_axis=2, concat_axis=2, tiled=True)


def strike_modes(block):
    return lax.all_to_all(block, "bx", split_axis=4, concat_axis=4, tiled=True)


def widen(fields):
    return extended(fields, (("bx", 2), ("by", 3)), 1)


def strike_diff(padded):
    return 0.5 * (padded[..., 2:, 1:-1] - padded[..., :-2, 1:-1])


def dip_diff(padded):
    return 0.5 * (padded[..., 1:-1, 2:] - padded[..., 1:-1, :-2])


def depth_diff(layered, ghost_layer):
    above_layer = jnp.concatenate([layered[1:], jnp.zeros_like(layered[:1])], axis=0)
    below_layer = jnp.concatenate([ghost_layer[None], layered[:-1]], axis=0)
    return 0.5 * (above_layer - below_layer)


def yield_limit(trial_stress, cohesion):
    pressure = (trial_stress[0] + trial_stress[1] + trial_stress[2]) / 3.0
    normal_dev = trial_stress[:3] - pressure[None]
    second = 0.5 * jnp.sum(normal_dev * normal_dev, axis=0) + jnp.sum(
        trial_stress[3:] * trial_stress[3:], axis=0
    )
    shear_stress = jnp.sqrt(second)
    yield_stress = cohesion + FRICTION * jnp.maximum(-pressure, 0.0)
    factor = yield_stress / jnp.maximum(shear_stress, yield_stress)
    return jnp.concatenate(
        [pressure[None] + factor[None] * normal_dev, factor[None] * trial_stress[3:]], axis=0
    )


def advance_bulk(velocity, stress, traction, interface_velocity, cohesion):
    padded_stress = widen(stress)
    forcing = jnp.stack(
        [
            strike_diff(padded_stress[0])
            + dip_diff(padded_stress[3])
            + depth_diff(stress[4], traction[0]),
            strike_diff(padded_stress[3])
            + dip_diff(padded_stress[1])
            + depth_diff(stress[5], traction[1]),
            strike_diff(padded_stress[4])
            + dip_diff(padded_stress[5])
            + depth_diff(stress[2], traction[2]),
        ]
    )
    velocity_new = velocity + COURANT * forcing
    padded_velocity = widen(velocity_new)
    strike_grad = strike_diff(padded_velocity)
    dip_grad = dip_diff(padded_velocity)
    depth_grad = jnp.stack(
        [
            depth_diff(velocity_new[component], interface_velocity[component])
            for component in range(3)
        ]
    )
    dilation = strike_grad[0] + dip_grad[1] + depth_grad[2]
    rates = jnp.stack(
        [
            dilation + 2.0 * strike_grad[0],
            dilation + 2.0 * dip_grad[1],
            dilation + 2.0 * depth_grad[2],
            dip_grad[0] + strike_grad[1],
            depth_grad[0] + strike_grad[2],
            depth_grad[1] + dip_grad[2],
        ]
    )
    trial_stress = stress + COURANT * rates
    return (velocity_new, yield_limit(trial_stress, cohesion))


def local(interface_velocity, history, kernel, velocity, stress, cohesion):
    strike_count = lax.axis_size("bx")
    dip_count = lax.axis_size("by")
    strike_index = lax.axis_index("bx")
    strike_cells = interface_velocity.shape[1]
    dip_cells = interface_velocity.shape[2]
    row_block = dip_cells // strike_count
    mode_block = strike_cells // dip_count
    strike_length = strike_cells * strike_count
    dip_length = dip_cells * dip_count
    scale = 1.0 / math.sqrt(strike_length * dip_length)
    strike_table = phase_table(counting(strike_count), counting(strike_count), strike_count, -1.0)
    strike_twist = phase_table(counting(strike_cells), counting(strike_count), strike_length, -1.0)
    cell_table = phase_table(counting(strike_cells), counting(strike_cells), strike_cells, -1.0)
    dip_table = phase_table(counting(dip_count), counting(dip_count), dip_count, -1.0)
    column_table = phase_table(counting(dip_cells), counting(dip_cells), dip_cells, -1.0)
    gathered = lax.all_gather(interface_velocity, "bx", axis=1, tiled=True)
    own_columns = lax.dynamic_slice_in_dim(gathered, strike_index * row_block, row_block, 2)
    grouped = own_columns.reshape(3, strike_count, strike_cells, row_block)
    first_pattern = "cpqr,pk->cqkr"
    real_part = jnp.einsum(first_pattern, grouped, strike_table[0], precision=HIGHEST)
    imag_part = jnp.einsum(first_pattern, grouped, strike_table[1], precision=HIGHEST)
    real_part, imag_part = twist(
        real_part, imag_part, strike_twist[0][None, :, :, None], strike_twist[1][None, :, :, None]
    )
    real_part, imag_part = complex_apply("cqkr,qm->cmkr", real_part, imag_part, cell_table)
    stacked = jnp.stack([real_part, imag_part])
    dip_offsets = row_block * strike_index + counting(row_block)
    dip_twist = phase_table(counting(dip_count), dip_offsets, dip_length, -1.0)
    arrived = dip_blocks(stacked.reshape(2, 3, strike_cells, dip_cells))
    arrived = arrived.reshape(2, 3, dip_count, mode_block, strike_count, row_block)
    real_part, imag_part = complex_apply("cjukr,jl->clukr", arrived[0], arrived[1], dip_table)
    real_part, imag_part = twist(
        real_part,
        imag_part,
        dip_twist[0][None, :, None, None, :],
        dip_twist[1][None, :, None, None, :],
    )
    arrived = strike_modes(
        jnp.stack([real_part, imag_part]).reshape(2, 3, dip_count, mode_block, dip_cells)
    )
    real_part, imag_part = (arrived[0], arrived[1])
    real_part, imag_part = complex_apply("clus,sm->culm", real_part, imag_part, column_table)
    spectrum = scale * jnp.stack([real_part, imag_part])[:, :, :, None]
    past_terms = jnp.einsum("hupks,hzcupks->zcupks", kernel[1:], history, precision=HIGHEST)
    response = kernel[0][None, None] * spectrum + past_terms
    real_part, imag_part = complex_apply(
        "cuks,sm->ckum", response[0, :, :, 0], response[1, :, :, 0], conjugate(column_table)
    )
    dip_offsets = row_block * strike_index + counting(row_block)
    back_twist = conjugate(phase_table(counting(dip_count), dip_offsets, dip_length, -1.0))
    arrived = strike_modes(jnp.stack([real_part, imag_part]))
    arrived = arrived.reshape(2, 3, dip_count, mode_block, strike_count, row_block)
    real_part, imag_part = twist(
        arrived[0],
        arrived[1],
        back_twist[0][None, :, None, None, :],
        back_twist[1][None, :, None, None, :],
    )
    real_part, imag_part = complex_apply(
        "clukr,lj->cjukr", real_part, imag_part, conjugate(dip_table)
    )
    arrived = dip_blocks(jnp.stack([real_part, imag_part]).reshape(2, 3, strike_cells, dip_cells))
    arrived = arrived.reshape(2, 3, strike_cells, strike_count, row_block)
    real_part, imag_part = complex_apply(
        "cmkr,mq->cqkr", arrived[0], arrived[1], conjugate(cell_table)
    )
    back_strike = conjugate(strike_twist)
    real_part, imag_part = twist(
        real_part, imag_part, back_strike[0][None, :, :, None], back_strike[1][None, :, :, None]
    )
    inverse_table = conjugate(strike_table)
    spatial = jnp.einsum(
        "cqkr,kp->cpqr", real_part, inverse_table[0], precision=HIGHEST
    ) - jnp.einsum("cqkr,kp->cpqr", imag_part, inverse_table[1], precision=HIGHEST)
    gathered = lax.all_gather(
        spatial.reshape(3, strike_length, row_block), "bx", axis=2, tiled=True
    )
    traction = scale * lax.dynamic_slice_in_dim(
        gathered, strike_index * strike_cells, strike_cells, 1
    )
    velocity_new, stress_new = advance_bulk(
        velocity, stress, traction, interface_velocity, cohesion
    )
    return (velocity_new, stress_new)


def solution(mesh):
    return jax.shard_map(
        local,
        mesh=mesh,
        in_specs=(
            P(None, "bx", "by"),
            P(None, None, None, "by", "bx", None, None),
            P(None, "by", "bx", None, None),
            P(None, None, "bx", "by"),
            P(None, None, "bx", "by"),
            P(None, "bx", "by"),
        ),
        out_specs=(P(None, None, "bx", "by"), P(None, None, "bx", "by")),
        check_vma=False,
    )
```

profile of v0, /device:TPU:6, one launch (start us, length us, event | category | flops | bytes accessed | tf_op | source)
XLA Modules:
  0.0 401.7 jit_solution(16210227547957793094)
XLA Ops:
  8.0 108.7 %all-gather.3.cloned.1.call-done = f32[3,2048,128]{2,1,0:T(8,128)} async-done(((f32[3,64,128]{2,1,0:T(8,128)}), f32[3,2048,128]{2,1,0:T(8,128)}) %all-gather.3.cloned.1.call-update) | async-done | bytes 3145744 | tf_op jit(solution)/shard_map/all_gather | solution.py:153
  116.7 2.8 constant_dynamic-slice_fusion
  124.5 5.6 %all-to-all-start = ((f32[2,3,64,128]{3,0,1,2:T(2,128)}), f32[2,3,64,128]{3,0,1,2:T(2,128)S(1)}, u32[]{:S(2)}, u32[]{:S(2)}) async-start(f32[2,3,64,128]{3,0,1,2:T(2,128)} %copy.159), calls=%async_computation | async-start | bytes 393216 | tf_op jit(solution)/shard_map/all_to_all | solution.py:58
  131.5 6.1 %all-to-all-done = f32[2,3,64,128]{3,0,1,2:T(2,128)S(1)} async-done(((f32[2,3,64,128]{3,0,1,2:T(2,128)}), f32[2,3,64,128]{3,0,1,2:T(2,128)S(1)}, u32[]{:S(2)}, u32[]{:S(2)}) %all-to-all-start) | async-done | bytes 196640 | tf_op jit(solution)/shard_map/all_to_all | solution.py:58
  138.7 3.4 reshape.256
  146.2 4.2 %reshape.257 = f32[3,16,4,32,4]{4,3,0,2,1:T(8,128)S(1)} reshape(f32[3,64,128]{2,0,1:T(4,128)} %get-tuple-element.10) | data formatting | bytes 196608 | tf_op jit(solution)/shard_map/squeeze | solution.py:168
  157.1 1.9 reshape.260
  159.0 6.0 %all-to-all-start.1 = ((f32[32,1,1536]{2,1,0:T(1,128)}), f32[32,1,1536]{2,1,0:T(1,128)S(1)}, u32[]{:S(2)}, u32[]{:S(2)}) async-start(f32[32,1,1536]{2,1,0:T(1,128)} %reshape.260), calls=%async_computation.1 | async-start | bytes 393216 | tf_op jit(solution)/shard_map/all_to_all | solution.py:62
  166.5 14.2 %all-to-all-done.1 = f32[32,1,1536]{2,1,0:T(1,128)S(1)} async-done(((f32[32,1,1536]{2,1,0:T(1,128)}), f32[32,1,1536]{2,1,0:T(1,128)S(1)}, u32[]{:S(2)}, u32[]{:S(2)}) %all-to-all-start.1) | async-done | bytes 196640 | tf_op jit(solution)/shard_map/all_to_all | solution.py:62
  190.4 19.2 %all_to_all.20 = f32[32,1,1536]{2,1,0:T(1,128)S(1)} all-to-all(f32[32,1,1536]{2,1,0:T(1,128)S(1)} %reshape.262), channel_id=1, replica_groups=mesh['bx'=32,'by'=16] {'bx'}, dimensions={0} | all-to-all | bytes 393216 | tf_op jit(solution)/shard_map/all_to_all | solution.py:62
  216.6 2.2 copy.176
  218.8 3.2 stack.88
  225.0 2.6 stack.89
  228.4 5.8 %all-to-all-start.3 = ((f32[2,3,64,128]{3,0,1,2:T(2,128)}), f32[2,3,64,128]{3,0,1,2:T(2,128)S(1)}, u32[]{:S(2)}, u32[]{:S(2)}) async-start(f32[2,3,64,128]{3,0,1,2:T(2,128)} %copy.180), calls=%async_computation.3 | async-start | bytes 393216 | tf_op jit(solution)/shard_map/all_to_all | solution.py:58
  234.5 6.4 %all-to-all-done.3 = f32[2,3,64,128]{3,0,1,2:T(2,128)S(1)} async-done(((f32[2,3,64,128]{3,0,1,2:T(2,128)}), f32[2,3,64,128]{3,0,1,2:T(2,128)S(1)}, u32[]{:S(2)}, u32[]{:S(2)}) %all-to-all-start.3) | async-done | bytes 196640 | tf_op jit(solution)/shard_map/all_to_all | solution.py:58
  244.8 1.9 collective-permute-start
  246.8 9.7 %collective-permute-start.1 = (f32[6,4,1,128]{3,1,2,0:T(4,128)S(1)}, f32[6,4,1,128]{3,1,2,0:T(4,128)S(1)}, u32[]{:S(2)}, u32[]{:S(2)}) collective-permute-start(f32[6,4,1,128]{3,1,2,0:T(4,128)S(1)} %bitcast.319), channel_id=1, source_target_pairs={{16,0},{32,16},{48,32},{64,48},{80,64},{96,80},{112,96},{128,112},... | collective-permute-start | bytes 36872 | tf_op jit(solution)/shard_map/ppermute | solution.py:23
  260.3 2.7 collective-permute-start.2
  263.0 5.9 %collective-permute-start.3 = (f32[6,4,66,1]{2,1,3,0:T(4,128)S(1)}, f32[6,4,66,1]{2,1,3,0:T(4,128)S(1)}, u32[]{:S(2)}, u32[]{:S(2)}) collective-permute-start(f32[6,4,66,1]{2,1,3,0:T(4,128)S(1)} %get-tuple-element.20), channel_id=1, source_target_pairs={{1,0},{2,1},{3,2},{4,3},{5,4},{6,5},{7,6},{8,7},{9,8},{10,9},{11,1... | collective-permute-start | bytes 19016 | tf_op jit(solution)/shard_map/ppermute | solution.py:23
  270.1 2.1 copy.193
  272.3 2.5 maximum_bitcast_fusion.2
  274.7 1.8 maximum_bitcast_fusion.3
  276.6 68.3 %all-gather.5.cloned.1.call-done = f32[3,2048,128]{1,0,2:T(4,128)} async-done(((f32[3,2048,4]{1,0,2:T(4,128)}), f32[3,2048,128]{1,0,2:T(4,128)}) %all-gather.5.cloned.1.call-update) | async-done | bytes 3145744 | tf_op jit(solution)/shard_map/all_gather | solution.py:212
  346.1 1.9 fusion.27
  352.4 1.9 collective-permute-start.4
  355.2 2.4 collective-permute-start.5
  359.7 6.7 %collective-permute-done.5 = f32[3,4,1,128]{3,1,2,0:T(4,128)} collective-permute-done((f32[3,4,1,128]{3,1,2,0:T(4,128)}, f32[3,4,1,128]{3,1,2,0:T(4,128)}, u32[]{:S(2)}, u32[]{:S(2)}) %collective-permute-start.5) | collective-permute-done | bytes 6176 | tf_op jit(solution)/shard_map/ppermute | solution.py:20
  366.5 1.9 copy.197
  369.7 5.9 %collective-permute-start.6 = (f32[3,4,66,1]{2,1,3,0:T(4,128)}, f32[3,4,66,1]{2,1,3,0:T(4,128)S(1)}, u32[]{:S(2)}, u32[]{:S(2)}) collective-permute-start(f32[3,4,66,1]{2,1,3,0:T(4,128)} %get-tuple-element.23), channel_id=1, source_target_pairs={{1,0},{2,1},{3,2},{4,3},{5,4},{6,5},{7,6},{8,7},{9,8},{10,9},{11,1... | collective-permute-start | bytes 9512 | tf_op jit(solution)/shard_map/ppermute | solution.py:23
  375.6 2.1 collective-permute-start.7
  379.9 4.1 %collective-permute-done.7 = f32[3,4,66,1]{2,1,3,0:T(4,128)S(1)} collective-permute-done((f32[3,4,66,1]{2,1,3,0:T(4,128)}, f32[3,4,66,1]{2,1,3,0:T(4,128)S(1)}, u32[]{:S(2)}, u32[]{:S(2)}) %collective-permute-start.7) | collective-permute-done | bytes 3200 | tf_op jit(solution)/shard_map/ppermute | solution.py:20
  384.1 4.8 %fusion.11 = (f32[3,4,64,128]{2,1,3,0:T(4,128)S(1)}, f32[3,4,64,128]{2,1,3,0:T(4,128)S(1)}) fusion(f32[3,4,66,1]{2,1,3,0:T(4,128)S(1)} %collective-permute-done.7, f32[3,4,1,128]{2,1,3,0:T(4,128)S(1)} %copy.195, f32[3,4,64,128]{2,1,3,0:T(4,128)S(1)} %fusion.14, f32[3,4,1,128]{2,1,3,0:T(4,128)} %copy.197, f32[3,4,66,1]{2,1,3,0:T(4,128)S(1)} %collective-permute-done.6), kind=kLoop, calls=%fused_computation.32 | loop fusion | flops 1179648 | bytes 1198272 | tf_op jit(solution)/shard_map/mul | solution.py:74
  (170 shorter events, 67.8 us)
Async XLA Ops:
  7.2 109.5 %all-gather.3.cloned.1.call-start = ((), (), s32[]{:S(2)}) async-start(), calls=%async_computation.4 | async-start | bytes 3244032 | tf_op jit(solution)/shard_map/all_gather | solution.py:153
  123.0 7.8 %copy-start.20 = (f32[7,4,1,16,128]{4,3,2,1,0:T(8,128)S(1)}, f32[7,4,1,16,128]{4,3,2,1,0:T(8,128)}, u32[]{:S(2)}) copy-start(f32[7,4,1,16,128]{4,3,2,1,0:T(8,128)} %param.8) | copy-start | bytes 688132
  124.5 13.1 %all-to-all-start = ((f32[2,3,64,128]{3,0,1,2:T(2,128)}), f32[2,3,64,128]{3,0,1,2:T(2,128)S(1)}, u32[]{:S(2)}, u32[]{:S(2)}) async-start(f32[2,3,64,128]{3,0,1,2:T(2,128)} %copy.159), calls=%async_computation | async-start | bytes 393216 | tf_op jit(solution)/shard_map/all_to_all | solution.py:58
  157.1 7.9 %copy-start.5 = (f32[6,2,3,4,1,16,128]{6,5,4,3,2,1,0:T(8,128)S(1)}, f32[6,2,3,4,1,16,128]{6,5,4,3,2,1,0:T(8,128)}, u32[]{:S(2)}) copy-start(f32[6,2,3,4,1,16,128]{6,5,4,3,2,1,0:T(8,128)} %param.7) | copy-start | bytes 3538948
  157.1 7.9 %copy-start.16 = (f32[4,16,128,6]{2,1,0,3:T(8,128)S(1)}, f32[4,16,128,6]{2,1,0,3:T(8,128)}, u32[]{:S(2)}) copy-start(f32[4,16,128,6]{2,1,0,3:T(8,128)} %slice_bitcast_fusion.14) | copy-start | bytes 589828
  159.0 21.8 %all-to-all-start.1 = ((f32[32,1,1536]{2,1,0:T(1,128)}), f32[32,1,1536]{2,1,0:T(1,128)S(1)}, u32[]{:S(2)}, u32[]{:S(2)}) async-start(f32[32,1,1536]{2,1,0:T(1,128)} %reshape.260), calls=%async_computation.1 | async-start | bytes 393216 | tf_op jit(solution)/shard_map/all_to_all | solution.py:62
  183.8 2.6 copy-start.22
  224.9 2.6 copy-start.17
  228.4 12.4 %all-to-all-start.3 = ((f32[2,3,64,128]{3,0,1,2:T(2,128)}), f32[2,3,64,128]{3,0,1,2:T(2,128)S(1)}, u32[]{:S(2)}, u32[]{:S(2)}) async-start(f32[2,3,64,128]{3,0,1,2:T(2,128)} %copy.180), calls=%async_computation.3 | async-start | bytes 393216 | tf_op jit(solution)/shard_map/all_to_all | solution.py:58
  234.2 110.7 %all-gather.5.cloned.1.call-start = ((), (), s32[]{:S(2)}) async-start(), calls=%async_computation.5 | async-start | bytes 4325376 | tf_op jit(solution)/shard_map/all_gather | solution.py:212
  242.2 2.6 copy-start.15
  244.8 12.3 %collective-permute-start = (f32[6,4,1,128]{3,1,2,0:T(4,128)S(1)}, f32[6,4,1,128]{3,1,2,0:T(4,128)S(1)}, u32[]{:S(2)}, u32[]{:S(2)}) collective-permute-start(f32[6,4,1,128]{3,1,2,0:T(4,128)S(1)} %bitcast.320), channel_id=1, source_target_pairs={{0,16},{16,32},{32,48},{48,64},{64,80},{80,96},{96,112},{112,128},... | collective-permute-start | bytes 36872 | tf_op jit(solution)/shard_map/ppermute | solution.py:20
  246.8 11.2 %collective-permute-start.1 = (f32[6,4,1,128]{3,1,2,0:T(4,128)S(1)}, f32[6,4,1,128]{3,1,2,0:T(4,128)S(1)}, u32[]{:S(2)}, u32[]{:S(2)}) collective-permute-start(f32[6,4,1,128]{3,1,2,0:T(4,128)S(1)} %bitcast.319), channel_id=1, source_target_pairs={{16,0},{32,16},{48,32},{64,48},{80,64},{96,80},{112,96},{128,112},... | collective-permute-start | bytes 36872 | tf_op jit(solution)/shard_map/ppermute | solution.py:23
  260.3 12.0 %collective-permute-start.2 = (f32[6,4,66,1]{2,1,3,0:T(4,128)S(1)}, f32[6,4,66,1]{2,1,3,0:T(4,128)S(1)}, u32[]{:S(2)}, u32[]{:S(2)}) collective-permute-start(f32[6,4,66,1]{2,1,3,0:T(4,128)S(1)} %get-tuple-element.19), channel_id=1, source_target_pairs={{0,1},{1,2},{2,3},{3,4},{4,5},{5,6},{6,7},{7,8},{8,9},{9,10},{10,1... | collective-permute-start | bytes 19016 | tf_op jit(solution)/shard_map/ppermute | solution.py:20
  263.0 9.3 %collective-permute-start.3 = (f32[6,4,66,1]{2,1,3,0:T(4,128)S(1)}, f32[6,4,66,1]{2,1,3,0:T(4,128)S(1)}, u32[]{:S(2)}, u32[]{:S(2)}) collective-permute-start(f32[6,4,66,1]{2,1,3,0:T(4,128)S(1)} %get-tuple-element.20), channel_id=1, source_target_pairs={{1,0},{2,1},{3,2},{4,3},{5,4},{6,5},{7,6},{8,7},{9,8},{10,9},{11,1... | collective-permute-start | bytes 19016 | tf_op jit(solution)/shard_map/ppermute | solution.py:23
  272.3 2.5 copy-start
  276.5 71.5 %copy-start.3 = (f32[4,66,130]{1,0,2:T(4,128)S(1)}, f32[4,66,130]{1,0,2:T(4,128)}, u32[]{:S(2)}) copy-start(f32[4,66,130]{1,0,2:T(4,128)} %get-tuple-element.14) | copy-start | bytes 411844
  276.5 71.6 %copy-start.4 = (f32[4,66,130]{1,0,2:T(4,128)S(1)}, f32[4,66,130]{1,0,2:T(4,128)}, u32[]{:S(2)}) copy-start(f32[4,66,130]{1,0,2:T(4,128)} %get-tuple-element.16) | copy-start | bytes 411844
  276.5 71.6 %copy-start.11 = (f32[3,64,128]{1,0,2:T(4,128)S(1)}, f32[3,64,128]{1,0,2:T(4,128)}, u32[]{:S(2)}) copy-start(f32[3,64,128]{1,0,2:T(4,128)} %get-tuple-element.29) | copy-start | bytes 294916
  276.5 71.6 %copy-start.12 = (f32[3,64,128]{1,0,2:T(4,128)S(1)}, f32[3,64,128]{1,0,2:T(4,128)}, u32[]{:S(2)}) copy-start(f32[3,64,128]{1,0,2:T(4,128)} %get-tuple-element.32) | copy-start | bytes 294916
  276.6 71.6 %copy-start.13 = (f32[3,64,128]{1,0,2:T(4,128)S(1)}, f32[3,64,128]{1,0,2:T(4,128)}, u32[]{:S(2)}) copy-start(f32[3,64,128]{1,0,2:T(4,128)} %get-tuple-element.33) | copy-start | bytes 294916
  276.6 71.6 %copy-start.14 = (f32[3,64,128]{1,0,2:T(4,128)S(1)}, f32[3,64,128]{1,0,2:T(4,128)}, u32[]{:S(2)}) copy-start(f32[3,64,128]{1,0,2:T(4,128)} %get-tuple-element.34) | copy-start | bytes 294916
  348.1 1.1 copy-start.1
  351.0 6.6 %copy-start.18 = (f32[3,64,128]{2,1,0:T(8,128)S(1)}, f32[3,64,128]{2,1,0:T(8,128)}, u32[]{:S(2)}) copy-start(f32[3,64,128]{2,1,0:T(8,128)} %param.6) | copy-start | bytes 294916
  351.0 7.6 %copy-start.21 = (f32[4,64,128]{2,1,0:T(8,128)S(1)}, f32[4,64,128]{2,1,0:T(8,128)}, u32[]{:S(2)}) copy-start(f32[4,64,128]{2,1,0:T(8,128)} %param.11) | copy-start | bytes 393220
  352.4 7.0 %collective-permute-start.4 = (f32[3,4,1,128]{3,1,2,0:T(4,128)S(1)}, f32[3,4,1,128]{3,1,2,0:T(4,128)S(1)}, u32[]{:S(2)}, u32[]{:S(2)}) collective-permute-start(f32[3,4,1,128]{3,1,2,0:T(4,128)S(1)} %copy.194), channel_id=1, source_target_pairs={{16,0},{32,16},{48,32},{64,48},{80,64},{96,80},{112,96},{128,112},... | collective-permute-start | bytes 18440 | tf_op jit(solution)/shard_map/ppermute | solution.py:23
  355.2 11.3 %collective-permute-start.5 = (f32[3,4,1,128]{3,1,2,0:T(4,128)}, f32[3,4,1,128]{3,1,2,0:T(4,128)}, u32[]{:S(2)}, u32[]{:S(2)}) collective-permute-start(f32[3,4,1,128]{3,1,2,0:T(4,128)} %copy.196), channel_id=1, source_target_pairs={{0,16},{16,32},{32,48},{48,64},{64,80},{80,96},{96,112},{112,128},... | collective-permute-start | bytes 18440 | tf_op jit(solution)/shard_map/ppermute | solution.py:20
  369.7 10.2 %collective-permute-start.6 = (f32[3,4,66,1]{2,1,3,0:T(4,128)}, f32[3,4,66,1]{2,1,3,0:T(4,128)S(1)}, u32[]{:S(2)}, u32[]{:S(2)}) collective-permute-start(f32[3,4,66,1]{2,1,3,0:T(4,128)} %get-tuple-element.23), channel_id=1, source_target_pairs={{1,0},{2,1},{3,2},{4,3},{5,4},{6,5},{7,6},{8,7},{9,8},{10,9},{11,1... | collective-permute-start | bytes 9512 | tf_op jit(solution)/shard_map/ppermute | solution.py:23
  375.6 8.4 %collective-permute-start.7 = (f32[3,4,66,1]{2,1,3,0:T(4,128)}, f32[3,4,66,1]{2,1,3,0:T(4,128)S(1)}, u32[]{:S(2)}, u32[]{:S(2)}) collective-permute-start(f32[3,4,66,1]{2,1,3,0:T(4,128)} %get-tuple-element.24), channel_id=1, source_target_pairs={{0,1},{1,2},{2,3},{3,4},{4,5},{5,6},{6,7},{7,8},{8,9},{9,10},{10,1... | collective-permute-start | bytes 9512 | tf_op jit(solution)/shard_map/ppermute | solution.py:20
  379.9 8.9 %copy-start.2 = (f32[3,64,128]{1,0,2:T(4,128)S(1)}, f32[3,64,128]{1,0,2:T(4,128)}, u32[]{:S(2)}) copy-start(f32[3,64,128]{1,0,2:T(4,128)} %get-tuple-element.46) | copy-start | bytes 294916
  389.3 1.1 copy-start.6
  389.3 1.1 copy-start.7
  (6 other events, 5.3 us)
Sparse Core Ops, SparseCore 0:
  11.4 105.2 all-gather.2
  244.9 99.8 all-gather.4
where the time goes:
time: 407 us; the launch traced here: 402 us
  waiting for transfers between devices  215 us (53%)
  local copies, waits for them, and re-layouts  58.5 us (14%)
  starting transfers between devices  50.1 us (12%)
  other arithmetic  24.1 us (6%)
  matrix products  19.5 us (5%)
  blocking collectives  19.2 us (5%)
  between operations  15.2 us (4%)
    all_gather x1, waiting for transfers between devices, local(): gathered = lax.all_gather(interface_velocity, 'bx', axis=1, tiled=True)  109 us
    all_gather x1, waiting for transfers between devices, local(): lax.all_gather(spatial.reshape(3, strike_length, row_block), 'bx', axis=2...  68.3 us
    ppermute x4, starting transfers between devices, extended(): lax.ppermute(lax.slice_in_dim(block, 0, width, axis=dim), axis, backward)  23.4 us
    all_to_all x1, blocking collectives, strike_modes(): return lax.all_to_all(block, 'bx', split_axis=4, concat_axis=4, tiled=True)  19.2 us
    unnamed x66, local copies, waits for them, and re-layouts  14.5 us
    all_to_all x1, waiting for transfers between devices, strike_modes(): return lax.all_to_all(block, 'bx', split_axis=4, concat_axis=4, tiled=True)  14.2 us
    all_to_all x2, waiting for transfers between devices, dip_blocks(): return lax.all_to_all(block, 'by', split_axis=2, concat_axis=2, tiled=True)  12.4 us
    all_to_all x2, starting transfers between devices, dip_blocks(): return lax.all_to_all(block, 'by', split_axis=2, concat_axis=2, tiled=True)  11.3 us
  transfers between devices with their start and end apart: 13, of which 7 were waited for; matrix products, arithmetic and copies ran while one was open for 5% of the time, Pallas kernels for 0%

commit v1 on v0

v1 whole, which is shorter than its diff:
```python
from functools import partial
import math

import jax
import jax.numpy as jnp
import ml_dtypes
import numpy as np
from jax import lax
from jax.experimental import pallas as pl
from jax.experimental.pallas import tpu as pltpu
from jax.sharding import PartitionSpec as P

COURANT = 0.3
FRICTION = 0.6
NP_, NQ = 32, 64
NJ = 16
NF = 512
SCALE = 1.0 / 2048.0
VMEM = pl.BlockSpec(memory_space=pltpu.VMEM)
PARAMS = pltpu.CompilerParams(vmem_limit_bytes=48 * 1024 * 1024)


def split_table(table):
    high = table.astype(ml_dtypes.bfloat16)
    low = (table - high.astype(np.float64)).astype(ml_dtypes.bfloat16)
    return high, low


def angles(rows, cols, length):
    return 2.0 * np.pi / length * ((rows[:, None] * cols[None, :]) % length)


def strike_tables():
    theta = angles(np.arange(32), np.arange(32), 32)
    cos, sin = np.cos(theta), np.sin(theta)
    high, low = split_table(np.concatenate([cos, -sin], axis=0))
    forward = np.concatenate([high, high, low], axis=1)
    high, low = split_table(np.concatenate([cos, -sin], axis=1))
    inverse = np.concatenate([high, high, low], axis=1)
    return forward, inverse


def strike_twiddle():
    theta = angles(np.arange(32), np.arange(64), 2048)
    theta = np.concatenate([theta, theta], axis=1)
    return np.stack([np.cos(theta), np.sin(theta)]).astype(np.float32)


def cell_tables():
    theta = angles(np.arange(64), np.arange(64), 64).reshape(64, 16, 4)
    cos, sin = np.cos(theta) * SCALE, np.sin(theta) * SCALE
    table = np.zeros((2, 2, 64, 16, 2, 2, 4))
    for h in range(2):
        table[0, h, :, :, 0, h] = cos
        table[1, h, :, :, 0, h] = sin
        table[0, h, :, :, 1, h] = -sin
        table[1, h, :, :, 1, h] = cos
    table = table.reshape(256, 256)
    return split_table(table), split_table(np.ascontiguousarray(table.T))


def dip_order():
    lane = np.arange(NF)
    return 16 * (lane % 32) + lane // 32


def dip_tables():
    theta = angles(np.arange(NF), dip_order(), NF)
    forward = split_table(np.concatenate([np.cos(theta), np.sin(theta)], axis=1))
    inverse = split_table(np.concatenate([np.cos(theta).T, np.sin(theta).T], axis=1))
    return forward, inverse


def dip_twiddle():
    theta = angles(np.arange(4), dip_order(), 2048).reshape(2, 2, 1, NF)
    theta = np.broadcast_to(theta, (2, 2, 4, NF)).reshape(2, 8, NF)
    return np.stack([np.cos(theta), np.sin(theta)], axis=1).astype(np.float32)


def halves(value):
    high = value.astype(jnp.bfloat16)
    low = (value - high.astype(jnp.float32)).astype(jnp.bfloat16)
    return high, low


def dot(a, b):
    return jnp.dot(a, b, preferred_element_type=jnp.float32)


def stacked_dot(table, value):
    high, low = halves(value)
    return dot(table, jnp.concatenate([high, low, high], axis=0))


def rows_dot(value, table_high, table_low):
    rows = value.shape[0]
    high, low = halves(value)
    both = dot(jnp.concatenate([high, low], axis=0), table_high)
    return both[:rows] + both[rows:] + dot(high, table_low)


def roll(value, shift, axis):
    return pltpu.roll(value, shift % value.shape[axis], axis)


def lane_of(shape):
    return lax.broadcasted_iota(jnp.int32, shape, len(shape) - 1)


def row_of(shape):
    return lax.broadcasted_iota(jnp.int32, shape, len(shape) - 2)


def block_transpose(parts):
    parts = list(parts)
    block = lane_of(parts[0].shape) // 16
    for step in (1, 2, 4):
        upper = (block // step) % 2 == 1
        for t in range(8):
            if (t // step) % 2 == 0:
                low, high = parts[t], parts[t + step]
                parts[t] = jnp.where(upper, roll(high, 16 * step, 1), low)
                parts[t + step] = jnp.where(upper, high, roll(low, -16 * step, 1))
    return parts


def scatter_kernel(iv_ref, out_ref, flipped_ref):
    for c in range(3):
        flipped_ref[...] = iv_ref[c].T
        for s in range(2):
            for h in range(2):
                out_ref[:, 2 * c + s, NQ * h : NQ * (h + 1)] = flipped_ref[
                    pl.ds(2 * s + h, 32, stride=4), :
                ]
    zero = jnp.zeros((32, 128), jnp.float32)
    out_ref[:, 6, :] = zero
    out_ref[:, 7, :] = zero


def strike_forward_kernel(in_ref, strike_ref, twiddle_ref, high_ref, low_ref, out_ref):
    value = jnp.concatenate([in_ref[:, m, :] for m in range(6)], axis=1)
    value = stacked_dot(strike_ref[...], value)
    cos, sin = twiddle_ref[0], twiddle_ref[1]
    rows = []
    for m in range(6):
        real = value[:32, 128 * m : 128 * (m + 1)]
        imag = value[32:, 128 * m : 128 * (m + 1)]
        rows.append(
            jnp.concatenate([real * cos + imag * sin, imag * cos - real * sin], axis=1)
        )
    value = rows_dot(jnp.concatenate(rows, axis=0), high_ref[...], low_ref[...])
    zero = jnp.zeros((32, 128), jnp.float32)
    for t in range(2):
        parts = [value[32 * m : 32 * (m + 1), 128 * t : 128 * (t + 1)] for m in range(6)]
        parts = block_transpose(parts + [zero, zero])
        for b in range(8):
            out_ref[32 * (8 * t + b) : 32 * (8 * t + b + 1), :] = parts[b]


def strike_inverse_kernel(in_ref, strike_ref, twiddle_ref, high_ref, low_ref, out_ref):
    columns = []
    for t in range(2):
        columns.append(
            block_transpose([in_ref[32 * (8 * t + b) : 32 * (8 * t + b + 1), :] for b in range(8)])
        )
    rows = [jnp.concatenate([columns[0][m], columns[1][m]], axis=1) for m in range(8)]
    value = rows_dot(jnp.concatenate(rows, axis=0), high_ref[...], low_ref[...])
    cos, sin = twiddle_ref[0], twiddle_ref[1]
    reals, imags = [], []
    for m in range(8):
        real = value[32 * m : 32 * (m + 1), :128]
        imag = value[32 * m : 32 * (m + 1), 128:]
        reals.append(real * cos - imag * sin)
        imags.append(imag * cos + real * sin)
    value = jnp.concatenate(
        [jnp.concatenate(reals, axis=1), jnp.concatenate(imags, axis=1)], axis=0
    )
    value = stacked_dot(strike_ref[...], value)
    parts = [value[:, 128 * m : 128 * (m + 1)] for m in range(8)]
    lane = lane_of((32, 128))
    last = parts[7]
    for m in range(6):
        before = roll(parts[m], 1, 0)
        after = roll(parts[m], -1, 0)
        for h in range(2):
            to = 64 + 2 * (2 * m + h)
            last = jnp.where(lane == to, roll(before, to - (NQ * h + 63), 1), last)
            last = jnp.where(lane == to + 1, roll(after, to + 1 - NQ * h, 1), last)
    parts[7] = last
    for m in range(8):
        out_ref[:, m, :] = parts[m]


def dip_kernel(
    in_ref, weight_ref, past_ref, twiddle_ref, fh_ref, fl_ref, ih_ref, il_ref, out_ref
):
    flipped = in_ref[...].T[:96]
    product = rows_dot(flipped, fh_ref[...], fl_ref[...])
    top = row_of((8, NF)) < 4
    sign = jnp.where(top, 1.0, -1.0).astype(jnp.float32)
    early = lane_of((8, NF)) % 32 < 16
    inverse_rows = []
    for c in range(3):
        even, odd = [], []
        turned = []
        for s in range(2):
            at = 32 * c + 16 * s
            real = product[at : at + 8, :NF] + product[at + 8 : at + 16, NF:]
            imag = product[at + 8 : at + 16, :NF] - product[at : at + 8, NF:]
            cos, sin = twiddle_ref[s, 0], twiddle_ref[s, 1]
            turned.append((real * cos + imag * sin, imag * cos - real * sin))
        even = [turned[0][ri] + turned[1][ri] for ri in range(2)]
        odd = [turned[0][ri] - turned[1][ri] for ri in range(2)]
        odd = [jnp.where(top, odd[0], odd[1]), jnp.where(top, odd[1], -odd[0])]
        response = []
        for parity, value in enumerate((even, odd)):
            spectrum = [roll(part, 4, 0) + sign * part for part in value]
            response.append(
                [
                    weight_ref[parity] * spectrum[ri] + past_ref[c, parity, ri]
                    for ri in range(2)
                ]
            )
        response = [[roll(part, 4, 0) + sign * part for part in pair] for pair in response]
        even = response[0]
        odd = [
            jnp.where(top, response[1][0], -response[1][1]),
            jnp.where(top, response[1][1], response[1][0]),
        ]
        for s in range(2):
            if s == 0:
                real, imag = even[0] + odd[0], even[1] + odd[1]
            else:
                real, imag = even[0] - odd[0], even[1] - odd[1]
            cos, sin = twiddle_ref[s, 0], twiddle_ref[s, 1]
            inverse_rows += [real * cos - imag * sin, imag * cos + real * sin]
    product = rows_dot(jnp.concatenate(inverse_rows, axis=0), ih_ref[...], il_ref[...])
    groups = []
    for c in range(3):
        for s in range(2):
            at = 32 * c + 16 * s
            groups.append(product[at : at + 8, :NF] - product[at + 8 : at + 16, NF:])
            groups.append(product[at + 8 : at + 16, :NF] + product[at : at + 8, NF:])
    edges = []
    for c in range(3):
        for ri in range(2):
            before = roll(roll(groups[4 * c + 2 + ri], 4, 0), 1, 1)
            after = roll(groups[4 * c + ri], -1, 1)
            edges.append(jnp.where(early, before, after))
    for ri in range(2):
        groups.append(jnp.where(top, edges[ri], roll(edges[2 + ri], 4, 0)))
    for ri in range(2):
        groups.append(jnp.where(top, edges[4 + ri], 0.0))
    out_ref[...] = jnp.concatenate(groups, axis=0).T


def past_kernel(kernel_ref, history_ref, out_ref):
    for a in range(4):
        weights = [kernel_ref[h + 1, a, 0] for h in range(6)]
        for z in range(2):
            for c in range(3):
                total = weights[0] * history_ref[0, z, c, a, 0]
                for h in range(1, 6):
                    total = total + weights[h] * history_ref[h, z, c, a, 0]
                out_ref[z, c, a] = total


def edge_kernel(fields_ref, xlo_ref, xhi_ref, ylo_ref, yhi_ref, *, across, along):
    pad = jnp.zeros((4, 128), jnp.float32)
    xlo, xhi = [], []
    lane = lane_of((64, 128))
    ylo = jnp.zeros((64, 128), jnp.float32)
    yhi = jnp.zeros((64, 128), jnp.float32)
    for n in range(3):
        for z in range(4):
            field = fields_ref[across[n], z]
            xlo.append(field[0:1])
            xhi.append(field[63:64])
            field = fields_ref[along[n], z]
            to = 4 * n + z
            ylo = jnp.where(lane == to, roll(field, to, 1), ylo)
            yhi = jnp.where(lane == to, roll(field, to - 127, 1), yhi)
    xlo_ref[...] = jnp.concatenate(xlo + [pad], axis=0)
    xhi_ref[...] = jnp.concatenate(xhi + [pad], axis=0)
    ylo_ref[...] = ylo
    yhi_ref[...] = yhi


def strike_diff(field, low, high):
    row = row_of(field.shape)
    before = jnp.where(row == 0, low, roll(field, 1, 0))
    after = jnp.where(row == 63, high, roll(field, -1, 0))
    return 0.5 * (after - before)


def dip_diff(field, low, high, to):
    lane = lane_of(field.shape)
    before = jnp.where(lane == 0, roll(low, -to, 1), roll(field, 1, 1))
    after = jnp.where(lane == 127, roll(high, 127 - to, 1), roll(field, -1, 1))
    return 0.5 * (after - before)


def velocity_kernel(velocity_ref, stress_ref, xlo_ref, xhi_ref, ylo_ref, yhi_ref, out_ref):
    across, along, deep = (0, 3, 4), (3, 1, 5), (4, 5, 2)
    ylo, yhi = ylo_ref[...], yhi_ref[...]
    for n in range(3):
        for z in range(4):
            at = 4 * n + z
            total = strike_diff(
                stress_ref[across[n], z], xlo_ref[at : at + 1], xhi_ref[at : at + 1]
            ) + dip_diff(stress_ref[along[n], z], ylo, yhi, at)
            if z < 3:
                total = total + 0.5 * stress_ref[deep[n], z + 1]
            if z > 0:
                total = total - 0.5 * stress_ref[deep[n], z - 1]
            out_ref[n, z] = velocity_ref[n, z] + COURANT * total


def slab_kernel(
    in_ref, before_ref, stress_ref, cohesion_ref, iv_ref,
    xlo_ref, xhi_ref, ylo_ref, yhi_ref,
    velocity_ref, out_ref, flipped_ref, edge_ref,
):
    last = in_ref[:, 7, :]
    xlo, xhi = [], []
    half = lane_of((32, 128)) < 64
    edge_ref[...] = jnp.zeros((128, 128), jnp.float32)
    for c in range(3):
        for s in range(2):
            for h in range(2):
                to = pl.ds(2 * s + h, 32, stride=4)
                piece = in_ref[:, 2 * c + s, :]
                piece = roll(piece, 64, 1) if h else piece
                shifted = roll(last, -2 * (4 * c + 2 * s + h), 1)
                flipped_ref[to, :] = jnp.where(half, piece, shifted)
        m, h = 6 + c // 2, c % 2
        edge_ref[4 * c : 4 * c + 1, 0:64] = in_ref[0, m : m + 1, NQ * h : NQ * (h + 1)]
        edge_ref[12 + 4 * c : 13 + 4 * c, 0:64] = in_ref[31, m : m + 1, NQ * h : NQ * (h + 1)]
        traction = flipped_ref[...].T
        velocity_ref[c, 0] = before_ref[c, 0] - 0.5 * COURANT * traction[:64]
        xlo.append(traction[64:65])
        xhi.append(traction[65:66])
        for z in range(1, 4):
            velocity_ref[c, z] = before_ref[c, z]
    edges = edge_ref[...].T[:64]
    lane = lane_of((64, 128))
    ylo = ylo_ref[...] - 0.5 * COURANT * jnp.where(lane < 12, edges, 0.0)
    yhi = yhi_ref[...] - 0.5 * COURANT * jnp.where(lane < 12, roll(edges, -12, 1), 0.0)
    for z in range(4):
        dx, dy, dz = [], [], []
        for c in range(3):
            field = velocity_ref[c, z]
            at = 4 * c + z
            low, high = xlo_ref[at : at + 1], xhi_ref[at : at + 1]
            if z == 0:
                low = low - 0.5 * COURANT * xlo[c]
                high = high - 0.5 * COURANT * xhi[c]
            dx.append(strike_diff(field, low, high))
            dy.append(dip_diff(field, ylo, yhi, at))
            under = iv_ref[c] if z == 0 else velocity_ref[c, z - 1]
            if z < 3:
                dz.append(0.5 * (velocity_ref[c, z + 1] - under))
            else:
                dz.append(-0.5 * under)
        dilation = dx[0] + dy[1] + dz[2]
        rates = [
            dilation + 2.0 * dx[0],
            dilation + 2.0 * dy[1],
            dilation + 2.0 * dz[2],
            dy[0] + dx[1],
            dz[0] + dx[2],
            dz[1] + dy[2],
        ]
        trial = [stress_ref[n, z] + COURANT * rates[n] for n in range(6)]
        pressure = (trial[0] + trial[1] + trial[2]) * (1.0 / 3.0)
        normal = [trial[n] - pressure for n in range(3)]
        second = 0.5 * (
            normal[0] * normal[0] + normal[1] * normal[1] + normal[2] * normal[2]
        ) + (trial[3] * trial[3] + trial[4] * trial[4] + trial[5] * trial[5])
        shear = jnp.sqrt(second)
        limit = cohesion_ref[z] + FRICTION * jnp.maximum(-pressure, 0.0)
        factor = limit / jnp.maximum(shear, limit)
        for n in range(3):
            out_ref[n, z] = pressure + factor * normal[n]
            out_ref[3 + n, z] = factor * trial[3 + n]


def f32(*shape):
    return jax.ShapeDtypeStruct(shape, jnp.float32)


def call(kernel, out_shape, arguments, scratch=()):
    many = isinstance(out_shape, tuple)
    return pl.pallas_call(
        kernel,
        out_shape=out_shape,
        in_specs=[VMEM] * len(arguments),
        out_specs=(VMEM,) * len(out_shape) if many else VMEM,
        scratch_shapes=list(scratch),
        compiler_params=PARAMS,
    )(*arguments)


def scatter(iv):
    return call(scatter_kernel, f32(32, 8, 128), (iv,), [pltpu.VMEM((128, 64), jnp.float32)])


def strike_forward(arrived):
    forward, _ = strike_tables()
    (high, low), _ = cell_tables()
    return call(
        strike_forward_kernel, f32(512, 128), (arrived, forward, strike_twiddle(), high, low)
    )


def strike_inverse(arrived):
    _, inverse = strike_tables()
    _, (high, low) = cell_tables()
    return call(
        strike_inverse_kernel, f32(32, 8, 128), (arrived, inverse, strike_twiddle(), high, low)
    )


def dip(arrived, weight, past):
    forward, inverse = dip_tables()
    return call(
        dip_kernel, f32(512, 128), (arrived, weight, past, dip_twiddle(), *forward, *inverse)
    )


def mode_order(value):
    lead = value.shape[:-3]
    n = len(lead)
    value = value.reshape(*lead, 4, 16, 2, 2, 32)
    value = jnp.transpose(value, (*range(n), n + 3, n + 2, n, n + 1, n + 4))
    return value.reshape(*lead, 2, 8, NF)


def past_terms(kernel, history):
    past = call(past_kernel, f32(2, 3, 4, 16, 128), (kernel, history))
    past = jnp.moveaxis(mode_order(past), 0, 2)
    return mode_order(kernel[0, :, 0]), past


def edges(fields, across, along):
    return call(
        partial(edge_kernel, across=across, along=along),
        (f32(16, 128), f32(16, 128), f32(64, 128), f32(64, 128)),
        (fields,),
    )


def velocity_before(velocity, stress, halo):
    return call(velocity_kernel, f32(3, 4, 64, 128), (velocity, stress, *halo))


def slab(arrived, before, stress, cohesion, iv, halo):
    return call(
        slab_kernel,
        (f32(3, 4, 64, 128), f32(6, 4, 64, 128)),
        (arrived, before, stress, cohesion, iv, *halo),
        [pltpu.VMEM((128, 128), jnp.float32), pltpu.VMEM((128, 128), jnp.float32)],
    )


def exchange(xlo, xhi, ylo, yhi):
    def shift(value, axis, step):
        count = lax.axis_size(axis)
        return lax.ppermute(value, axis, [(i, (i + step) % count) for i in range(count)])

    return (shift(xhi, "bx", 1), shift(xlo, "bx", -1), shift(yhi, "by", 1), shift(ylo, "by", -1))


def strike_swap(value):
    return lax.all_to_all(value, "bx", split_axis=0, concat_axis=0, tiled=True)


def whole_swap(value):
    value = value.reshape(512, 1, 128)
    value = lax.all_to_all(value, ("by", "bx"), split_axis=0, concat_axis=0, tiled=True)
    return value.reshape(512, 128)


def local(interface_velocity, history, kernel, velocity, stress, cohesion):
    arrived = strike_swap(scatter(interface_velocity))
    weight, past = past_terms(kernel, history)
    stress_halo = exchange(*edges(stress, (0, 3, 4), (3, 1, 5)))
    arrived = whole_swap(strike_forward(arrived))
    before = velocity_before(velocity, stress, stress_halo)
    halo = exchange(*edges(before, (0, 1, 2), (0, 1, 2)))
    arrived = whole_swap(dip(arrived, weight, past))
    arrived = strike_swap(strike_inverse(arrived))
    return slab(arrived, before, stress, cohesion, interface_velocity, halo)


def solution(mesh):
    return jax.shard_map(
        local,
        mesh=mesh,
        in_specs=(
            P(None, "bx", "by"),
            P(None, None, None, "by", "bx", None, None),
            P(None, "by", "bx", None, None),
            P(None, None, "bx", "by"),
            P(None, None, "bx", "by"),
            P(None, "bx", "by"),
        ),
        out_specs=(P(None, None, "bx", "by"), P(None, None, "bx", "by")),
        check_vma=False,
    )
```

time: 407 us -> 154 us (0.38)
  the two profiles are of different devices: /device:TPU:6 before, /device:TPU:57 now
where the time goes in v1:
time: 154 us; the launch traced here: 153 us
  blocking collectives  53 us (34%)
  starting transfers between devices  52.9 us (34%)
  waiting for transfers between devices  26.4 us (17%)
  local copies, waits for them, and re-layouts  12.6 us (8%)
  Pallas kernels  7.39 us (5%)
    ppermute x8, starting transfers between devices, shift(): lax.ppermute(value, axis, [(i, (i + step) % count) for i in range(count)])  32.7 us
    all_to_all x1, blocking collectives, strike_swap(): return lax.all_to_all(value, 'bx', split_axis=0, concat_axis=0, tiled=True)  26.9 us
    all_to_all x1, blocking collectives, whole_swap(): lax.all_to_all(value, ('by', 'bx'), split_axis=0, concat_axis=0, tiled=True)  26.1 us
    ppermute x8, waiting for transfers between devices, shift(): lax.ppermute(value, axis, [(i, (i + step) % count) for i in range(count)])  18.1 us
    all_to_all x1, starting transfers between devices, whole_swap(): lax.all_to_all(value, ('by', 'bx'), split_axis=0, concat_axis=0, tiled=True)  13.4 us
    all_to_all x1, waiting for transfers between devices, whole_swap(): lax.all_to_all(value, ('by', 'bx'), split_axis=0, concat_axis=0, tiled=True)  8.31 us
    pallas_call x9, Pallas kernels, call(): pl.pallas_call(kernel, out_shape=out_shape, in_specs=[VMEM] * len(argumen...  7.39 us
    all_to_all x1, starting transfers between devices, strike_swap(): return lax.all_to_all(value, 'bx', split_axis=0, concat_axis=0, tiled=True)  6.85 us
  transfers between devices with their start and end apart: 10, of which 3 were waited for; matrix products, arithmetic and copies ran while one was open for 4% of the time, Pallas kernels for 1%

profile of v1, /device:TPU:57, one launch (start us, length us, event | category | flops | bytes accessed | tf_op | source)
XLA Modules:
  0.0 153.2 jit_solution(17447288297157451652)
XLA Ops:
  0.7 1.0 copy-done.7
  1.6 0.4 shard_map.194
  2.0 26.9 %all_to_all.20.in_ref = f32[32,8,128]{2,1,0:T(8,128)S(1)} all-to-all(f32[32,8,128]{2,1,0:T(8,128)S(1)} %shard_map.194), channel_id=1, replica_groups=mesh['bx'=32,'by'=16] {'bx'}, dimensions={0} | all-to-all | bytes 262144 | tf_op jit(solution)/shard_map/all_to_all | solution.py:475
  28.9 0.8 copy-done.12
  29.6 0.9 copy-done.16
  30.5 0.9 copy-done.17
  31.4 0.7 copy-done.20
  32.2 1.4 shard_map.195
  33.5 13.4 %all-to-all-start.1 = ((f32[512,1,128]{2,1,0:T(1,128)}), f32[512,1,128]{2,1,0:T(1,128)S(1)}, u32[]{:S(2)}, u32[]{:S(2)}) async-start(f32[512,1,128]{2,1,0:T(1,128)} %bitcast.1), calls=%async_computation.1 | async-start | bytes 524288 | tf_op jit(solution)/shard_map/all_to_all | solution.py:480
  47.3 1.5 reshape.28
  48.9 2.3 %copy.29 = f32[2,3,4,16,2,2,32]{6,3,2,4,0,5,1:T(8,128)} copy(f32[2,3,4,16,2,2,32]{6,5,4,3,2,1,0:T(2,128)} %reshape.28) | data formatting | bytes 393216 | tf_op jit(solution)/shard_map/reshape | solution.py:434
  51.1 2.1 %reshape.29 = f32[2,3,2,8,512]{4,3,0,2,1:T(8,128)} reshape(f32[2,3,2,2,4,16,32]{6,5,4,3,0,2,1:T(8,128)} %bitcast.29) | data formatting | bytes 393216 | tf_op jit(solution)/shard_map/reshape | solution.py:436
  53.2 8.3 %all-to-all-done.1 = f32[512,1,128]{2,1,0:T(1,128)S(1)} async-done(((f32[512,1,128]{2,1,0:T(1,128)}), f32[512,1,128]{2,1,0:T(1,128)S(1)}, u32[]{:S(2)}, u32[]{:S(2)}) %all-to-all-start.1) | async-done | bytes 262176 | tf_op jit(solution)/shard_map/all_to_all | solution.py:480
  61.6 1.2 copy-done.5
  62.8 0.9 copy-done.6
  63.7 1.3 shard_map.197
  65.1 26.1 %all_to_all.21 = f32[512,1,128]{2,1,0:T(1,128)S(1)} all-to-all(f32[512,1,128]{2,1,0:T(1,128)S(1)} %bitcast.26), channel_id=1, replica_groups=mesh['bx'=32,'by'=16] {'by','bx'}, dimensions={0} | all-to-all | bytes 524288 | tf_op jit(solution)/shard_map/all_to_all | solution.py:480
  91.2 1.4 shard_map.198
  92.7 6.9 %all-to-all-start.3 = ((f32[32,8,128]{2,1,0:T(8,128)}), f32[32,8,128]{2,1,0:T(8,128)S(1)}, u32[]{:S(2)}, u32[]{:S(2)}) async-start(f32[32,8,128]{2,1,0:T(8,128)} %shard_map.198), calls=%async_computation.3 | async-start | bytes 262144 | tf_op jit(solution)/shard_map/all_to_all | solution.py:475
  99.5 0.3 shard_map.199
  99.8 2.4 %collective-permute-start.2 = (f32[64,128]{1,0:T(8,128)S(1)}, f32[64,128]{1,0:T(8,128)S(1)}, u32[]{:S(2)}, u32[]{:S(2)}) collective-permute-start(f32[64,128]{1,0:T(8,128)S(1)} %get-tuple-element.12), channel_id=1, source_target_pairs={{0,1},{1,2},{2,3},{3,4},{4,5},{5,6},{6,7},{7,8},{8,9},{9,10},{10,1... | collective-permute-start | bytes 98312 | tf_op jit(solution)/shard_map/ppermute | solution.py:469
  102.2 6.9 %collective-permute-start.3 = (f32[64,128]{1,0:T(8,128)S(1)}, f32[64,128]{1,0:T(8,128)S(1)}, u32[]{:S(2)}, u32[]{:S(2)}) collective-permute-start(f32[64,128]{1,0:T(8,128)S(1)} %get-tuple-element.13), channel_id=1, source_target_pairs={{0,15},{1,0},{2,1},{3,2},{4,3},{5,4},{6,5},{7,6},{8,7},{9,8},{10,9... | collective-permute-start | bytes 98312 | tf_op jit(solution)/shard_map/ppermute | solution.py:469
  109.2 7.8 %collective-permute-start = (f32[16,128]{1,0:T(8,128)S(1)}, f32[16,128]{1,0:T(8,128)S(1)}, u32[]{:S(2)}, u32[]{:S(2)}) collective-permute-start(f32[16,128]{1,0:T(8,128)S(1)} %get-tuple-element.10), channel_id=1, source_target_pairs={{0,16},{16,32},{32,48},{48,64},{64,80},{80,96},{96,112},{112,128},... | collective-permute-start | bytes 24584 | tf_op jit(solution)/shard_map/ppermute | solution.py:469
  117.0 1.9 %collective-permute-start.1 = (f32[16,128]{1,0:T(8,128)S(1)}, f32[16,128]{1,0:T(8,128)S(1)}, u32[]{:S(2)}, u32[]{:S(2)}) collective-permute-start(f32[16,128]{1,0:T(8,128)S(1)} %get-tuple-element.11), channel_id=1, source_target_pairs={{0,496},{16,0},{32,16},{48,32},{64,48},{80,64},{96,80},{112,96},{1... | collective-permute-start | bytes 24584 | tf_op jit(solution)/shard_map/ppermute | solution.py:469
  118.9 9.0 %collective-permute-done.1.xhi_ref = f32[16,128]{1,0:T(8,128)S(1)} collective-permute-done((f32[16,128]{1,0:T(8,128)S(1)}, f32[16,128]{1,0:T(8,128)S(1)}, u32[]{:S(2)}, u32[]{:S(2)}) %collective-permute-start.1) | collective-permute-done | bytes 8224 | tf_op jit(solution)/shard_map/ppermute | solution.py:469
  128.0 0.5 shard_map.200.fields_ref.before_ref
  128.7 1.9 %collective-permute-start.6 = (f32[64,128]{1,0:T(8,128)S(1)}, f32[64,128]{1,0:T(8,128)S(1)}, u32[]{:S(2)}, u32[]{:S(2)}) collective-permute-start(f32[64,128]{1,0:T(8,128)S(1)} %get-tuple-element.16), channel_id=1, source_target_pairs={{0,1},{1,2},{2,3},{3,4},{4,5},{5,6},{6,7},{7,8},{8,9},{9,10},{10,1... | collective-permute-start | bytes 98312 | tf_op jit(solution)/shard_map/ppermute | solution.py:469
  130.6 7.3 %collective-permute-start.7 = (f32[64,128]{1,0:T(8,128)S(1)}, f32[64,128]{1,0:T(8,128)S(1)}, u32[]{:S(2)}, u32[]{:S(2)}) collective-permute-start(f32[64,128]{1,0:T(8,128)S(1)} %get-tuple-element.17), channel_id=1, source_target_pairs={{0,15},{1,0},{2,1},{3,2},{4,3},{5,4},{6,5},{7,6},{8,7},{9,8},{10,9... | collective-permute-start | bytes 98312 | tf_op jit(solution)/shard_map/ppermute | solution.py:469
  137.9 2.5 %collective-permute-start.4 = (f32[16,128]{1,0:T(8,128)S(1)}, f32[16,128]{1,0:T(8,128)S(1)}, u32[]{:S(2)}, u32[]{:S(2)}) collective-permute-start(f32[16,128]{1,0:T(8,128)S(1)} %get-tuple-element.14), channel_id=1, source_target_pairs={{0,16},{16,32},{32,48},{48,64},{64,80},{80,96},{96,112},{112,128},... | collective-permute-start | bytes 24584 | tf_op jit(solution)/shard_map/ppermute | solution.py:469
  140.4 1.9 %collective-permute-start.5 = (f32[16,128]{1,0:T(8,128)S(1)}, f32[16,128]{1,0:T(8,128)S(1)}, u32[]{:S(2)}, u32[]{:S(2)}) collective-permute-start(f32[16,128]{1,0:T(8,128)S(1)} %get-tuple-element.15), channel_id=1, source_target_pairs={{0,496},{16,0},{32,16},{48,32},{64,48},{80,64},{96,80},{112,96},{1... | collective-permute-start | bytes 24584 | tf_op jit(solution)/shard_map/ppermute | solution.py:469
  142.4 9.0 %collective-permute-done.5.xhi_ref = f32[16,128]{1,0:T(8,128)S(1)} collective-permute-done((f32[16,128]{1,0:T(8,128)S(1)}, f32[16,128]{1,0:T(8,128)S(1)}, u32[]{:S(2)}, u32[]{:S(2)}) %collective-permute-start.5) | collective-permute-done | bytes 8224 | tf_op jit(solution)/shard_map/ppermute | solution.py:469
  151.4 1.8 %shard_map.202 = (f32[3,4,64,128]{3,2,1,0:T(8,128)}, f32[6,4,64,128]{3,2,1,0:T(8,128)}) custom-call(f32[32,8,128]{2,1,0:T(8,128)S(1)} %all-to-all-done.3.in_ref, f32[3,4,64,128]{3,2,1,0:T(8,128)S(1)} %shard_map.200.fields_ref.before_ref, f32[6,4,64,128]{3,2,1,0:T(8,128)S(1)} %copy-done, f32[4,64,128]{2,1,0:T(8,128)S(1)} %copy-done.11, ...), custom_call_target="tpu_custom_call" | custom-call | tf_op jit(solution)/shard_map/pallas_call | solution.py:394
  (49 shorter events, 0.7 us)
Async XLA Ops:
  0.6 46.6 %copy-start.1 = (f32[6,2,3,4,1,16,128]{6,5,4,3,2,1,0:T(8,128)S(1)}, f32[6,2,3,4,1,16,128]{6,5,4,3,2,1,0:T(8,128)}, u32[]{:S(2)}) copy-start(f32[6,2,3,4,1,16,128]{6,5,4,3,2,1,0:T(8,128)} %history_ref.1) | copy-start | bytes 3538948
  0.6 1.0 copy-start.7
  1.6 45.3 %slice-start = ((f32[7,4,1,16,128]{4,3,2,1,0:T(8,128)}), f32[1,4,1,16,128]{4,3,2,1,0:T(8,128)S(1)}, s32[]{:S(2)}) async-start(f32[7,4,1,16,128]{4,3,2,1,0:T(8,128)} %kernel_ref.1), calls=%async_computation.4 | async-start | bytes 65536 | tf_op jit(solution)/shard_map/slice | solution.py:442
  1.6 45.6 %copy-start.10 = (f32[7,4,1,16,128]{4,3,2,1,0:T(8,128)S(1)}, f32[7,4,1,16,128]{4,3,2,1,0:T(8,128)}, u32[]{:S(2)}) copy-start(f32[7,4,1,16,128]{4,3,2,1,0:T(8,128)} %kernel_ref.1) | copy-start | bytes 688132
  28.9 0.8 copy-start.12
  29.6 0.9 copy-start.16
  30.5 0.9 copy-start.17
  31.4 0.7 copy-start.20
  33.5 28.0 %all-to-all-start.1 = ((f32[512,1,128]{2,1,0:T(1,128)}), f32[512,1,128]{2,1,0:T(1,128)S(1)}, u32[]{:S(2)}, u32[]{:S(2)}) async-start(f32[512,1,128]{2,1,0:T(1,128)} %bitcast.1), calls=%async_computation.1 | async-start | bytes 524288 | tf_op jit(solution)/shard_map/all_to_all | solution.py:480
  47.3 14.2 %copy-start.4 = (bf16[512,1024]{1,0:T(8,128)(2,1)S(1)}, bf16[512,1024]{1,0:T(8,128)(2,1)}, u32[]{:S(2)}) copy-start(bf16[512,1024]{1,0:T(8,128)(2,1)} %constant.31.clone.ih_ref) | copy-start | bytes 3145732
  48.8 12.7 %copy-start.2 = (bf16[512,1024]{1,0:T(8,128)(2,1)S(1)}, bf16[512,1024]{1,0:T(8,128)(2,1)}, u32[]{:S(2)}) copy-start(bf16[512,1024]{1,0:T(8,128)(2,1)} %constant.29.clone.fh_ref) | copy-start | bytes 3145732
  48.8 12.7 %copy-start.3 = (bf16[512,1024]{1,0:T(8,128)(2,1)S(1)}, bf16[512,1024]{1,0:T(8,128)(2,1)}, u32[]{:S(2)}) copy-start(bf16[512,1024]{1,0:T(8,128)(2,1)} %constant.30.clone.fl_ref) | copy-start | bytes 3145732
  48.8 12.7 %copy-start.18 = (f32[2,2,8,512]{3,2,1,0:T(8,128)S(1)}, f32[2,2,8,512]{3,2,1,0:T(8,128)}, u32[]{:S(2)}) copy-start(f32[2,2,8,512]{3,2,1,0:T(8,128)} %constant.28.clone.twiddle_ref) | copy-start | bytes 196612
  61.5 1.2 copy-start.5
  62.8 0.9 copy-start.6
  63.7 27.5 %copy-start.13 = (f32[2,32,128]{2,1,0:T(8,128)S(1)}, f32[2,32,128]{2,1,0:T(8,128)}, u32[]{:S(2)}) copy-start(f32[2,32,128]{2,1,0:T(8,128)} %constant.25.clone.twiddle_ref) | copy-start | bytes 98308
  63.7 27.5 %copy-start.14 = (bf16[256,256]{1,0:T(8,128)(2,1)S(1)}, bf16[256,256]{1,0:T(8,128)(2,1)}, u32[]{:S(2)}) copy-start(bf16[256,256]{1,0:T(8,128)(2,1)} %constant.34.clone.high_ref) | copy-start | bytes 393220
  63.7 27.5 %copy-start.15 = (bf16[256,256]{1,0:T(8,128)(2,1)S(1)}, bf16[256,256]{1,0:T(8,128)(2,1)}, u32[]{:S(2)}) copy-start(bf16[256,256]{1,0:T(8,128)(2,1)} %constant.35.clone.low_ref) | copy-start | bytes 393220
  63.7 27.5 %copy-start.19 = (bf16[32,192]{1,0:T(8,128)(2,1)S(1)}, bf16[32,192]{1,0:T(8,128)(2,1)}, u32[]{:S(2)}) copy-start(bf16[32,192]{1,0:T(8,128)(2,1)} %constant.33.clone.strike_ref) | copy-start | bytes 36868
  65.1 34.5 %copy-start = (f32[6,4,64,128]{3,2,1,0:T(8,128)S(1)}, f32[6,4,64,128]{3,2,1,0:T(8,128)}, u32[]{:S(2)}) copy-start(f32[6,4,64,128]{3,2,1,0:T(8,128)} %stress_ref.3) | copy-start | bytes 2359300
  65.1 62.9 %copy-start.9 = (f32[3,4,64,128]{3,2,1,0:T(8,128)S(1)}, f32[3,4,64,128]{3,2,1,0:T(8,128)}, u32[]{:S(2)}) copy-start(f32[3,4,64,128]{3,2,1,0:T(8,128)} %velocity_ref.1) | copy-start | bytes 1179652
  92.7 58.8 %all-to-all-start.3 = ((f32[32,8,128]{2,1,0:T(8,128)}), f32[32,8,128]{2,1,0:T(8,128)S(1)}, u32[]{:S(2)}, u32[]{:S(2)}) async-start(f32[32,8,128]{2,1,0:T(8,128)} %shard_map.198), calls=%async_computation.3 | async-start | bytes 262144 | tf_op jit(solution)/shard_map/all_to_all | solution.py:475
  99.8 51.6 %copy-start.8 = (f32[3,64,128]{2,1,0:T(8,128)S(1)}, f32[3,64,128]{2,1,0:T(8,128)}, u32[]{:S(2)}) copy-start(f32[3,64,128]{2,1,0:T(8,128)} %iv_ref.3) | copy-start | bytes 294916
  99.8 51.6 %copy-start.11 = (f32[4,64,128]{2,1,0:T(8,128)S(1)}, f32[4,64,128]{2,1,0:T(8,128)}, u32[]{:S(2)}) copy-start(f32[4,64,128]{2,1,0:T(8,128)} %cohesion_ref.1) | copy-start | bytes 393220
  99.8 28.1 %collective-permute-start.2 = (f32[64,128]{1,0:T(8,128)S(1)}, f32[64,128]{1,0:T(8,128)S(1)}, u32[]{:S(2)}, u32[]{:S(2)}) collective-permute-start(f32[64,128]{1,0:T(8,128)S(1)} %get-tuple-element.12), channel_id=1, source_target_pairs={{0,1},{1,2},{2,3},{3,4},{4,5},{5,6},{6,7},{7,8},{8,9},{9,10},{10,1... | collective-permute-start | bytes 98312 | tf_op jit(solution)/shard_map/ppermute | solution.py:469
  102.2 25.8 %collective-permute-start.3 = (f32[64,128]{1,0:T(8,128)S(1)}, f32[64,128]{1,0:T(8,128)S(1)}, u32[]{:S(2)}, u32[]{:S(2)}) collective-permute-start(f32[64,128]{1,0:T(8,128)S(1)} %get-tuple-element.13), channel_id=1, source_target_pairs={{0,15},{1,0},{2,1},{3,2},{4,3},{5,4},{6,5},{7,6},{8,7},{9,8},{10,9... | collective-permute-start | bytes 98312 | tf_op jit(solution)/shard_map/ppermute | solution.py:469
  109.2 9.7 %collective-permute-start = (f32[16,128]{1,0:T(8,128)S(1)}, f32[16,128]{1,0:T(8,128)S(1)}, u32[]{:S(2)}, u32[]{:S(2)}) collective-permute-start(f32[16,128]{1,0:T(8,128)S(1)} %get-tuple-element.10), channel_id=1, source_target_pairs={{0,16},{16,32},{32,48},{48,64},{64,80},{80,96},{96,112},{112,128},... | collective-permute-start | bytes 24584 | tf_op jit(solution)/shard_map/ppermute | solution.py:469
  117.0 11.0 %collective-permute-start.1 = (f32[16,128]{1,0:T(8,128)S(1)}, f32[16,128]{1,0:T(8,128)S(1)}, u32[]{:S(2)}, u32[]{:S(2)}) collective-permute-start(f32[16,128]{1,0:T(8,128)S(1)} %get-tuple-element.11), channel_id=1, source_target_pairs={{0,496},{16,0},{32,16},{48,32},{64,48},{80,64},{96,80},{112,96},{1... | collective-permute-start | bytes 24584 | tf_op jit(solution)/shard_map/ppermute | solution.py:469
  128.7 22.7 %collective-permute-start.6 = (f32[64,128]{1,0:T(8,128)S(1)}, f32[64,128]{1,0:T(8,128)S(1)}, u32[]{:S(2)}, u32[]{:S(2)}) collective-permute-start(f32[64,128]{1,0:T(8,128)S(1)} %get-tuple-element.16), channel_id=1, source_target_pairs={{0,1},{1,2},{2,3},{3,4},{4,5},{5,6},{6,7},{7,8},{8,9},{9,10},{10,1... | collective-permute-start | bytes 98312 | tf_op jit(solution)/shard_map/ppermute | solution.py:469
  130.6 20.8 %collective-permute-start.7 = (f32[64,128]{1,0:T(8,128)S(1)}, f32[64,128]{1,0:T(8,128)S(1)}, u32[]{:S(2)}, u32[]{:S(2)}) collective-permute-start(f32[64,128]{1,0:T(8,128)S(1)} %get-tuple-element.17), channel_id=1, source_target_pairs={{0,15},{1,0},{2,1},{3,2},{4,3},{5,4},{6,5},{7,6},{8,7},{9,8},{10,9... | collective-permute-start | bytes 98312 | tf_op jit(solution)/shard_map/ppermute | solution.py:469
  137.9 4.4 %collective-permute-start.4 = (f32[16,128]{1,0:T(8,128)S(1)}, f32[16,128]{1,0:T(8,128)S(1)}, u32[]{:S(2)}, u32[]{:S(2)}) collective-permute-start(f32[16,128]{1,0:T(8,128)S(1)} %get-tuple-element.14), channel_id=1, source_target_pairs={{0,16},{16,32},{32,48},{48,64},{64,80},{80,96},{96,112},{112,128},... | collective-permute-start | bytes 24584 | tf_op jit(solution)/shard_map/ppermute | solution.py:469
  140.4 11.0 %collective-permute-start.5 = (f32[16,128]{1,0:T(8,128)S(1)}, f32[16,128]{1,0:T(8,128)S(1)}, u32[]{:S(2)}, u32[]{:S(2)}) collective-permute-start(f32[16,128]{1,0:T(8,128)S(1)} %get-tuple-element.15), channel_id=1, source_target_pairs={{0,496},{16,0},{32,16},{48,32},{64,48},{80,64},{96,80},{112,96},{1... | collective-permute-start | bytes 24584 | tf_op jit(solution)/shard_map/ppermute | solution.py:469

commit v2 on v1

--- a/solution.py
+++ b/solution.py
@@ -1,6 +1,3 @@
-from functools import partial
-import math
-
 import jax
 import jax.numpy as jnp
 import ml_dtypes
@@ -17,7 +14,7 @@
 NF = 512
 SCALE = 1.0 / 2048.0
 VMEM = pl.BlockSpec(memory_space=pltpu.VMEM)
-PARAMS = pltpu.CompilerParams(vmem_limit_bytes=48 * 1024 * 1024)
+PARAMS = pltpu.CompilerParams(vmem_limit_bytes=16 * 1024 * 1024)
 
 
 def split_table(table):
@@ -60,19 +57,25 @@
 
 
 def dip_order():
-    lane = np.arange(NF)
-    return 16 * (lane % 32) + lane // 32
+    lane = np.arange(128)
+    return 4 * (lane % 32) + lane // 32
 
 
 def dip_tables():
-    theta = angles(np.arange(NF), dip_order(), NF)
-    forward = split_table(np.concatenate([np.cos(theta), np.sin(theta)], axis=1))
-    inverse = split_table(np.concatenate([np.cos(theta).T, np.sin(theta).T], axis=1))
-    return forward, inverse
+    theta = angles(np.arange(128), dip_order(), 128)
+    forward = np.concatenate([np.cos(theta), np.sin(theta)], axis=1)
+    inverse = np.concatenate([np.cos(theta).T, np.sin(theta).T], axis=1)
+    return split_table(forward) + split_table(inverse)
+
+
+def dip_inner_twiddle():
+    theta = angles(np.arange(4), np.arange(128), 512)
+    return np.stack([np.cos(theta), np.sin(theta)], axis=1).astype(np.float32)
 
 
 def dip_twiddle():
-    theta = angles(np.arange(4), dip_order(), 2048).reshape(2, 2, 1, NF)
+    f = (4 * dip_order()[None, :] + np.arange(4)[:, None]).reshape(NF)
+    theta = angles(np.arange(4), f, 2048).reshape(2, 2, 1, NF)
     theta = np.broadcast_to(theta, (2, 2, 4, NF)).reshape(2, 8, NF)
     return np.stack([np.cos(theta), np.sin(theta)], axis=1).astype(np.float32)
 
@@ -97,6 +100,39 @@
     high, low = halves(value)
     both = dot(jnp.concatenate([high, low], axis=0), table_high)
     return both[:rows] + both[rows:] + dot(high, table_low)
+
+
+def radix_four(values, sign):
+    (r0, i0), (r1, i1), (r2, i2), (r3, i3) = values
+    ar, ai, br, bi = r0 + r2, i0 + i2, r0 - r2, i0 - i2
+    cr, ci, dr, di = r1 + r3, i1 + i3, sign * (r1 - r3), sign * (i1 - i3)
+    return [
+        (ar + cr, ai + ci),
+        (br - di, bi + dr),
+        (ar - cr, ai - ci),
+        (br + di, bi - dr),
+    ]
+
+
+def turn(real, imag, cos, sin, sign):
+    if sign > 0:
+        return real * cos - imag * sin, imag * cos + real * sin
+    return real * cos + imag * sin, imag * cos - real * sin
+
+
+def dip_transform(values, high, low, sign):
+    stacked = jnp.concatenate([part for pair in values for part in pair], axis=0)
+    product = rows_dot(stacked, high, low)
+    out = []
+    for n in range(4):
+        real, imag = product[96 * n : 96 * n + 48], product[96 * n + 48 : 96 * (n + 1)]
+        out.append(
+            (
+                real[:, :128] - sign * imag[:, 128:],
+                imag[:, :128] + sign * real[:, 128:],
+            )
+        )
+    return out
 
 
 def roll(value, shift, axis):
@@ -137,7 +173,9 @@
     out_ref[:, 7, :] = zero
 
 
-def strike_forward_kernel(in_ref, strike_ref, twiddle_ref, high_ref, low_ref, out_ref):
+def strike_forward_kernel(
+    in_ref, strike_ref, twiddle_ref, high_ref, low_ref, after_ref, also_ref, out_ref
+):
     value = jnp.concatenate([in_ref[:, m, :] for m in range(6)], axis=1)
     value = stacked_dot(strike_ref[...], value)
     cos, sin = twiddle_ref[0], twiddle_ref[1]
@@ -157,7 +195,9 @@
             out_ref[32 * (8 * t + b) : 32 * (8 * t + b + 1), :] = parts[b]
 
 
-def strike_inverse_kernel(in_ref, strike_ref, twiddle_ref, high_ref, low_ref, out_ref):
+def strike_inverse_kernel(
+    in_ref, strike_ref, twiddle_ref, high_ref, low_ref, after_ref, also_ref, out_ref
+):
     columns = []
     for t in range(2):
         columns.append(
@@ -192,23 +232,36 @@
 
 
 def dip_kernel(
-    in_ref, weight_ref, past_ref, twiddle_ref, fh_ref, fl_ref, ih_ref, il_ref, out_ref
+    in_ref, weight_ref, past_ref, twiddle_ref, inner_ref,
+    fh_ref, fl_ref, ih_ref, il_ref, after_ref, also_ref, out_ref,
 ):
-    flipped = in_ref[...].T[:96]
-    product = rows_dot(flipped, fh_ref[...], fl_ref[...])
+    flipped = in_ref[...].T
+    values = []
+    for v in range(4):
+        lanes = slice(128 * v, 128 * (v + 1))
+        values.append(
+            [
+                jnp.concatenate(
+                    [flipped[16 * m + 8 * ri : 16 * m + 8 * ri + 8, lanes] for m in range(6)],
+                    axis=0,
+                )
+                for ri in range(2)
+            ]
+        )
+    inner = [(inner_ref[b, 0:1, :], inner_ref[b, 1:2, :]) for b in range(4)]
+    values = radix_four(values, -1)
+    values = [turn(*values[b], *inner[b], -1) for b in range(4)]
+    values = dip_transform(values, fh_ref[...], fl_ref[...], -1)
+    real = jnp.concatenate([pair[0] for pair in values], axis=1)
+    imag = jnp.concatenate([pair[1] for pair in values], axis=1)
     top = row_of((8, NF)) < 4
     sign = jnp.where(top, 1.0, -1.0).astype(jnp.float32)
-    early = lane_of((8, NF)) % 32 < 16
-    inverse_rows = []
+    reals, imags = [], []
     for c in range(3):
-        even, odd = [], []
         turned = []
         for s in range(2):
-            at = 32 * c + 16 * s
-            real = product[at : at + 8, :NF] + product[at + 8 : at + 16, NF:]
-            imag = product[at + 8 : at + 16, :NF] - product[at : at + 8, NF:]
-            cos, sin = twiddle_ref[s, 0], twiddle_ref[s, 1]
-            turned.append((real * cos + imag * sin, imag * cos - real * sin))
+            rows = slice(16 * c + 8 * s, 16 * c + 8 * s + 8)
+            turned.append(turn(real[rows], imag[rows], twiddle_ref[s, 0], twiddle_ref[s, 1], -1))
         even = [turned[0][ri] + turned[1][ri] for ri in range(2)]
         odd = [turned[0][ri] - turned[1][ri] for ri in range(2)]
         odd = [jnp.where(top, odd[0], odd[1]), jnp.where(top, odd[1], -odd[0])]
@@ -228,19 +281,23 @@
             jnp.where(top, response[1][1], response[1][0]),
         ]
         for s in range(2):
-            if s == 0:
-                real, imag = even[0] + odd[0], even[1] + odd[1]
-            else:
-                real, imag = even[0] - odd[0], even[1] - odd[1]
-            cos, sin = twiddle_ref[s, 0], twiddle_ref[s, 1]
-            inverse_rows += [real * cos - imag * sin, imag * cos + real * sin]
-    product = rows_dot(jnp.concatenate(inverse_rows, axis=0), ih_ref[...], il_ref[...])
+            pair = [even[ri] + odd[ri] if s == 0 else even[ri] - odd[ri] for ri in range(2)]
+            pair = turn(*pair, twiddle_ref[s, 0], twiddle_ref[s, 1], 1)
+            reals.append(pair[0])
+            imags.append(pair[1])
+    real, imag = jnp.concatenate(reals, axis=0), jnp.concatenate(imags, axis=0)
+    values = [
+        (real[:, 128 * b : 128 * (b + 1)], imag[:, 128 * b : 128 * (b + 1)]) for b in range(4)
+    ]
+    values = dip_transform(values, ih_ref[...], il_ref[...], 1)
+    values = [turn(*values[b], *inner[b], 1) for b in range(4)]
+    values = radix_four(values, 1)
+    real = jnp.concatenate([pair[0] for pair in values], axis=1)
+    imag = jnp.concatenate([pair[1] for pair in values], axis=1)
     groups = []
-    for c in range(3):
-        for s in range(2):
-            at = 32 * c + 16 * s
-            groups.append(product[at : at + 8, :NF] - product[at + 8 : at + 16, NF:])
-            groups.append(product[at + 8 : at + 16, :NF] + product[at : at + 8, NF:])
+    for m in range(6):
+        groups += [real[8 * m : 8 * m + 8], imag[8 * m : 8 * m + 8]]
+    early = lane_of((8, NF)) % 32 < 16
     edges = []
     for c in range(3):
         for ri in range(2):
@@ -254,36 +311,73 @@
     out_ref[...] = jnp.concatenate(groups, axis=0).T
 
 
-def past_kernel(kernel_ref, history_ref, out_ref):
+def mode_groups(tiles, rows_ref):
     for a in range(4):
-        weights = [kernel_ref[h + 1, a, 0] for h in range(6)]
-        for z in range(2):
-            for c in range(3):
-                total = weights[0] * history_ref[0, z, c, a, 0]
+        rows_ref[:, a, :] = tiles[a]
+        rows_ref[:, 4 + a, :] = tiles[a]
+    block = lane_of((8, 128)) // 32
+    top = row_of((8, 128)) < 4
+    columns = []
+    for t in range(4):
+        parts = [rows_ref[4 * n + t] for n in range(4)]
+        for step in (1, 2):
+            upper = (block // step) % 2 == 1
+            for n in range(4):
+                if (n // step) % 2 == 0:
+                    low, high = parts[n], parts[n + step]
+                    parts[n] = jnp.where(upper, roll(high, 32 * step, 1), low)
+                    parts[n + step] = jnp.where(upper, high, roll(low, -32 * step, 1))
+        columns.append([jnp.where(top, parts[n], parts[2 + n]) for n in range(2)])
+    return [jnp.concatenate([column[n] for column in columns], axis=1) for n in range(2)]
+
+
+def past_kernel(kernel_ref, history_ref, weight_ref, out_ref, rows_ref):
+    groups = mode_groups([kernel_ref[0, a, 0] for a in range(4)], rows_ref.at[6])
+    for parity in range(2):
+        weight_ref[parity] = groups[parity]
+    for z in range(2):
+        for c in range(3):
+            tiles = []
+            for a in range(4):
+                total = kernel_ref[1, a, 0] * history_ref[0, z, c, a, 0]
                 for h in range(1, 6):
-                    total = total + weights[h] * history_ref[h, z, c, a, 0]
-                out_ref[z, c, a] = total
-
-
-def edge_kernel(fields_ref, xlo_ref, xhi_ref, ylo_ref, yhi_ref, *, across, along):
+                    total = total + kernel_ref[h + 1, a, 0] * history_ref[h, z, c, a, 0]
+                tiles.append(total)
+            groups = mode_groups(tiles, rows_ref.at[3 * z + c])
+            for parity in range(2):
+                out_ref[c, parity, z] = groups[parity]
+
+
+def strike_edges(fields_ref, chosen):
     pad = jnp.zeros((4, 128), jnp.float32)
-    xlo, xhi = [], []
+    low = [fields_ref[n, z, 0:1, :] for n in chosen for z in range(4)]
+    high = [fields_ref[n, z, 63:64, :] for n in chosen for z in range(4)]
+    return jnp.concatenate(low + [pad], axis=0), jnp.concatenate(high + [pad], axis=0)
+
+
+def dip_edges(fields_ref, chosen):
     lane = lane_of((64, 128))
-    ylo = jnp.zeros((64, 128), jnp.float32)
-    yhi = jnp.zeros((64, 128), jnp.float32)
-    for n in range(3):
+    low = jnp.zeros((64, 128), jnp.float32)
+    high = jnp.zeros((64, 128), jnp.float32)
+    for i, n in enumerate(chosen):
         for z in range(4):
-            field = fields_ref[across[n], z]
-            xlo.append(field[0:1])
-            xhi.append(field[63:64])
-            field = fields_ref[along[n], z]
-            to = 4 * n + z
-            ylo = jnp.where(lane == to, roll(field, to, 1), ylo)
-            yhi = jnp.where(lane == to, roll(field, to - 127, 1), yhi)
-    xlo_ref[...] = jnp.concatenate(xlo + [pad], axis=0)
-    xhi_ref[...] = jnp.concatenate(xhi + [pad], axis=0)
-    ylo_ref[...] = ylo
-    yhi_ref[...] = yhi
+            to = 4 * i + z
+            low = jnp.where(lane == to, roll(fields_ref[n, z], to, 1), low)
+            high = jnp.where(lane == to, roll(fields_ref[n, z], to - 127, 1), high)
+    return low, high
+
+
+def strike_edge_kernel(fields_ref, low_ref, high_ref):
+    low_ref[...], high_ref[...] = strike_edges(fields_ref, (0, 3, 4))
+
+
+def dip_edge_kernel(fields_ref, after_ref, low_ref, high_ref):
+    low_ref[...], high_ref[...] = dip_edges(fields_ref, (3, 1, 5))
+
+
+def hold_kernel(low_ref, high_ref, after_ref, low_out_ref, high_out_ref):
+    low_out_ref[...] = low_ref[...]
+    high_out_ref[...] = high_ref[...]
 
 
 def strike_diff(field, low, high):
@@ -300,7 +394,10 @@
     return 0.5 * (after - before)
 
 
-def velocity_kernel(velocity_ref, stress_ref, xlo_ref, xhi_ref, ylo_ref, yhi_ref, out_ref):
+def velocity_kernel(
+    velocity_ref, stress_ref, xlo_ref, xhi_ref, ylo_ref, yhi_ref,
+    out_ref, xlo_out_ref, xhi_out_ref, ylo_out_ref, yhi_out_ref,
+):
     across, along, deep = (0, 3, 4), (3, 1, 5), (4, 5, 2)
     ylo, yhi = ylo_ref[...], yhi_ref[...]
     for n in range(3):
@@ -314,6 +411,8 @@
             if z > 0:
                 total = total - 0.5 * stress_ref[deep[n], z - 1]
             out_ref[n, z] = velocity_ref[n, z] + COURANT * total
+    xlo_out_ref[...], xhi_out_ref[...] = strike_edges(out_ref, (0, 1, 2))
+    ylo_out_ref[...], yhi_out_ref[...] = dip_edges(out_ref, (0, 1, 2))
 
 
 def slab_kernel(
@@ -389,69 +488,71 @@
     return jax.ShapeDtypeStruct(shape, jnp.float32)
 
 
-def call(kernel, out_shape, arguments, scratch=()):
+def call(kernel, out_shape, arguments, after=(), scratch=()):
     many = isinstance(out_shape, tuple)
     return pl.pallas_call(
         kernel,
         out_shape=out_shape,
-        in_specs=[VMEM] * len(arguments),
+        in_specs=[VMEM] * len(arguments) + [pl.BlockSpec(memory_space=pl.ANY)] * len(after),
         out_specs=(VMEM,) * len(out_shape) if many else VMEM,
         scratch_shapes=list(scratch),
         compiler_params=PARAMS,
-    )(*arguments)
+    )(*arguments, *after)
 
 
 def scatter(iv):
-    return call(scatter_kernel, f32(32, 8, 128), (iv,), [pltpu.VMEM((128, 64), jnp.float32)])
-
-
-def strike_forward(arrived):
+    return call(
+        scatter_kernel, f32(32, 8, 128), (iv,), scratch=[pltpu.VMEM((128, 64), jnp.float32)]
+    )
+
+
+def strike_forward(arrived, after):
     forward, _ = strike_tables()
     (high, low), _ = cell_tables()
-    return call(
-        strike_forward_kernel, f32(512, 128), (arrived, forward, strike_twiddle(), high, low)
-    )
-
-
-def strike_inverse(arrived):
+    arguments = (arrived, forward, strike_twiddle(), high, low)
+    return call(strike_forward_kernel, f32(512, 128), arguments, after)
+
+
+def strike_inverse(arrived, after):
     _, inverse = strike_tables()
     _, (high, low) = cell_tables()
+    arguments = (arrived, inverse, strike_twiddle(), high, low)
+    return call(strike_inverse_kernel, f32(32, 8, 128), arguments, after)
+
+
+def dip(arrived, weight, past, after):
+    tables = (dip_twiddle(), dip_inner_twiddle(), *dip_tables())
+    arguments = (arrived, weight, past, *tables)
+    return call(dip_kernel, f32(512, 128), arguments, after)
+
+
+def past_terms(kernel, history):
     return call(
-        strike_inverse_kernel, f32(32, 8, 128), (arrived, inverse, strike_twiddle(), high, low)
-    )
-
-
-def dip(arrived, weight, past):
-    forward, inverse = dip_tables()
+        past_kernel,
+        (f32(2, 8, NF), f32(3, 2, 2, 8, NF)),
+        (kernel, history),
+        scratch=[pltpu.VMEM((7, 16, 8, 128), jnp.float32)],
+    )
+
+
+def stress_strike_edges(stress):
+    return call(strike_edge_kernel, (f32(16, 128),) * 2, (stress,))
+
+
+def stress_dip_edges(stress, after):
+    return call(dip_edge_kernel, (f32(64, 128),) * 2, (stress,), (after,))
+
+
+def hold(low, high, after):
+    return call(hold_kernel, (f32(*low.shape),) * 2, (low, high), (after,))
+
+
+def velocity_before(velocity, stress, halo):
     return call(
-        dip_kernel, f32(512, 128), (arrived, weight, past, dip_twiddle(), *forward, *inverse)
-    )
-
-
-def mode_order(value):
-    lead = value.shape[:-3]
-    n = len(lead)
-    value = value.reshape(*lead, 4, 16, 2, 2, 32)
-    value = jnp.transpose(value, (*range(n), n + 3, n + 2, n, n + 1, n + 4))
-    return value.reshape(*lead, 2, 8, NF)
-
-
-def past_terms(kernel, history):
-    past = call(past_kernel, f32(2, 3, 4, 16, 128), (kernel, history))
-    past = jnp.moveaxis(mode_order(past), 0, 2)
-    return mode_order(kernel[0, :, 0]), past
-
-
-def edges(fields, across, along):
-    return call(
-        partial(edge_kernel, across=across, along=along),
-        (f32(16, 128), f32(16, 128), f32(64, 128), f32(64, 128)),
-        (fields,),
-    )
-
-
-def velocity_before(velocity, stress, halo):
-    return call(velocity_kernel, f32(3, 4, 64, 128), (velocity, stress, *halo))
+        velocity_kernel,
+        (f32(3, 4, 64, 128), f32(16, 128), f32(16, 128), f32(64, 128), f32(64, 128)),
+        (velocity, stress, *halo),
+    )
 
 
 def slab(arrived, before, stress, cohesion, iv, halo):
@@ -459,16 +560,16 @@
         slab_kernel,
         (f32(3, 4, 64, 128), f32(6, 4, 64, 128)),
         (arrived, before, stress, cohesion, iv, *halo),
-        [pltpu.VMEM((128, 128), jnp.float32), pltpu.VMEM((128, 128), jnp.float32)],
-    )
-
-
-def exchange(xlo, xhi, ylo, yhi):
-    def shift(value, axis, step):
-        count = lax.axis_size(axis)
-        return lax.ppermute(value, axis, [(i, (i + step) % count) for i in range(count)])
-
-    return (shift(xhi, "bx", 1), shift(xlo, "bx", -1), shift(yhi, "by", 1), shift(ylo, "by", -1))
+        scratch=[pltpu.VMEM((128, 128), jnp.float32), pltpu.VMEM((128, 128), jnp.float32)],
+    )
+
+
+def exchange(axis, low, high):
+    count = lax.axis_size(axis)
+    return (
+        lax.ppermute(high, axis, [(i, (i + 1) % count) for i in range(count)]),
+        lax.ppermute(low, axis, [(i, (i - 1) % count) for i in range(count)]),
+    )
 
 
 def strike_swap(value):
@@ -483,14 +584,21 @@
 
 def local(interface_velocity, history, kernel, velocity, stress, cohesion):
     arrived = strike_swap(scatter(interface_velocity))
+    strike_halo = exchange("bx", *stress_strike_edges(stress))
+    sent = strike_forward(arrived, strike_halo)
+    arrived = whole_swap(sent)
+    dip_halo = exchange("by", *stress_dip_edges(stress, sent))
     weight, past = past_terms(kernel, history)
-    stress_halo = exchange(*edges(stress, (0, 3, 4), (3, 1, 5)))
-    arrived = whole_swap(strike_forward(arrived))
-    before = velocity_before(velocity, stress, stress_halo)
-    halo = exchange(*edges(before, (0, 1, 2), (0, 1, 2)))
-    arrived = whole_swap(dip(arrived, weight, past))
-    arrived = strike_swap(strike_inverse(arrived))
-    return slab(arrived, before, stress, cohesion, interface_velocity, halo)
+    sent = dip(arrived, weight, past, dip_halo)
+    arrived = whole_swap(sent)
+    before, *edges = velocity_before(velocity, stress, (*strike_halo, *dip_halo))
+    strike_halo = exchange("bx", *hold(edges[0], edges[1], sent))
+    sent = strike_inverse(arrived, strike_halo)
+    arrived = strike_swap(sent)
+    dip_halo = exchange("by", *hold(edges[2], edges[3], sent))
+    return slab(
+        arrived, before, stress, cohesion, interface_velocity, (*strike_halo, *dip_halo)
+    )
 
 
 def solution(mesh):

time: 154 us -> 130 us (0.84)
  the two profiles are of different devices: /device:TPU:57 before, /device:TPU:1 now
where the time goes in v2:
time: 130 us
  starting transfers between devices  93.7 us (72%)
  waiting for transfers between devices  23.2 us (18%)
  Pallas kernels  9.59 us (7%)
  local copies, waits for them, and re-layouts  2.13 us (2%)
    all_to_all x2, starting transfers between devices, whole_swap(): lax.all_to_all(value, ('by', 'bx'), split_axis=0, concat_axis=0, tiled=True)  33 us
    all_to_all x2, starting transfers between devices, strike_swap(): return lax.all_to_all(value, 'bx', split_axis=0, concat_axis=0, tiled=True)  27.1 us
    ppermute x4, starting transfers between devices, exchange(): lax.ppermute(low, axis, [(i, (i - 1) % count) for i in range(count)])  20.7 us
    ppermute x4, starting transfers between devices, exchange(): lax.ppermute(high, axis, [(i, (i + 1) % count) for i in range(count)])  12.8 us
    all_to_all x2, waiting for transfers between devices, whole_swap(): lax.all_to_all(value, ('by', 'bx'), split_axis=0, concat_axis=0, tiled=True)  12.5 us
    pallas_call x11, Pallas kernels, call(): pl.pallas_call(kernel, out_shape=out_shape, in_specs=[VMEM] * len(argumen...  9.59 us
    all_to_all x2, waiting for transfers between devices, strike_swap(): return lax.all_to_all(value, 'bx', split_axis=0, concat_axis=0, tiled=True)  5.6 us
    ppermute x4, waiting for transfers between devices, exchange(): lax.ppermute(low, axis, [(i, (i - 1) % count) for i in range(count)])  5.12 us
  transfers between devices with their start and end apart: 12, of which 7 were waited for; matrix products, arithmetic and copies ran while one was open for 0% of the time, Pallas kernels for 2%

profile of v2, /device:TPU:1, one launch (start us, length us, event | category | flops | bytes accessed | tf_op | source)
XLA Modules:
  0.0 129.7 jit_solution(4090417851075164683)
XLA Ops:
  0.6 0.0 copy-start.19
  0.7 0.9 copy-done.4
  1.5 1.0 shard_map.203
  2.6 17.2 %all-to-all-start = ((f32[32,8,128]{2,1,0:T(8,128)}), f32[32,8,128]{2,1,0:T(8,128)S(1)}, u32[]{:S(2)}, u32[]{:S(2)}) async-start(f32[32,8,128]{2,1,0:T(8,128)} %shard_map.203), calls=%async_computation | async-start | bytes 262144 | tf_op jit(solution)/shard_map/all_to_all | solution.py:576
  19.8 1.1 copy-done
  21.0 3.7 %collective-permute-start = (f32[16,128]{1,0:T(8,128)S(1)}, f32[16,128]{1,0:T(8,128)S(1)}, u32[]{:S(2)}, u32[]{:S(2)}) collective-permute-start(f32[16,128]{1,0:T(8,128)S(1)} %get-tuple-element.17), channel_id=1, source_target_pairs={{0,16},{16,32},{32,48},{48,64},{64,80},{80,96},{96,112},{112,128},... | collective-permute-start | bytes 24584 | tf_op jit(solution)/shard_map/ppermute | solution.py:570
  24.7 1.9 %collective-permute-start.1 = (f32[16,128]{1,0:T(8,128)S(1)}, f32[16,128]{1,0:T(8,128)S(1)}, u32[]{:S(2)}, u32[]{:S(2)}) collective-permute-start(f32[16,128]{1,0:T(8,128)S(1)} %get-tuple-element.18), channel_id=1, source_target_pairs={{0,496},{16,0},{32,16},{48,32},{64,48},{80,64},{96,80},{112,96},{1... | collective-permute-start | bytes 24584 | tf_op jit(solution)/shard_map/ppermute | solution.py:571
  26.6 3.3 %collective-permute-done.1.also_ref.xhi_ref = f32[16,128]{1,0:T(8,128)S(1)} collective-permute-done((f32[16,128]{1,0:T(8,128)S(1)}, f32[16,128]{1,0:T(8,128)S(1)}, u32[]{:S(2)}, u32[]{:S(2)}) %collective-permute-start.1) | collective-permute-done | bytes 8224 | tf_op jit(solution)/shard_map/ppermute | solution.py:571
  29.9 2.9 %all-to-all-done.in_ref = f32[32,8,128]{2,1,0:T(8,128)S(1)} async-done(((f32[32,8,128]{2,1,0:T(8,128)}), f32[32,8,128]{2,1,0:T(8,128)S(1)}, u32[]{:S(2)}, u32[]{:S(2)}) %all-to-all-start) | async-done | bytes 131104 | tf_op jit(solution)/shard_map/all_to_all | solution.py:576
  32.8 1.4 %shard_map.205.after_ref = f32[512,128]{1,0:T(8,128)} custom-call(f32[32,8,128]{2,1,0:T(8,128)S(1)} %all-to-all-done.in_ref, bf16[64,96]{1,0:T(8,128)(2,1)S(1)} %copy-done.19, f32[2,32,128]{2,1,0:T(8,128)S(1)} %copy-done.8, bf16[256,256]{1,0:T(8,128)(2,1)S(1)} %copy-done.12, bf16[256,256]{1,0:T(8,128)(2,1)S(1)} %copy-done.11, ...), custom_call_target="tpu_custom_call" | custom-call | tf_op jit(solution)/shard_map/pallas_call | solution.py:493
  34.2 18.7 %all-to-all-start.1 = ((f32[512,1,128]{2,1,0:T(1,128)}), f32[512,1,128]{2,1,0:T(1,128)S(1)}, u32[]{:S(2)}, u32[]{:S(2)}) async-start(f32[512,1,128]{2,1,0:T(1,128)} %bitcast.1), calls=%async_computation.1 | async-start | bytes 524288 | tf_op jit(solution)/shard_map/all_to_all | solution.py:581
  52.8 0.0 copy-start.13
  52.9 0.0 copy-start.14
  52.9 0.3 shard_map.207
  53.2 3.7 %collective-permute-start.2 = (f32[64,128]{1,0:T(8,128)S(1)}, f32[64,128]{1,0:T(8,128)S(1)}, u32[]{:S(2)}, u32[]{:S(2)}) collective-permute-start(f32[64,128]{1,0:T(8,128)S(1)} %get-tuple-element.21), channel_id=1, source_target_pairs={{0,1},{1,2},{2,3},{3,4},{4,5},{5,6},{6,7},{7,8},{8,9},{9,10},{10,1... | collective-permute-start | bytes 98312 | tf_op jit(solution)/shard_map/ppermute | solution.py:570
  56.9 7.0 %collective-permute-start.3 = (f32[64,128]{1,0:T(8,128)S(1)}, f32[64,128]{1,0:T(8,128)S(1)}, u32[]{:S(2)}, u32[]{:S(2)}) collective-permute-start(f32[64,128]{1,0:T(8,128)S(1)} %get-tuple-element.22), channel_id=1, source_target_pairs={{0,15},{1,0},{2,1},{3,2},{4,3},{5,4},{6,5},{7,6},{8,7},{9,8},{10,9... | collective-permute-start | bytes 98312 | tf_op jit(solution)/shard_map/ppermute | solution.py:571
  63.9 1.2 shard_map.206
  65.1 5.0 %all-to-all-done.1 = f32[512,1,128]{2,1,0:T(1,128)S(1)} async-done(((f32[512,1,128]{2,1,0:T(1,128)}), f32[512,1,128]{2,1,0:T(1,128)S(1)}, u32[]{:S(2)}, u32[]{:S(2)}) %all-to-all-start.1) | async-done | bytes 262176 | tf_op jit(solution)/shard_map/all_to_all | solution.py:581
  70.1 1.8 %shard_map.208.after_ref = f32[512,128]{1,0:T(8,128)} custom-call(f32[512,128]{1,0:T(8,128)S(1)} %bitcast.9, f32[2,8,512]{2,1,0:T(8,128)S(1)} %get-tuple-element.19.weight_ref, f32[3,2,2,8,512]{4,3,2,1,0:T(8,128)S(1)} %get-tuple-element.20.past_ref, f32[2,2,8,512]{3,2,1,0:T(8,128)S(1)} %copy-done.17, f32[4,2,128]{2,1,0:T(2,128)S(1)} %copy-done.20, ...), custom_call_target="tpu_custom_call" | custom-call | tf_op jit(solution)/shard_map/pallas_call | solution.py:493
  71.9 14.4 %all-to-all-start.2 = ((f32[512,1,128]{2,1,0:T(1,128)}), f32[512,1,128]{2,1,0:T(1,128)S(1)}, u32[]{:S(2)}, u32[]{:S(2)}) async-start(f32[512,1,128]{2,1,0:T(1,128)} %bitcast.4), calls=%async_computation.2 | async-start | bytes 524288 | tf_op jit(solution)/shard_map/all_to_all | solution.py:581
  86.3 0.7 shard_map.209
  87.0 3.5 %collective-permute-start.4 = (f32[16,128]{1,0:T(8,128)S(1)}, f32[16,128]{1,0:T(8,128)S(1)}, u32[]{:S(2)}, u32[]{:S(2)}) collective-permute-start(f32[16,128]{1,0:T(8,128)S(1)} %get-tuple-element.25), channel_id=1, source_target_pairs={{0,16},{16,32},{32,48},{48,64},{64,80},{80,96},{96,112},{112,128},... | collective-permute-start | bytes 24584 | tf_op jit(solution)/shard_map/ppermute | solution.py:570
  90.6 4.6 %collective-permute-start.5 = (f32[16,128]{1,0:T(8,128)S(1)}, f32[16,128]{1,0:T(8,128)S(1)}, u32[]{:S(2)}, u32[]{:S(2)}) collective-permute-start(f32[16,128]{1,0:T(8,128)S(1)} %get-tuple-element.26), channel_id=1, source_target_pairs={{0,496},{16,0},{32,16},{48,32},{64,48},{80,64},{96,80},{112,96},{1... | collective-permute-start | bytes 24584 | tf_op jit(solution)/shard_map/ppermute | solution.py:571
  95.2 0.8 collective-permute-done.5.also_ref.xhi_ref
  96.0 7.5 %all-to-all-done.2 = f32[512,1,128]{2,1,0:T(1,128)S(1)} async-done(((f32[512,1,128]{2,1,0:T(1,128)}), f32[512,1,128]{2,1,0:T(1,128)S(1)}, u32[]{:S(2)}, u32[]{:S(2)}) %all-to-all-start.2) | async-done | bytes 262176 | tf_op jit(solution)/shard_map/all_to_all | solution.py:581
  103.5 1.5 %shard_map.211.after_ref = f32[32,8,128]{2,1,0:T(8,128)} custom-call(f32[512,128]{1,0:T(8,128)S(1)} %bitcast.8, bf16[32,192]{1,0:T(8,128)(2,1)S(1)} %copy-done.18, f32[2,32,128]{2,1,0:T(8,128)S(1)} %copy-done.8, bf16[256,256]{1,0:T(8,128)(2,1)S(1)} %copy-done.10, bf16[256,256]{1,0:T(8,128)(2,1)S(1)} %copy-done.9, ...), custom_call_target="tpu_custom_call" | custom-call | tf_op jit(solution)/shard_map/pallas_call | solution.py:493
  105.0 9.9 %all-to-all-start.3 = ((f32[32,8,128]{2,1,0:T(8,128)}), f32[32,8,128]{2,1,0:T(8,128)S(1)}, u32[]{:S(2)}, u32[]{:S(2)}) async-start(f32[32,8,128]{2,1,0:T(8,128)} %shard_map.211.after_ref), calls=%async_computation.3 | async-start | bytes 262144 | tf_op jit(solution)/shard_map/all_to_all | solution.py:576
  114.9 1.9 %collective-permute-start.6 = (f32[64,128]{1,0:T(8,128)S(1)}, f32[64,128]{1,0:T(8,128)S(1)}, u32[]{:S(2)}, u32[]{:S(2)}) collective-permute-start(f32[64,128]{1,0:T(8,128)S(1)} %get-tuple-element.30), channel_id=1, source_target_pairs={{0,1},{1,2},{2,3},{3,4},{4,5},{5,6},{6,7},{7,8},{8,9},{9,10},{10,1... | collective-permute-start | bytes 98312 | tf_op jit(solution)/shard_map/ppermute | solution.py:570
  116.9 7.3 %collective-permute-start.7 = (f32[64,128]{1,0:T(8,128)S(1)}, f32[64,128]{1,0:T(8,128)S(1)}, u32[]{:S(2)}, u32[]{:S(2)}) collective-permute-start(f32[64,128]{1,0:T(8,128)S(1)} %get-tuple-element.31), channel_id=1, source_target_pairs={{0,15},{1,0},{2,1},{3,2},{4,3},{5,4},{6,5},{7,6},{8,7},{9,8},{10,9... | collective-permute-start | bytes 98312 | tf_op jit(solution)/shard_map/ppermute | solution.py:571
  124.1 1.0 collective-permute-done.7.yhi_ref
  125.1 2.7 %all-to-all-done.3.in_ref = f32[32,8,128]{2,1,0:T(8,128)S(1)} async-done(((f32[32,8,128]{2,1,0:T(8,128)}), f32[32,8,128]{2,1,0:T(8,128)S(1)}, u32[]{:S(2)}, u32[]{:S(2)}) %all-to-all-start.3) | async-done | bytes 131104 | tf_op jit(solution)/shard_map/all_to_all | solution.py:576
  127.9 1.8 %shard_map.213 = (f32[3,4,64,128]{3,2,1,0:T(8,128)}, f32[6,4,64,128]{3,2,1,0:T(8,128)}) custom-call(f32[32,8,128]{2,1,0:T(8,128)S(1)} %all-to-all-done.3.in_ref, f32[3,4,64,128]{3,2,1,0:T(8,128)S(1)} %get-tuple-element.27.before_ref, f32[6,4,64,128]{3,2,1,0:T(8,128)S(1)} %copy-done.1, f32[4,64,128]{2,1,0:T(8,128)S(1)} %copy-done.7, ...), custom_call_target="tpu_custom_call" | custom-call | tf_op jit(solution)/shard_map/pallas_call | solution.py:493
  (45 shorter events, 0.1 us)
Async XLA Ops:
  0.6 32.1 %copy-start.19 = (bf16[64,96]{1,0:T(8,128)(2,1)S(1)}, bf16[64,96]{1,0:T(8,128)(2,1)}, u32[]{:S(2)}) copy-start(bf16[64,96]{1,0:T(8,128)(2,1)} %constant.26.clone.strike_ref) | copy-start | bytes 36868
  1.5 31.2 %copy-start.8 = (f32[2,32,128]{2,1,0:T(8,128)S(1)}, f32[2,32,128]{2,1,0:T(8,128)}, u32[]{:S(2)}) copy-start(f32[2,32,128]{2,1,0:T(8,128)} %constant.27.clone.twiddle_ref) | copy-start | bytes 98308
  1.5 31.2 %copy-start.11 = (bf16[256,256]{1,0:T(8,128)(2,1)S(1)}, bf16[256,256]{1,0:T(8,128)(2,1)}, u32[]{:S(2)}) copy-start(bf16[256,256]{1,0:T(8,128)(2,1)} %constant.29.clone.low_ref) | copy-start | bytes 393220
  1.5 31.2 %copy-start.12 = (bf16[256,256]{1,0:T(8,128)(2,1)S(1)}, bf16[256,256]{1,0:T(8,128)(2,1)}, u32[]{:S(2)}) copy-start(bf16[256,256]{1,0:T(8,128)(2,1)} %constant.28.clone.high_ref) | copy-start | bytes 393220
  2.6 30.2 %all-to-all-start = ((f32[32,8,128]{2,1,0:T(8,128)}), f32[32,8,128]{2,1,0:T(8,128)S(1)}, u32[]{:S(2)}, u32[]{:S(2)}) async-start(f32[32,8,128]{2,1,0:T(8,128)} %shard_map.203), calls=%async_computation | async-start | bytes 262144 | tf_op jit(solution)/shard_map/all_to_all | solution.py:576
  19.8 1.1 copy-start
  20.9 31.9 %copy-start.1 = (f32[6,4,64,128]{3,2,1,0:T(8,128)S(1)}, f32[6,4,64,128]{3,2,1,0:T(8,128)}, u32[]{:S(2)}) copy-start(f32[6,4,64,128]{3,2,1,0:T(8,128)} %stress_ref.3) | copy-start | bytes 2359300
  21.0 42.9 %copy-start.2 = (f32[6,2,3,4,1,16,128]{6,5,4,3,2,1,0:T(8,128)S(1)}, f32[6,2,3,4,1,16,128]{6,5,4,3,2,1,0:T(8,128)}, u32[]{:S(2)}) copy-start(f32[6,2,3,4,1,16,128]{6,5,4,3,2,1,0:T(8,128)} %history_ref.1) | copy-start | bytes 3538948
  21.0 42.9 %copy-start.6 = (f32[7,4,1,16,128]{4,3,2,1,0:T(8,128)S(1)}, f32[7,4,1,16,128]{4,3,2,1,0:T(8,128)}, u32[]{:S(2)}) copy-start(f32[7,4,1,16,128]{4,3,2,1,0:T(8,128)} %kernel_ref.1) | copy-start | bytes 688132
  21.0 5.6 %collective-permute-start = (f32[16,128]{1,0:T(8,128)S(1)}, f32[16,128]{1,0:T(8,128)S(1)}, u32[]{:S(2)}, u32[]{:S(2)}) collective-permute-start(f32[16,128]{1,0:T(8,128)S(1)} %get-tuple-element.17), channel_id=1, source_target_pairs={{0,16},{16,32},{32,48},{48,64},{64,80},{80,96},{96,112},{112,128},... | collective-permute-start | bytes 24584 | tf_op jit(solution)/shard_map/ppermute | solution.py:570
  24.7 5.3 %collective-permute-start.1 = (f32[16,128]{1,0:T(8,128)S(1)}, f32[16,128]{1,0:T(8,128)S(1)}, u32[]{:S(2)}, u32[]{:S(2)}) collective-permute-start(f32[16,128]{1,0:T(8,128)S(1)} %get-tuple-element.18), channel_id=1, source_target_pairs={{0,496},{16,0},{32,16},{48,32},{64,48},{80,64},{96,80},{112,96},{1... | collective-permute-start | bytes 24584 | tf_op jit(solution)/shard_map/ppermute | solution.py:571
  34.2 35.9 %all-to-all-start.1 = ((f32[512,1,128]{2,1,0:T(1,128)}), f32[512,1,128]{2,1,0:T(1,128)S(1)}, u32[]{:S(2)}, u32[]{:S(2)}) async-start(f32[512,1,128]{2,1,0:T(1,128)} %bitcast.1), calls=%async_computation.1 | async-start | bytes 524288 | tf_op jit(solution)/shard_map/all_to_all | solution.py:581
  52.8 17.2 %copy-start.13 = (bf16[128,256]{1,0:T(8,128)(2,1)S(1)}, bf16[128,256]{1,0:T(8,128)(2,1)}, u32[]{:S(2)}) copy-start(bf16[128,256]{1,0:T(8,128)(2,1)} %constant.35.clone.il_ref) | copy-start | bytes 196612
  52.9 17.2 %copy-start.14 = (bf16[128,256]{1,0:T(8,128)(2,1)S(1)}, bf16[128,256]{1,0:T(8,128)(2,1)}, u32[]{:S(2)}) copy-start(bf16[128,256]{1,0:T(8,128)(2,1)} %constant.34.clone.ih_ref) | copy-start | bytes 196612
  52.9 17.2 %copy-start.15 = (bf16[128,256]{1,0:T(8,128)(2,1)S(1)}, bf16[128,256]{1,0:T(8,128)(2,1)}, u32[]{:S(2)}) copy-start(bf16[128,256]{1,0:T(8,128)(2,1)} %constant.33.clone.fl_ref) | copy-start | bytes 196612
  52.9 17.2 %copy-start.16 = (bf16[128,256]{1,0:T(8,128)(2,1)S(1)}, bf16[128,256]{1,0:T(8,128)(2,1)}, u32[]{:S(2)}) copy-start(bf16[128,256]{1,0:T(8,128)(2,1)} %constant.32.clone.fh_ref) | copy-start | bytes 196612
  52.9 17.2 %copy-start.17 = (f32[2,2,8,512]{3,2,1,0:T(8,128)S(1)}, f32[2,2,8,512]{3,2,1,0:T(8,128)}, u32[]{:S(2)}) copy-start(f32[2,2,8,512]{3,2,1,0:T(8,128)} %constant.30.clone.twiddle_ref) | copy-start | bytes 196612
  52.9 17.2 %copy-start.20 = (f32[4,2,128]{2,1,0:T(2,128)S(1)}, f32[4,2,128]{2,1,0:T(2,128)}, u32[]{:S(2)}) copy-start(f32[4,2,128]{2,1,0:T(2,128)} %constant.31.clone.inner_ref) | copy-start | bytes 12292
  53.2 11.9 %collective-permute-start.2 = (f32[64,128]{1,0:T(8,128)S(1)}, f32[64,128]{1,0:T(8,128)S(1)}, u32[]{:S(2)}, u32[]{:S(2)}) collective-permute-start(f32[64,128]{1,0:T(8,128)S(1)} %get-tuple-element.21), channel_id=1, source_target_pairs={{0,1},{1,2},{2,3},{3,4},{4,5},{5,6},{6,7},{7,8},{8,9},{9,10},{10,1... | collective-permute-start | bytes 98312 | tf_op jit(solution)/shard_map/ppermute | solution.py:570
  56.9 8.2 %collective-permute-start.3 = (f32[64,128]{1,0:T(8,128)S(1)}, f32[64,128]{1,0:T(8,128)S(1)}, u32[]{:S(2)}, u32[]{:S(2)}) collective-permute-start(f32[64,128]{1,0:T(8,128)S(1)} %get-tuple-element.22), channel_id=1, source_target_pairs={{0,15},{1,0},{2,1},{3,2},{4,3},{5,4},{6,5},{7,6},{8,7},{9,8},{10,9... | collective-permute-start | bytes 98312 | tf_op jit(solution)/shard_map/ppermute | solution.py:571
  65.0 21.3 %copy-start.3 = (f32[3,4,64,128]{3,2,1,0:T(8,128)S(1)}, f32[3,4,64,128]{3,2,1,0:T(8,128)}, u32[]{:S(2)}) copy-start(f32[3,4,64,128]{3,2,1,0:T(8,128)} %velocity_ref.1) | copy-start | bytes 1179652
  71.9 31.6 %copy-start.9 = (bf16[256,256]{1,0:T(8,128)(2,1)S(1)}, bf16[256,256]{1,0:T(8,128)(2,1)}, u32[]{:S(2)}) copy-start(bf16[256,256]{1,0:T(8,128)(2,1)} %constant.38.clone.low_ref) | copy-start | bytes 393220
  71.9 31.6 %copy-start.10 = (bf16[256,256]{1,0:T(8,128)(2,1)S(1)}, bf16[256,256]{1,0:T(8,128)(2,1)}, u32[]{:S(2)}) copy-start(bf16[256,256]{1,0:T(8,128)(2,1)} %constant.37.clone.high_ref) | copy-start | bytes 393220
  71.9 31.6 %copy-start.18 = (bf16[32,192]{1,0:T(8,128)(2,1)S(1)}, bf16[32,192]{1,0:T(8,128)(2,1)}, u32[]{:S(2)}) copy-start(bf16[32,192]{1,0:T(8,128)(2,1)} %constant.36.clone.strike_ref) | copy-start | bytes 36868
  71.9 31.6 %all-to-all-start.2 = ((f32[512,1,128]{2,1,0:T(1,128)}), f32[512,1,128]{2,1,0:T(1,128)S(1)}, u32[]{:S(2)}, u32[]{:S(2)}) async-start(f32[512,1,128]{2,1,0:T(1,128)} %bitcast.4), calls=%async_computation.2 | async-start | bytes 524288 | tf_op jit(solution)/shard_map/all_to_all | solution.py:581
  86.3 41.6 %copy-start.5 = (f32[3,64,128]{2,1,0:T(8,128)S(1)}, f32[3,64,128]{2,1,0:T(8,128)}, u32[]{:S(2)}) copy-start(f32[3,64,128]{2,1,0:T(8,128)} %iv_ref.3) | copy-start | bytes 294916
  86.3 41.6 %copy-start.7 = (f32[4,64,128]{2,1,0:T(8,128)S(1)}, f32[4,64,128]{2,1,0:T(8,128)}, u32[]{:S(2)}) copy-start(f32[4,64,128]{2,1,0:T(8,128)} %cohesion_ref.1) | copy-start | bytes 393220
  87.0 8.1 %collective-permute-start.4 = (f32[16,128]{1,0:T(8,128)S(1)}, f32[16,128]{1,0:T(8,128)S(1)}, u32[]{:S(2)}, u32[]{:S(2)}) collective-permute-start(f32[16,128]{1,0:T(8,128)S(1)} %get-tuple-element.25), channel_id=1, source_target_pairs={{0,16},{16,32},{32,48},{48,64},{64,80},{80,96},{96,112},{112,128},... | collective-permute-start | bytes 24584 | tf_op jit(solution)/shard_map/ppermute | solution.py:570
  90.6 5.4 %collective-permute-start.5 = (f32[16,128]{1,0:T(8,128)S(1)}, f32[16,128]{1,0:T(8,128)S(1)}, u32[]{:S(2)}, u32[]{:S(2)}) collective-permute-start(f32[16,128]{1,0:T(8,128)S(1)} %get-tuple-element.26), channel_id=1, source_target_pairs={{0,496},{16,0},{32,16},{48,32},{64,48},{80,64},{96,80},{112,96},{1... | collective-permute-start | bytes 24584 | tf_op jit(solution)/shard_map/ppermute | solution.py:571
  105.0 22.9 %all-to-all-start.3 = ((f32[32,8,128]{2,1,0:T(8,128)}), f32[32,8,128]{2,1,0:T(8,128)S(1)}, u32[]{:S(2)}, u32[]{:S(2)}) async-start(f32[32,8,128]{2,1,0:T(8,128)} %shard_map.211.after_ref), calls=%async_computation.3 | async-start | bytes 262144 | tf_op jit(solution)/shard_map/all_to_all | solution.py:576
  114.9 9.2 %collective-permute-start.6 = (f32[64,128]{1,0:T(8,128)S(1)}, f32[64,128]{1,0:T(8,128)S(1)}, u32[]{:S(2)}, u32[]{:S(2)}) collective-permute-start(f32[64,128]{1,0:T(8,128)S(1)} %get-tuple-element.30), channel_id=1, source_target_pairs={{0,1},{1,2},{2,3},{3,4},{4,5},{5,6},{6,7},{7,8},{8,9},{9,10},{10,1... | collective-permute-start | bytes 98312 | tf_op jit(solution)/shard_map/ppermute | solution.py:570
  116.9 8.3 %collective-permute-start.7 = (f32[64,128]{1,0:T(8,128)S(1)}, f32[64,128]{1,0:T(8,128)S(1)}, u32[]{:S(2)}, u32[]{:S(2)}) collective-permute-start(f32[64,128]{1,0:T(8,128)S(1)} %get-tuple-element.31), channel_id=1, source_target_pairs={{0,15},{1,0},{2,1},{3,2},{4,3},{5,4},{6,5},{7,6},{8,7},{9,8},{10,9... | collective-permute-start | bytes 98312 | tf_op jit(solution)/shard_map/ppermute | solution.py:571
  (1 other events, 0.9 us)

commit v3 on v2

--- a/solution.py
+++ b/solution.py
@@ -160,7 +160,7 @@
     return parts
 
 
-def scatter_kernel(iv_ref, out_ref, flipped_ref):
+def scatter_kernel(iv_ref, after_ref, out_ref, flipped_ref):
     for c in range(3):
         flipped_ref[...] = iv_ref[c].T
         for s in range(2):
@@ -196,7 +196,7 @@
 
 
 def strike_inverse_kernel(
-    in_ref, strike_ref, twiddle_ref, high_ref, low_ref, after_ref, also_ref, out_ref
+    in_ref, strike_ref, twiddle_ref, high_ref, low_ref, out_ref
 ):
     columns = []
     for t in range(2):
@@ -348,36 +348,84 @@
                 out_ref[c, parity, z] = groups[parity]
 
 
-def strike_edges(fields_ref, chosen):
-    pad = jnp.zeros((4, 128), jnp.float32)
-    low = [fields_ref[n, z, 0:1, :] for n in chosen for z in range(4)]
-    high = [fields_ref[n, z, 63:64, :] for n in chosen for z in range(4)]
-    return jnp.concatenate(low + [pad], axis=0), jnp.concatenate(high + [pad], axis=0)
-
-
-def dip_edges(fields_ref, chosen):
+ACROSS, ALONG, DEEP = (0, 3, 4), (3, 1, 5), (4, 5, 2)
+STEP = 0.5 * COURANT
+
+
+def pack_columns(stress_ref, part_ref, side):
     lane = lane_of((64, 128))
-    low = jnp.zeros((64, 128), jnp.float32)
-    high = jnp.zeros((64, 128), jnp.float32)
-    for i, n in enumerate(chosen):
+    total = jnp.zeros((64, 128), jnp.float32)
+    for n in range(3):
         for z in range(4):
-            to = 4 * i + z
-            low = jnp.where(lane == to, roll(fields_ref[n, z], to, 1), low)
-            high = jnp.where(lane == to, roll(fields_ref[n, z], to - 127, 1), high)
-    return low, high
-
-
-def strike_edge_kernel(fields_ref, low_ref, high_ref):
-    low_ref[...], high_ref[...] = strike_edges(fields_ref, (0, 3, 4))
-
-
-def dip_edge_kernel(fields_ref, after_ref, low_ref, high_ref):
-    low_ref[...], high_ref[...] = dip_edges(fields_ref, (3, 1, 5))
-
-
-def hold_kernel(low_ref, high_ref, after_ref, low_out_ref, high_out_ref):
-    low_out_ref[...] = low_ref[...]
-    high_out_ref[...] = high_ref[...]
+            fields = (stress_ref[ALONG[n], z], part_ref[n, z], stress_ref[ACROSS[n], z])
+            for i in range(3):
+                to = 12 * i + 4 * n + z
+                total = jnp.where(lane == to, roll(fields[i], to - side, 1), total)
+    return total
+
+
+def part_kernel(velocity_ref, stress_ref, part_ref, low_ref, high_ref):
+    row, lane = row_of((64, 128)), lane_of((64, 128))
+    for n in range(3):
+        for z in range(4):
+            across, along = stress_ref[ACROSS[n], z], stress_ref[ALONG[n], z]
+            total = jnp.where(row == 63, 0.0, roll(across, -1, 0))
+            total = total - jnp.where(row == 0, 0.0, roll(across, 1, 0))
+            total = total + jnp.where(lane == 127, 0.0, roll(along, -1, 1))
+            total = total - jnp.where(lane == 0, 0.0, roll(along, 1, 1))
+            if z < 3:
+                total = total + stress_ref[DEEP[n], z + 1]
+            if z > 0:
+                total = total - stress_ref[DEEP[n], z - 1]
+            part_ref[n, z] = velocity_ref[n, z] + STEP * total
+    low_ref[...] = pack_columns(stress_ref, part_ref, 0)
+    high_ref[...] = pack_columns(stress_ref, part_ref, 127)
+
+
+def column_kernel(part_ref, stress_ref, ylo_ref, yhi_ref, out_ref, low_ref, high_ref):
+    lane = lane_of((64, 128))
+    ylo, yhi = ylo_ref[...], yhi_ref[...]
+    edges = [[], []]
+    for n in range(3):
+        for z in range(4):
+            at = 4 * n + z
+            field = part_ref[n, z]
+            field = field - jnp.where(lane == 0, STEP * roll(ylo, -at, 1), 0.0)
+            field = field + jnp.where(lane == 127, STEP * roll(yhi, 127 - at, 1), 0.0)
+            out_ref[n, z] = field
+            edges[0].append(field[0:1])
+            edges[1].append(field[63:64])
+    pad = jnp.zeros((6, 128), jnp.float32)
+    for i, ref in enumerate((low_ref, high_ref)):
+        at = 63 * i
+        rows = [stress_ref[ACROSS[n], z, at : at + 1, :] for n in range(3) for z in range(4)]
+        rows += edges[i] + [ylo[at : at + 1], yhi[at : at + 1], pad]
+        ref[...] = jnp.concatenate(rows, axis=0)
+
+
+def row_kernel(
+    part_ref, xlo_ref, xhi_ref, ylo_ref, yhi_ref,
+    own_xlo_ref, own_xhi_ref, own_ylo_ref, own_yhi_ref, after_ref,
+    out_ref, vxlo_ref, vxhi_ref, vylo_ref, vyhi_ref,
+):
+    row = row_of((64, 128))
+    for n in range(3):
+        for z in range(4):
+            at = 4 * n + z
+            field = part_ref[n, z]
+            field = field - jnp.where(row == 0, STEP * xlo_ref[at : at + 1, :], 0.0)
+            field = field + jnp.where(row == 63, STEP * xhi_ref[at : at + 1, :], 0.0)
+            out_ref[n, z] = field
+    vxlo_ref[...] = xlo_ref[12:28, :] + STEP * own_xlo_ref[0:16, :]
+    vxhi_ref[...] = xhi_ref[12:28, :] - STEP * own_xhi_ref[0:16, :]
+    for side, ref in enumerate((vylo_ref, vyhi_ref)):
+        corner = jnp.where(row == 63, STEP * xhi_ref[24 + side : 25 + side, :], 0.0)
+        corner = corner - jnp.where(row == 0, STEP * xlo_ref[24 + side : 25 + side, :], 0.0)
+        if side == 0:
+            columns = roll(ylo_ref[...], -12, 1) + STEP * own_ylo_ref[...]
+        else:
+            columns = roll(yhi_ref[...], -12, 1) - STEP * own_yhi_ref[...]
+        ref[...] = columns + roll(corner, -24, 1)
 
 
 def strike_diff(field, low, high):
@@ -392,27 +440,6 @@
     before = jnp.where(lane == 0, roll(low, -to, 1), roll(field, 1, 1))
     after = jnp.where(lane == 127, roll(high, 127 - to, 1), roll(field, -1, 1))
     return 0.5 * (after - before)
-
-
-def velocity_kernel(
-    velocity_ref, stress_ref, xlo_ref, xhi_ref, ylo_ref, yhi_ref,
-    out_ref, xlo_out_ref, xhi_out_ref, ylo_out_ref, yhi_out_ref,
-):
-    across, along, deep = (0, 3, 4), (3, 1, 5), (4, 5, 2)
-    ylo, yhi = ylo_ref[...], yhi_ref[...]
-    for n in range(3):
-        for z in range(4):
-            at = 4 * n + z
-            total = strike_diff(
-                stress_ref[across[n], z], xlo_ref[at : at + 1], xhi_ref[at : at + 1]
-            ) + dip_diff(stress_ref[along[n], z], ylo, yhi, at)
-            if z < 3:
-                total = total + 0.5 * stress_ref[deep[n], z + 1]
-            if z > 0:
-                total = total - 0.5 * stress_ref[deep[n], z - 1]
-            out_ref[n, z] = velocity_ref[n, z] + COURANT * total
-    xlo_out_ref[...], xhi_out_ref[...] = strike_edges(out_ref, (0, 1, 2))
-    ylo_out_ref[...], yhi_out_ref[...] = dip_edges(out_ref, (0, 1, 2))
 
 
 def slab_kernel(
@@ -500,10 +527,9 @@
     )(*arguments, *after)
 
 
-def scatter(iv):
-    return call(
-        scatter_kernel, f32(32, 8, 128), (iv,), scratch=[pltpu.VMEM((128, 64), jnp.float32)]
-    )
+def scatter(iv, after):
+    scratch = [pltpu.VMEM((128, 64), jnp.float32)]
+    return call(scatter_kernel, f32(32, 8, 128), (iv,), after, scratch)
 
 
 def strike_forward(arrived, after):
@@ -513,11 +539,11 @@
     return call(strike_forward_kernel, f32(512, 128), arguments, after)
 
 
-def strike_inverse(arrived, after):
+def strike_inverse(arrived):
     _, inverse = strike_tables()
     _, (high, low) = cell_tables()
     arguments = (arrived, inverse, strike_twiddle(), high, low)
-    return call(strike_inverse_kernel, f32(32, 8, 128), arguments, after)
+    return call(strike_inverse_kernel, f32(32, 8, 128), arguments)
 
 
 def dip(arrived, weight, past, after):
@@ -535,23 +561,28 @@
     )
 
 
-def stress_strike_edges(stress):
-    return call(strike_edge_kernel, (f32(16, 128),) * 2, (stress,))
-
-
-def stress_dip_edges(stress, after):
-    return call(dip_edge_kernel, (f32(64, 128),) * 2, (stress,), (after,))
-
-
-def hold(low, high, after):
-    return call(hold_kernel, (f32(*low.shape),) * 2, (low, high), (after,))
-
-
-def velocity_before(velocity, stress, halo):
+def velocity_part(velocity, stress):
     return call(
-        velocity_kernel,
+        part_kernel,
+        (f32(3, 4, 64, 128), f32(64, 128), f32(64, 128)),
+        (velocity, stress),
+    )
+
+
+def velocity_columns(part, stress, halo):
+    return call(
+        column_kernel,
+        (f32(3, 4, 64, 128), f32(32, 128), f32(32, 128)),
+        (part, stress, *halo),
+    )
+
+
+def velocity_rows(part, halo, own, after):
+    return call(
+        row_kernel,
         (f32(3, 4, 64, 128), f32(16, 128), f32(16, 128), f32(64, 128), f32(64, 128)),
-        (velocity, stress, *halo),
+        (part, *halo, *own),
+        (after,),
     )
 
 
@@ -583,22 +614,19 @@
 
 
 def local(interface_velocity, history, kernel, velocity, stress, cohesion):
-    arrived = strike_swap(scatter(interface_velocity))
-    strike_halo = exchange("bx", *stress_strike_edges(stress))
-    sent = strike_forward(arrived, strike_halo)
+    part, *own_columns = velocity_part(velocity, stress)
+    columns = exchange("by", *own_columns)
+    arrived = strike_swap(scatter(interface_velocity, (part,)))
+    sent = strike_forward(arrived, columns)
+    part, *own_rows = velocity_columns(part, stress, columns)
+    rows = exchange("bx", *own_rows)
     arrived = whole_swap(sent)
-    dip_halo = exchange("by", *stress_dip_edges(stress, sent))
     weight, past = past_terms(kernel, history)
-    sent = dip(arrived, weight, past, dip_halo)
+    sent = dip(arrived, weight, past, rows)
+    before, *halo = velocity_rows(part, (*rows, *columns), (*own_rows, *own_columns), sent)
     arrived = whole_swap(sent)
-    before, *edges = velocity_before(velocity, stress, (*strike_halo, *dip_halo))
-    strike_halo = exchange("bx", *hold(edges[0], edges[1], sent))
-    sent = strike_inverse(arrived, strike_halo)
-    arrived = strike_swap(sent)
-    dip_halo = exchange("by", *hold(edges[2], edges[3], sent))
-    return slab(
-        arrived, before, stress, cohesion, interface_velocity, (*strike_halo, *dip_halo)
-    )
+    arrived = strike_swap(strike_inverse(arrived))
+    return slab(arrived, before, stress, cohesion, interface_velocity, halo)
 
 
 def solution(mesh):

time: 130 us -> 131 us (level)
  starting transfers between devices: 93.7 us -> 55.5 us
  blocking collectives: 0 us -> 31.6 us
  local copies, waits for them, and re-layouts: 2.13 us -> 10.1 us
    all_to_all x0 -> x1, blocking collectives: none -> 31.6 us  [whole_swap(): lax.all_to_all(value, ('by', 'bx'), split_axis=0, concat_axis=0, tiled=True)]
    all_to_all x2 -> x1, starting transfers between devices: 33 us -> 16.2 us  [whole_swap(): lax.all_to_all(value, ('by', 'bx'), split_axis=0, concat_axis=0, tiled=True)]
    all_to_all x2, waiting for transfers between devices: 5.6 us -> 15.4 us  [strike_swap(): return lax.all_to_all(value, 'bx', split_axis=0, concat_axis=0, tiled=True)]
    ppermute x4 -> x2, starting transfers between devices: 20.7 us -> 10.9 us  [exchange(): lax.ppermute(low, axis, [(i, (i - 1) % count) for i in range(count)])]
    unnamed x42 -> x64, local copies, waits for them, and re-layouts: 2.13 us -> 10.1 us
    all_to_all x2 -> x1, waiting for transfers between devices: 12.5 us -> 6.11 us  [whole_swap(): lax.all_to_all(value, ('by', 'bx'), split_axis=0, concat_axis=0, tiled=True)]
    ppermute x4 -> x2, starting transfers between devices: 12.8 us -> 6.64 us  [exchange(): lax.ppermute(high, axis, [(i, (i + 1) % count) for i in range(count)])]
    all_to_all x2, starting transfers between devices: 27.1 us -> 21.8 us  [strike_swap(): return lax.all_to_all(value, 'bx', split_axis=0, concat_axis=0, tiled=True)]
  transfers between devices with their start and end apart: 12 -> 7, of which waited for: 7 -> 4; matrix products, arithmetic and copies ran while one was open for 0% -> 0% of each run, Pallas kernels for 2% -> 1%
where the time goes in v3:
time: 131 us; the launch traced here: 130 us
  starting transfers between devices  55.5 us (42%)
  blocking collectives  31.6 us (24%)
  waiting for transfers between devices  22.5 us (17%)
  local copies, waits for them, and re-layouts  10.1 us (8%)
  Pallas kernels  9.22 us (7%)
    all_to_all x1, blocking collectives, whole_swap(): lax.all_to_all(value, ('by', 'bx'), split_axis=0, concat_axis=0, tiled=True)  31.6 us
    all_to_all x2, starting transfers between devices, strike_swap(): return lax.all_to_all(value, 'bx', split_axis=0, concat_axis=0, tiled=True)  21.8 us
    all_to_all x1, starting transfers between devices, whole_swap(): lax.all_to_all(value, ('by', 'bx'), split_axis=0, concat_axis=0, tiled=True)  16.2 us
    all_to_all x2, waiting for transfers between devices, strike_swap(): return lax.all_to_all(value, 'bx', split_axis=0, concat_axis=0, tiled=True)  15.4 us
    ppermute x2, starting transfers between devices, exchange(): lax.ppermute(low, axis, [(i, (i - 1) % count) for i in range(count)])  10.9 us
    unnamed x64, local copies, waits for them, and re-layouts  10.1 us
    pallas_call x9, Pallas kernels, call(): pl.pallas_call(kernel, out_shape=out_shape, in_specs=[VMEM] * len(argumen...  9.22 us
    ppermute x2, starting transfers between devices, exchange(): lax.ppermute(high, axis, [(i, (i + 1) % count) for i in range(count)])  6.64 us
  transfers between devices with their start and end apart: 7, of which 4 were waited for; matrix products, arithmetic and copies ran while one was open for 0% of the time, Pallas kernels for 1%

profile of v3, /device:TPU:1, one launch (start us, length us, event | category | flops | bytes accessed | tf_op | source)
XLA Modules:
  0.0 130.0 jit_solution(15914043045089115481)
XLA Ops:
  0.7 1.1 copy-done
  1.8 1.0 copy-done.4
  2.8 0.9 shard_map.203
  3.7 1.0 shard_map.204
  4.8 17.2 %all-to-all-start = ((f32[32,8,128]{2,1,0:T(8,128)}), f32[32,8,128]{2,1,0:T(8,128)S(1)}, u32[]{:S(2)}, u32[]{:S(2)}) async-start(f32[32,8,128]{2,1,0:T(8,128)} %shard_map.204), calls=%async_computation | async-start | bytes 262144 | tf_op jit(solution)/shard_map/all_to_all | solution.py:607
  22.0 3.1 %collective-permute-start = (f32[64,128]{1,0:T(8,128)S(1)}, f32[64,128]{1,0:T(8,128)S(1)}, u32[]{:S(2)}, u32[]{:S(2)}) collective-permute-start(f32[64,128]{1,0:T(8,128)S(1)} %get-tuple-element.16.own_yhi_ref), channel_id=1, source_target_pairs={{0,1},{1,2},{2,3},{3,4},{4,5},{5,6},{6,7},{7,8},{8,9},{9,10},{10,1... | collective-permute-start | bytes 98312 | tf_op jit(solution)/shard_map/ppermute | solution.py:601
  25.1 6.2 %collective-permute-start.1 = (f32[64,128]{1,0:T(8,128)S(1)}, f32[64,128]{1,0:T(8,128)S(1)}, u32[]{:S(2)}, u32[]{:S(2)}) collective-permute-start(f32[64,128]{1,0:T(8,128)S(1)} %get-tuple-element.17.own_ylo_ref), channel_id=1, source_target_pairs={{0,15},{1,0},{2,1},{3,2},{4,3},{5,4},{6,5},{7,6},{8,7},{9,8},{10,9... | collective-permute-start | bytes 98312 | tf_op jit(solution)/shard_map/ppermute | solution.py:602
  31.4 1.0 collective-permute-done.1.also_ref.yhi_ref
  32.4 2.6 %all-to-all-done.in_ref = f32[32,8,128]{2,1,0:T(8,128)S(1)} async-done(((f32[32,8,128]{2,1,0:T(8,128)}), f32[32,8,128]{2,1,0:T(8,128)S(1)}, u32[]{:S(2)}, u32[]{:S(2)}) %all-to-all-start) | async-done | bytes 131104 | tf_op jit(solution)/shard_map/all_to_all | solution.py:607
  35.0 1.4 %shard_map.205 = f32[512,128]{1,0:T(8,128)} custom-call(f32[32,8,128]{2,1,0:T(8,128)S(1)} %all-to-all-done.in_ref, bf16[64,96]{1,0:T(8,128)(2,1)S(1)} %copy-done.26, f32[2,32,128]{2,1,0:T(8,128)S(1)} %copy-done.9, bf16[256,256]{1,0:T(8,128)(2,1)S(1)} %copy-done.13, bf16[256,256]{1,0:T(8,128)(2,1)S(1)} %copy-done.12, ...), custom_call_target="tpu_custom_call" | custom-call | tf_op jit(solution)/shard_map/pallas_call | solution.py:520
  36.3 16.2 %all-to-all-start.1 = ((f32[512,1,128]{2,1,0:T(1,128)}), f32[512,1,128]{2,1,0:T(1,128)S(1)}, u32[]{:S(2)}, u32[]{:S(2)}) async-start(f32[512,1,128]{2,1,0:T(1,128)} %bitcast.1), calls=%async_computation.1 | async-start | bytes 524288 | tf_op jit(solution)/shard_map/all_to_all | solution.py:612
  52.6 0.3 shard_map.207
  52.9 3.5 %collective-permute-start.2 = (f32[32,128]{1,0:T(8,128)S(1)}, f32[32,128]{1,0:T(8,128)S(1)}, u32[]{:S(2)}, u32[]{:S(2)}) collective-permute-start(f32[32,128]{1,0:T(8,128)S(1)} %get-tuple-element.20.own_xhi_ref), channel_id=1, source_target_pairs={{0,16},{16,32},{32,48},{48,64},{64,80},{80,96},{96,112},{112,128},... | collective-permute-start | bytes 49160 | tf_op jit(solution)/shard_map/ppermute | solution.py:601
  56.4 4.7 %collective-permute-start.3 = (f32[32,128]{1,0:T(8,128)S(1)}, f32[32,128]{1,0:T(8,128)S(1)}, u32[]{:S(2)}, u32[]{:S(2)}) collective-permute-start(f32[32,128]{1,0:T(8,128)S(1)} %get-tuple-element.21.own_xlo_ref), channel_id=1, source_target_pairs={{0,496},{16,0},{32,16},{48,32},{64,48},{80,64},{96,80},{112,96},{1... | collective-permute-start | bytes 49160 | tf_op jit(solution)/shard_map/ppermute | solution.py:602
  61.2 1.2 shard_map.206
  62.4 0.7 copy-done.6
  63.0 0.6 copy-done.19
  63.6 6.1 %all-to-all-done.1 = f32[512,1,128]{2,1,0:T(1,128)S(1)} async-done(((f32[512,1,128]{2,1,0:T(1,128)}), f32[512,1,128]{2,1,0:T(1,128)S(1)}, u32[]{:S(2)}, u32[]{:S(2)}) %all-to-all-start.1) | async-done | bytes 262176 | tf_op jit(solution)/shard_map/all_to_all | solution.py:612
  69.8 0.9 copy-done.7
  70.7 0.8 copy-done.15
  71.5 0.8 copy-done.16
  72.4 0.8 copy-done.17
  73.2 0.8 copy-done.18
  74.1 0.8 copy-done.20
  74.8 0.7 copy-done.31
  75.5 1.1 shard_map.208.after_ref
  76.7 31.6 %all_to_all.20 = f32[512,1,128]{2,1,0:T(1,128)S(1)} all-to-all(f32[512,1,128]{2,1,0:T(1,128)S(1)} %bitcast.8), channel_id=1, replica_groups=mesh['bx'=32,'by'=16] {'by','bx'}, dimensions={0} | all-to-all | bytes 524288 | tf_op jit(solution)/shard_map/all_to_all | solution.py:612
  108.3 0.9 copy-done.11
  109.2 1.4 %shard_map.209 = f32[32,8,128]{2,1,0:T(8,128)} custom-call(f32[512,128]{1,0:T(8,128)S(1)} %bitcast.10, bf16[32,192]{1,0:T(8,128)(2,1)S(1)} %copy-done.25, f32[2,32,128]{2,1,0:T(8,128)S(1)} %copy-done.9, bf16[256,256]{1,0:T(8,128)(2,1)S(1)} %copy-done.11, bf16[256,256]{1,0:T(8,128)(2,1)S(1)} %copy-done.10), custom_call_target="tpu_custom_call" | custom-call | tf_op jit(solution)/shard_map/pallas_call | solution.py:520
  110.7 4.6 %all-to-all-start.3 = ((f32[32,8,128]{2,1,0:T(8,128)}), f32[32,8,128]{2,1,0:T(8,128)S(1)}, u32[]{:S(2)}, u32[]{:S(2)}) async-start(f32[32,8,128]{2,1,0:T(8,128)} %shard_map.209), calls=%async_computation.3 | async-start | bytes 262144 | tf_op jit(solution)/shard_map/all_to_all | solution.py:607
  115.4 12.8 %all-to-all-done.3.in_ref = f32[32,8,128]{2,1,0:T(8,128)S(1)} async-done(((f32[32,8,128]{2,1,0:T(8,128)}), f32[32,8,128]{2,1,0:T(8,128)S(1)}, u32[]{:S(2)}, u32[]{:S(2)}) %all-to-all-start.3) | async-done | bytes 131104 | tf_op jit(solution)/shard_map/all_to_all | solution.py:607
  128.2 1.8 %shard_map.211 = (f32[3,4,64,128]{3,2,1,0:T(8,128)}, f32[6,4,64,128]{3,2,1,0:T(8,128)}) custom-call(f32[32,8,128]{2,1,0:T(8,128)S(1)} %all-to-all-done.3.in_ref, f32[3,4,64,128]{3,2,1,0:T(8,128)S(1)} %get-tuple-element.23.before_ref, f32[6,4,64,128]{3,2,1,0:T(8,128)S(1)} %copy-done.1, f32[4,64,128]{2,1,0:T(8,128)S(1)} %copy-done.8, ...), custom_call_target="tpu_custom_call" | custom-call | tf_op jit(solution)/shard_map/pallas_call | solution.py:520
  (56 shorter events, 0.2 us)
Async XLA Ops:
  0.6 34.3 %copy-start.26 = (bf16[64,96]{1,0:T(8,128)(2,1)S(1)}, bf16[64,96]{1,0:T(8,128)(2,1)}, u32[]{:S(2)}) copy-start(bf16[64,96]{1,0:T(8,128)(2,1)} %constant.26.clone.strike_ref) | copy-start | bytes 36868
  0.6 1.1 copy-start
  1.8 1.0 copy-start.4
  2.8 1.0 copy-start.3
  2.8 32.2 %copy-start.9 = (f32[2,32,128]{2,1,0:T(8,128)S(1)}, f32[2,32,128]{2,1,0:T(8,128)}, u32[]{:S(2)}) copy-start(f32[2,32,128]{2,1,0:T(8,128)} %constant.27.clone.twiddle_ref) | copy-start | bytes 98308
  2.8 32.2 %copy-start.12 = (bf16[256,256]{1,0:T(8,128)(2,1)S(1)}, bf16[256,256]{1,0:T(8,128)(2,1)}, u32[]{:S(2)}) copy-start(bf16[256,256]{1,0:T(8,128)(2,1)} %constant.29.clone.low_ref) | copy-start | bytes 393220
  2.8 32.2 %copy-start.13 = (bf16[256,256]{1,0:T(8,128)(2,1)S(1)}, bf16[256,256]{1,0:T(8,128)(2,1)}, u32[]{:S(2)}) copy-start(bf16[256,256]{1,0:T(8,128)(2,1)} %constant.28.clone.high_ref) | copy-start | bytes 393220
  3.7 32.6 %copy-start.21 = (f32[64,128]{1,0:T(8,128)}, f32[64,128]{1,0:T(8,128)S(1)}, u32[]{:S(2)}) copy-start(f32[64,128]{1,0:T(8,128)S(1)} %get-tuple-element.17.own_ylo_ref) | copy-start | bytes 98308
  3.7 32.6 %copy-start.23 = (f32[64,128]{1,0:T(8,128)}, f32[64,128]{1,0:T(8,128)S(1)}, u32[]{:S(2)}) copy-start(f32[64,128]{1,0:T(8,128)S(1)} %get-tuple-element.16.own_yhi_ref) | copy-start | bytes 98308
  3.7 48.8 %copy-start.1 = (f32[6,4,64,128]{3,2,1,0:T(8,128)S(1)}, f32[6,4,64,128]{3,2,1,0:T(8,128)}, u32[]{:S(2)}) copy-start(f32[6,4,64,128]{3,2,1,0:T(8,128)} %stress_ref.5) | copy-start | bytes 2359300
  4.8 30.2 %all-to-all-start = ((f32[32,8,128]{2,1,0:T(8,128)}), f32[32,8,128]{2,1,0:T(8,128)S(1)}, u32[]{:S(2)}, u32[]{:S(2)}) async-start(f32[32,8,128]{2,1,0:T(8,128)} %shard_map.204), calls=%async_computation | async-start | bytes 262144 | tf_op jit(solution)/shard_map/all_to_all | solution.py:607
  22.0 9.4 %collective-permute-start = (f32[64,128]{1,0:T(8,128)S(1)}, f32[64,128]{1,0:T(8,128)S(1)}, u32[]{:S(2)}, u32[]{:S(2)}) collective-permute-start(f32[64,128]{1,0:T(8,128)S(1)} %get-tuple-element.16.own_yhi_ref), channel_id=1, source_target_pairs={{0,1},{1,2},{2,3},{3,4},{4,5},{5,6},{6,7},{7,8},{8,9},{9,10},{10,1... | collective-permute-start | bytes 98312 | tf_op jit(solution)/shard_map/ppermute | solution.py:601
  25.1 36.1 %copy-start.2 = (f32[6,2,3,4,1,16,128]{6,5,4,3,2,1,0:T(8,128)S(1)}, f32[6,2,3,4,1,16,128]{6,5,4,3,2,1,0:T(8,128)}, u32[]{:S(2)}) copy-start(f32[6,2,3,4,1,16,128]{6,5,4,3,2,1,0:T(8,128)} %history_ref.1) | copy-start | bytes 3538948
  25.1 36.1 %copy-start.5 = (f32[7,4,1,16,128]{4,3,2,1,0:T(8,128)S(1)}, f32[7,4,1,16,128]{4,3,2,1,0:T(8,128)}, u32[]{:S(2)}) copy-start(f32[7,4,1,16,128]{4,3,2,1,0:T(8,128)} %kernel_ref.1) | copy-start | bytes 688132
  25.1 7.2 %collective-permute-start.1 = (f32[64,128]{1,0:T(8,128)S(1)}, f32[64,128]{1,0:T(8,128)S(1)}, u32[]{:S(2)}, u32[]{:S(2)}) collective-permute-start(f32[64,128]{1,0:T(8,128)S(1)} %get-tuple-element.17.own_ylo_ref), channel_id=1, source_target_pairs={{0,15},{1,0},{2,1},{3,2},{4,3},{5,4},{6,5},{7,6},{8,7},{9,8},{10,9... | collective-permute-start | bytes 98312 | tf_op jit(solution)/shard_map/ppermute | solution.py:602
  36.3 33.4 %all-to-all-start.1 = ((f32[512,1,128]{2,1,0:T(1,128)}), f32[512,1,128]{2,1,0:T(1,128)S(1)}, u32[]{:S(2)}, u32[]{:S(2)}) async-start(f32[512,1,128]{2,1,0:T(1,128)} %bitcast.1), calls=%async_computation.1 | async-start | bytes 524288 | tf_op jit(solution)/shard_map/all_to_all | solution.py:612
  52.6 17.2 %copy-start.14 = (bf16[128,256]{1,0:T(8,128)(2,1)S(1)}, bf16[128,256]{1,0:T(8,128)(2,1)}, u32[]{:S(2)}) copy-start(bf16[128,256]{1,0:T(8,128)(2,1)} %constant.35.clone.il_ref) | copy-start | bytes 196612
  52.8 10.8 %copy-start.27 = (f32[32,128]{1,0:T(8,128)}, f32[32,128]{1,0:T(8,128)S(1)}, u32[]{:S(2)}) copy-start(f32[32,128]{1,0:T(8,128)S(1)} %get-tuple-element.21.own_xlo_ref) | copy-start | bytes 49156
  52.8 10.8 %copy-start.29 = (f32[32,128]{1,0:T(8,128)}, f32[32,128]{1,0:T(8,128)S(1)}, u32[]{:S(2)}) copy-start(f32[32,128]{1,0:T(8,128)S(1)} %get-tuple-element.20.own_xhi_ref) | copy-start | bytes 49156
  52.9 10.8 %collective-permute-start.2 = (f32[32,128]{1,0:T(8,128)S(1)}, f32[32,128]{1,0:T(8,128)S(1)}, u32[]{:S(2)}, u32[]{:S(2)}) collective-permute-start(f32[32,128]{1,0:T(8,128)S(1)} %get-tuple-element.20.own_xhi_ref), channel_id=1, source_target_pairs={{0,16},{16,32},{32,48},{48,64},{64,80},{80,96},{96,112},{112,128},... | collective-permute-start | bytes 49160 | tf_op jit(solution)/shard_map/ppermute | solution.py:601
  56.4 51.9 %copy-start.10 = (bf16[256,256]{1,0:T(8,128)(2,1)S(1)}, bf16[256,256]{1,0:T(8,128)(2,1)}, u32[]{:S(2)}) copy-start(bf16[256,256]{1,0:T(8,128)(2,1)} %constant.38.clone.low_ref) | copy-start | bytes 393220
  56.4 51.9 %copy-start.25 = (bf16[32,192]{1,0:T(8,128)(2,1)S(1)}, bf16[32,192]{1,0:T(8,128)(2,1)}, u32[]{:S(2)}) copy-start(bf16[32,192]{1,0:T(8,128)(2,1)} %constant.36.clone.strike_ref) | copy-start | bytes 36868
  56.4 7.2 %collective-permute-start.3 = (f32[32,128]{1,0:T(8,128)S(1)}, f32[32,128]{1,0:T(8,128)S(1)}, u32[]{:S(2)}, u32[]{:S(2)}) collective-permute-start(f32[32,128]{1,0:T(8,128)S(1)} %get-tuple-element.21.own_xlo_ref), channel_id=1, source_target_pairs={{0,496},{16,0},{32,16},{48,32},{64,48},{80,64},{96,80},{112,96},{1... | collective-permute-start | bytes 49160 | tf_op jit(solution)/shard_map/ppermute | solution.py:602
  69.8 0.9 copy-start.7
  70.7 0.8 copy-start.15
  75.5 39.7 %copy-start.22 = (f32[64,128]{1,0:T(8,128)S(1)}, f32[64,128]{1,0:T(8,128)}, u32[]{:S(2)}) copy-start(f32[64,128]{1,0:T(8,128)} %copy-done.21) | copy-start | bytes 98308
  75.5 39.7 %copy-start.24 = (f32[64,128]{1,0:T(8,128)S(1)}, f32[64,128]{1,0:T(8,128)}, u32[]{:S(2)}) copy-start(f32[64,128]{1,0:T(8,128)} %copy-done.23) | copy-start | bytes 98308
  75.5 39.7 %copy-start.28 = (f32[32,128]{1,0:T(8,128)S(1)}, f32[32,128]{1,0:T(8,128)}, u32[]{:S(2)}) copy-start(f32[32,128]{1,0:T(8,128)} %copy-done.27) | copy-start | bytes 49156
  75.5 39.7 %copy-start.30 = (f32[32,128]{1,0:T(8,128)S(1)}, f32[32,128]{1,0:T(8,128)}, u32[]{:S(2)}) copy-start(f32[32,128]{1,0:T(8,128)} %copy-done.29) | copy-start | bytes 49156
  76.6 51.5 %copy-start.8 = (f32[4,64,128]{2,1,0:T(8,128)S(1)}, f32[4,64,128]{2,1,0:T(8,128)}, u32[]{:S(2)}) copy-start(f32[4,64,128]{2,1,0:T(8,128)} %cohesion_ref.1) | copy-start | bytes 393220
  108.3 0.9 copy-start.11
  110.7 17.5 %all-to-all-start.3 = ((f32[32,8,128]{2,1,0:T(8,128)}), f32[32,8,128]{2,1,0:T(8,128)S(1)}, u32[]{:S(2)}, u32[]{:S(2)}) async-start(f32[32,8,128]{2,1,0:T(8,128)} %shard_map.209), calls=%async_computation.3 | async-start | bytes 262144 | tf_op jit(solution)/shard_map/all_to_all | solution.py:607
  (7 other events, 5.2 us)

commit v4 on v3

--- a/solution.py
+++ b/solution.py
@@ -1,6 +1,5 @@
 import jax
 import jax.numpy as jnp
-import ml_dtypes
 import numpy as np
 from jax import lax
 from jax.experimental import pallas as pl
@@ -17,33 +16,16 @@
 PARAMS = pltpu.CompilerParams(vmem_limit_bytes=16 * 1024 * 1024)
 
 
-def split_table(table):
-    high = table.astype(ml_dtypes.bfloat16)
-    low = (table - high.astype(np.float64)).astype(ml_dtypes.bfloat16)
-    return high, low
-
-
 def angles(rows, cols, length):
     return 2.0 * np.pi / length * ((rows[:, None] * cols[None, :]) % length)
 
 
-def strike_tables():
-    theta = angles(np.arange(32), np.arange(32), 32)
-    cos, sin = np.cos(theta), np.sin(theta)
-    high, low = split_table(np.concatenate([cos, -sin], axis=0))
-    forward = np.concatenate([high, high, low], axis=1)
-    high, low = split_table(np.concatenate([cos, -sin], axis=1))
-    inverse = np.concatenate([high, high, low], axis=1)
-    return forward, inverse
-
-
-def strike_twiddle():
-    theta = angles(np.arange(32), np.arange(64), 2048)
-    theta = np.concatenate([theta, theta], axis=1)
-    return np.stack([np.cos(theta), np.sin(theta)]).astype(np.float32)
-
-
-def cell_tables():
+def stack(*tables):
+    wide = [np.pad(table, ((0, 0), (0, 256 - table.shape[1]))) for table in tables]
+    return np.concatenate(wide, axis=0).astype(np.float32)
+
+
+def cell_table():
     theta = angles(np.arange(64), np.arange(64), 64).reshape(64, 16, 4)
     cos, sin = np.cos(theta) * SCALE, np.sin(theta) * SCALE
     table = np.zeros((2, 2, 64, 16, 2, 2, 4))
@@ -52,8 +34,17 @@
         table[1, h, :, :, 0, h] = sin
         table[0, h, :, :, 1, h] = -sin
         table[1, h, :, :, 1, h] = cos
-    table = table.reshape(256, 256)
-    return split_table(table), split_table(np.ascontiguousarray(table.T))
+    return table.reshape(256, 256)
+
+
+def strike_tables(inverse):
+    theta = angles(np.arange(32), np.arange(32), 32)
+    cos, sin = np.cos(theta), np.sin(theta)
+    twiddle = angles(np.arange(32), np.arange(128) % 64, 2048)
+    twiddle = np.concatenate([np.cos(twiddle), np.sin(twiddle)], axis=1)
+    if inverse:
+        return stack(cell_table().T, twiddle, np.concatenate([cos, -sin], axis=1))
+    return stack(cell_table(), twiddle, np.concatenate([cos, -sin], axis=0))
 
 
 def dip_order():
@@ -65,19 +56,14 @@
     theta = angles(np.arange(128), dip_order(), 128)
     forward = np.concatenate([np.cos(theta), np.sin(theta)], axis=1)
     inverse = np.concatenate([np.cos(theta).T, np.sin(theta).T], axis=1)
-    return split_table(forward) + split_table(inverse)
-
-
-def dip_inner_twiddle():
-    theta = angles(np.arange(4), np.arange(128), 512)
-    return np.stack([np.cos(theta), np.sin(theta)], axis=1).astype(np.float32)
-
-
-def dip_twiddle():
-    f = (4 * dip_order()[None, :] + np.arange(4)[:, None]).reshape(NF)
-    theta = angles(np.arange(4), f, 2048).reshape(2, 2, 1, NF)
-    theta = np.broadcast_to(theta, (2, 2, 4, NF)).reshape(2, 8, NF)
-    return np.stack([np.cos(theta), np.sin(theta)], axis=1).astype(np.float32)
+    theta = angles(np.arange(8), np.arange(128), 512)
+    inner = np.concatenate([np.cos(theta), np.sin(theta)], axis=1)
+    outer = []
+    for b in range(4):
+        for s in range(2):
+            theta = angles(2 * s + np.arange(8) // 4, 4 * dip_order() + b, 2048)
+            outer.append(np.concatenate([np.cos(theta), np.sin(theta)], axis=1))
+    return stack(forward, inverse, inner, *outer)
 
 
 def halves(value):
@@ -92,12 +78,15 @@
 
 def stacked_dot(table, value):
     high, low = halves(value)
+    table_high, table_low = halves(table)
+    table = jnp.concatenate([table_high, table_high, table_low], axis=1)
     return dot(table, jnp.concatenate([high, low, high], axis=0))
 
 
-def rows_dot(value, table_high, table_low):
+def rows_dot(value, table):
     rows = value.shape[0]
     high, low = halves(value)
+    table_high, table_low = halves(table)
     both = dot(jnp.concatenate([high, low], axis=0), table_high)
     return both[:rows] + both[rows:] + dot(high, table_low)
 
@@ -120,9 +109,9 @@
     return real * cos + imag * sin, imag * cos - real * sin
 
 
-def dip_transform(values, high, low, sign):
+def dip_transform(values, table, sign):
     stacked = jnp.concatenate([part for pair in values for part in pair], axis=0)
-    product = rows_dot(stacked, high, low)
+    product = rows_dot(stacked, table)
     out = []
     for n in range(4):
         real, imag = product[96 * n : 96 * n + 48], product[96 * n + 48 : 96 * (n + 1)]
@@ -160,7 +149,7 @@
     return parts
 
 
-def scatter_kernel(iv_ref, after_ref, out_ref, flipped_ref):
+def scatter_kernel(iv_ref, out_ref, flipped_ref):
     for c in range(3):
         flipped_ref[...] = iv_ref[c].T
         for s in range(2):
@@ -173,12 +162,10 @@
     out_ref[:, 7, :] = zero
 
 
-def strike_forward_kernel(
-    in_ref, strike_ref, twiddle_ref, high_ref, low_ref, after_ref, also_ref, out_ref
-):
+def strike_forward_kernel(in_ref, table_ref, after_ref, also_ref, out_ref):
     value = jnp.concatenate([in_ref[:, m, :] for m in range(6)], axis=1)
-    value = stacked_dot(strike_ref[...], value)
-    cos, sin = twiddle_ref[0], twiddle_ref[1]
+    value = stacked_dot(table_ref[288:352, 0:32], value)
+    cos, sin = table_ref[256:288, 0:128], table_ref[256:288, 128:256]
     rows = []
     for m in range(6):
         real = value[:32, 128 * m : 128 * (m + 1)]
@@ -186,7 +173,7 @@
         rows.append(
             jnp.concatenate([real * cos + imag * sin, imag * cos - real * sin], axis=1)
         )
-    value = rows_dot(jnp.concatenate(rows, axis=0), high_ref[...], low_ref[...])
+    value = rows_dot(jnp.concatenate(rows, axis=0), table_ref[0:256, :])
     zero = jnp.zeros((32, 128), jnp.float32)
     for t in range(2):
         parts = [value[32 * m : 32 * (m + 1), 128 * t : 128 * (t + 1)] for m in range(6)]
@@ -195,17 +182,15 @@
             out_ref[32 * (8 * t + b) : 32 * (8 * t + b + 1), :] = parts[b]
 
 
-def strike_inverse_kernel(
-    in_ref, strike_ref, twiddle_ref, high_ref, low_ref, out_ref
-):
+def strike_inverse_kernel(in_ref, table_ref, out_ref):
     columns = []
     for t in range(2):
         columns.append(
             block_transpose([in_ref[32 * (8 * t + b) : 32 * (8 * t + b + 1), :] for b in range(8)])
         )
     rows = [jnp.concatenate([columns[0][m], columns[1][m]], axis=1) for m in range(8)]
-    value = rows_dot(jnp.concatenate(rows, axis=0), high_ref[...], low_ref[...])
-    cos, sin = twiddle_ref[0], twiddle_ref[1]
+    value = rows_dot(jnp.concatenate(rows, axis=0), table_ref[0:256, :])
+    cos, sin = table_ref[256:288, 0:128], table_ref[256:288, 128:256]
     reals, imags = [], []
     for m in range(8):
         real = value[32 * m : 32 * (m + 1), :128]
@@ -215,7 +200,7 @@
     value = jnp.concatenate(
         [jnp.concatenate(reals, axis=1), jnp.concatenate(imags, axis=1)], axis=0
     )
-    value = stacked_dot(strike_ref[...], value)
+    value = stacked_dot(table_ref[288:320, 0:64], value)
     parts = [value[:, 128 * m : 128 * (m + 1)] for m in range(8)]
     lane = lane_of((32, 128))
     last = parts[7]
@@ -231,10 +216,7 @@
         out_ref[:, m, :] = parts[m]
 
 
-def dip_kernel(
-    in_ref, weight_ref, past_ref, twiddle_ref, inner_ref,
-    fh_ref, fl_ref, ih_ref, il_ref, after_ref, also_ref, out_ref,
-):
+def dip_kernel(in_ref, weight_ref, past_ref, table_ref, after_ref, also_ref, out_ref):
     flipped = in_ref[...].T
     values = []
     for v in range(4):
@@ -248,10 +230,18 @@
                 for ri in range(2)
             ]
         )
-    inner = [(inner_ref[b, 0:1, :], inner_ref[b, 1:2, :]) for b in range(4)]
+    inner = [
+        (table_ref[256 + b : 257 + b, 0:128], table_ref[256 + b : 257 + b, 128:256])
+        for b in range(4)
+    ]
+    outer = []
+    for s in range(2):
+        at = [264 + 16 * b + 8 * s for b in range(4)]
+        cos = jnp.concatenate([table_ref[n : n + 8, 0:128] for n in at], axis=1)
+        outer.append((cos, jnp.concatenate([table_ref[n : n + 8, 128:256] for n in at], axis=1)))
     values = radix_four(values, -1)
     values = [turn(*values[b], *inner[b], -1) for b in range(4)]
-    values = dip_transform(values, fh_ref[...], fl_ref[...], -1)
+    values = dip_transform(values, table_ref[0:128, :], -1)
     real = jnp.concatenate([pair[0] for pair in values], axis=1)
     imag = jnp.concatenate([pair[1] for pair in values], axis=1)
     top = row_of((8, NF)) < 4
@@ -261,7 +251,7 @@
         turned = []
         for s in range(2):
             rows = slice(16 * c + 8 * s, 16 * c + 8 * s + 8)
-            turned.append(turn(real[rows], imag[rows], twiddle_ref[s, 0], twiddle_ref[s, 1], -1))
+            turned.append(turn(real[rows], imag[rows], *outer[s], -1))
         even = [turned[0][ri] + turned[1][ri] for ri in range(2)]
         odd = [turned[0][ri] - turned[1][ri] for ri in range(2)]
         odd = [jnp.where(top, odd[0], odd[1]), jnp.where(top, odd[1], -odd[0])]
@@ -282,14 +272,14 @@
         ]
         for s in range(2):
             pair = [even[ri] + odd[ri] if s == 0 else even[ri] - odd[ri] for ri in range(2)]
-            pair = turn(*pair, twiddle_ref[s, 0], twiddle_ref[s, 1], 1)
+            pair = turn(*pair, *outer[s], 1)
             reals.append(pair[0])
             imags.append(pair[1])
     real, imag = jnp.concatenate(reals, axis=0), jnp.concatenate(imags, axis=0)
     values = [
         (real[:, 128 * b : 128 * (b + 1)], imag[:, 128 * b : 128 * (b + 1)]) for b in range(4)
     ]
-    values = dip_transform(values, ih_ref[...], il_ref[...], 1)
+    values = dip_transform(values, table_ref[128:256, :], 1)
     values = [turn(*values[b], *inner[b], 1) for b in range(4)]
     values = radix_four(values, 1)
     real = jnp.concatenate([pair[0] for pair in values], axis=1)
@@ -331,10 +321,18 @@
     return [jnp.concatenate([column[n] for column in columns], axis=1) for n in range(2)]
 
 
-def past_kernel(kernel_ref, history_ref, weight_ref, out_ref, rows_ref):
+def past_kernel(
+    kernel_hbm, history_hbm, weight_ref, out_ref, rows_ref, kernel_ref, history_ref, arrived
+):
+    first = pltpu.make_async_copy(kernel_hbm, kernel_ref, arrived.at[0])
+    second = pltpu.make_async_copy(history_hbm, history_ref, arrived.at[1])
+    first.start()
+    second.start()
+    first.wait()
     groups = mode_groups([kernel_ref[0, a, 0] for a in range(4)], rows_ref.at[6])
     for parity in range(2):
         weight_ref[parity] = groups[parity]
+    second.wait()
     for z in range(2):
         for c in range(3):
             tiles = []
@@ -364,7 +362,7 @@
     return total
 
 
-def part_kernel(velocity_ref, stress_ref, part_ref, low_ref, high_ref):
+def part_kernel(velocity_ref, stress_ref, part_ref, ylo_ref, yhi_ref, xlo_ref, xhi_ref):
     row, lane = row_of((64, 128)), lane_of((64, 128))
     for n in range(3):
         for z in range(4):
@@ -378,29 +376,28 @@
             if z > 0:
                 total = total - stress_ref[DEEP[n], z - 1]
             part_ref[n, z] = velocity_ref[n, z] + STEP * total
-    low_ref[...] = pack_columns(stress_ref, part_ref, 0)
-    high_ref[...] = pack_columns(stress_ref, part_ref, 127)
-
-
-def column_kernel(part_ref, stress_ref, ylo_ref, yhi_ref, out_ref, low_ref, high_ref):
-    lane = lane_of((64, 128))
-    ylo, yhi = ylo_ref[...], yhi_ref[...]
-    edges = [[], []]
-    for n in range(3):
-        for z in range(4):
-            at = 4 * n + z
-            field = part_ref[n, z]
-            field = field - jnp.where(lane == 0, STEP * roll(ylo, -at, 1), 0.0)
-            field = field + jnp.where(lane == 127, STEP * roll(yhi, 127 - at, 1), 0.0)
-            out_ref[n, z] = field
-            edges[0].append(field[0:1])
-            edges[1].append(field[63:64])
-    pad = jnp.zeros((6, 128), jnp.float32)
-    for i, ref in enumerate((low_ref, high_ref)):
-        at = 63 * i
+    ylo_ref[...] = pack_columns(stress_ref, part_ref, 0)
+    yhi_ref[...] = pack_columns(stress_ref, part_ref, 127)
+    pad = jnp.zeros((8, 128), jnp.float32)
+    for at, ref in ((0, xlo_ref), (63, xhi_ref)):
         rows = [stress_ref[ACROSS[n], z, at : at + 1, :] for n in range(3) for z in range(4)]
-        rows += edges[i] + [ylo[at : at + 1], yhi[at : at + 1], pad]
-        ref[...] = jnp.concatenate(rows, axis=0)
+        rows += [part_ref[n, z, at : at + 1, :] for n in range(3) for z in range(4)]
+        ref[...] = jnp.concatenate(rows + [pad], axis=0)
+
+
+def column_kernel(low_ref, high_ref, ylo_ref, yhi_ref, out_low_ref, out_high_ref):
+    lane, row = lane_of((32, 128)), row_of((32, 128))
+    for at, ref, out_ref in ((0, low_ref, out_low_ref), (63, high_ref, out_high_ref)):
+        low = jnp.broadcast_to(ylo_ref[at : at + 1, :], (32, 128))
+        high = jnp.broadcast_to(yhi_ref[at : at + 1, :], (32, 128))
+        before = jnp.zeros((32, 128), jnp.float32)
+        after = jnp.zeros((32, 128), jnp.float32)
+        for n in range(12):
+            before = jnp.where((row == 12 + n) & (lane == 0), roll(low, -n, 1), before)
+            after = jnp.where((row == 12 + n) & (lane == 127), roll(high, 127 - n, 1), after)
+        edge = ref[...] + STEP * (after - before)
+        edge = jnp.where(row == 24, low, edge)
+        out_ref[...] = jnp.where(row == 25, high, edge)
 
 
 def row_kernel(
@@ -408,13 +405,16 @@
     own_xlo_ref, own_xhi_ref, own_ylo_ref, own_yhi_ref, after_ref,
     out_ref, vxlo_ref, vxhi_ref, vylo_ref, vyhi_ref,
 ):
-    row = row_of((64, 128))
+    row, lane = row_of((64, 128)), lane_of((64, 128))
+    ylo, yhi = ylo_ref[...], yhi_ref[...]
     for n in range(3):
         for z in range(4):
             at = 4 * n + z
             field = part_ref[n, z]
             field = field - jnp.where(row == 0, STEP * xlo_ref[at : at + 1, :], 0.0)
             field = field + jnp.where(row == 63, STEP * xhi_ref[at : at + 1, :], 0.0)
+            field = field - jnp.where(lane == 0, STEP * roll(ylo, -at, 1), 0.0)
+            field = field + jnp.where(lane == 127, STEP * roll(yhi, 127 - at, 1), 0.0)
             out_ref[n, z] = field
     vxlo_ref[...] = xlo_ref[12:28, :] + STEP * own_xlo_ref[0:16, :]
     vxhi_ref[...] = xhi_ref[12:28, :] - STEP * own_xhi_ref[0:16, :]
@@ -422,9 +422,9 @@
         corner = jnp.where(row == 63, STEP * xhi_ref[24 + side : 25 + side, :], 0.0)
         corner = corner - jnp.where(row == 0, STEP * xlo_ref[24 + side : 25 + side, :], 0.0)
         if side == 0:
-            columns = roll(ylo_ref[...], -12, 1) + STEP * own_ylo_ref[...]
+            columns = roll(ylo, -12, 1) + STEP * own_ylo_ref[...]
         else:
-            columns = roll(yhi_ref[...], -12, 1) - STEP * own_yhi_ref[...]
+            columns = roll(yhi, -12, 1) - STEP * own_yhi_ref[...]
         ref[...] = columns + roll(corner, -24, 1)
 
 
@@ -527,54 +527,46 @@
     )(*arguments, *after)
 
 
-def scatter(iv, after):
+def scatter(iv):
     scratch = [pltpu.VMEM((128, 64), jnp.float32)]
-    return call(scatter_kernel, f32(32, 8, 128), (iv,), after, scratch)
+    return call(scatter_kernel, f32(32, 8, 128), (iv,), scratch=scratch)
 
 
 def strike_forward(arrived, after):
-    forward, _ = strike_tables()
-    (high, low), _ = cell_tables()
-    arguments = (arrived, forward, strike_twiddle(), high, low)
+    arguments = (arrived, strike_tables(False))
     return call(strike_forward_kernel, f32(512, 128), arguments, after)
 
 
 def strike_inverse(arrived):
-    _, inverse = strike_tables()
-    _, (high, low) = cell_tables()
-    arguments = (arrived, inverse, strike_twiddle(), high, low)
-    return call(strike_inverse_kernel, f32(32, 8, 128), arguments)
+    return call(strike_inverse_kernel, f32(32, 8, 128), (arrived, strike_tables(True)))
 
 
 def dip(arrived, weight, past, after):
-    tables = (dip_twiddle(), dip_inner_twiddle(), *dip_tables())
-    arguments = (arrived, weight, past, *tables)
-    return call(dip_kernel, f32(512, 128), arguments, after)
+    return call(dip_kernel, f32(512, 128), (arrived, weight, past, dip_tables()), after)
 
 
 def past_terms(kernel, history):
     return call(
         past_kernel,
         (f32(2, 8, NF), f32(3, 2, 2, 8, NF)),
+        (),
         (kernel, history),
-        scratch=[pltpu.VMEM((7, 16, 8, 128), jnp.float32)],
+        [
+            pltpu.VMEM((7, 16, 8, 128), jnp.float32),
+            pltpu.VMEM(kernel.shape, jnp.float32),
+            pltpu.VMEM(history.shape, jnp.float32),
+            pltpu.SemaphoreType.DMA((2,)),
+        ],
     )
 
 
 def velocity_part(velocity, stress):
-    return call(
-        part_kernel,
-        (f32(3, 4, 64, 128), f32(64, 128), f32(64, 128)),
-        (velocity, stress),
-    )
-
-
-def velocity_columns(part, stress, halo):
-    return call(
-        column_kernel,
-        (f32(3, 4, 64, 128), f32(32, 128), f32(32, 128)),
-        (part, stress, *halo),
-    )
+    columns, rows = (f32(64, 128),) * 2, (f32(32, 128),) * 2
+    return call(part_kernel, (f32(3, 4, 64, 128), *columns, *rows), (velocity, stress))
+
+
+def velocity_columns(edges, halo):
+    return call(column_kernel, (f32(32, 128),) * 2, (*edges, *halo))
 
 
 def velocity_rows(part, halo, own, after):
@@ -614,12 +606,12 @@
 
 
 def local(interface_velocity, history, kernel, velocity, stress, cohesion):
-    part, *own_columns = velocity_part(velocity, stress)
+    arrived = strike_swap(scatter(interface_velocity))
+    part, *edges = velocity_part(velocity, stress)
+    own_columns, own_rows = edges[:2], edges[2:]
     columns = exchange("by", *own_columns)
-    arrived = strike_swap(scatter(interface_velocity, (part,)))
     sent = strike_forward(arrived, columns)
-    part, *own_rows = velocity_columns(part, stress, columns)
-    rows = exchange("bx", *own_rows)
+    rows = exchange("bx", *velocity_columns(own_rows, columns))
     arrived = whole_swap(sent)
     weight, past = past_terms(kernel, history)
     sent = dip(arrived, weight, past, rows)

time: 131 us -> 124 us (0.947)
  local copies, waits for them, and re-layouts: 10.1 us -> 3.05 us
  starting transfers between devices: 55.5 us -> 57.9 us
  waiting for transfers between devices: 22.5 us -> 21 us
    unnamed x64 -> x22, local copies, waits for them, and re-layouts: 10.1 us -> 3.05 us
    all_to_all x2, waiting for transfers between devices: 15.4 us -> 12.7 us  [strike_swap(): return lax.all_to_all(value, 'bx', split_axis=0, concat_axis=0, tiled=True)]
    all_to_all x1, starting transfers between devices: 16.2 us -> 18.8 us  [whole_swap(): lax.all_to_all(value, ('by', 'bx'), split_axis=0, concat_axis=0, tiled=True)]
  transfers between devices with their start and end apart: 7 -> 7, of which waited for: 4 -> 3; matrix products, arithmetic and copies ran while one was open for 0% -> 0% of each run, Pallas kernels for 1% -> 2%
where the time goes in v4:
time: 124 us
  starting transfers between devices  57.9 us (47%)
  blocking collectives  31.3 us (25%)
  waiting for transfers between devices  21 us (17%)
  Pallas kernels  9.66 us (8%)
  local copies, waits for them, and re-layouts  3.05 us (2%)
    all_to_all x1, blocking collectives, whole_swap(): lax.all_to_all(value, ('by', 'bx'), split_axis=0, concat_axis=0, tiled=True)  31.3 us
    all_to_all x2, starting transfers between devices, strike_swap(): return lax.all_to_all(value, 'bx', split_axis=0, concat_axis=0, tiled=True)  21.8 us
    all_to_all x1, starting transfers between devices, whole_swap(): lax.all_to_all(value, ('by', 'bx'), split_axis=0, concat_axis=0, tiled=True)  18.8 us
    all_to_all x2, waiting for transfers between devices, strike_swap(): return lax.all_to_all(value, 'bx', split_axis=0, concat_axis=0, tiled=True)  12.7 us
    ppermute x2, starting transfers between devices, exchange(): lax.ppermute(low, axis, [(i, (i - 1) % count) for i in range(count)])  10.7 us
    pallas_call x9, Pallas kernels, call(): pl.pallas_call(kernel, out_shape=out_shape, in_specs=[VMEM] * len(argumen...  9.66 us
    all_to_all x1, waiting for transfers between devices, whole_swap(): lax.all_to_all(value, ('by', 'bx'), split_axis=0, concat_axis=0, tiled=True)  7.31 us
    ppermute x2, starting transfers between devices, exchange(): lax.ppermute(high, axis, [(i, (i + 1) % count) for i in range(count)])  6.64 us
  transfers between devices with their start and end apart: 7, of which 3 were waited for; matrix products, arithmetic and copies ran while one was open for 0% of the time, Pallas kernels for 2%

profile of v4, /device:TPU:1, one launch (start us, length us, event | category | flops | bytes accessed | tf_op | source)
XLA Modules:
  0.0 123.7 jit_solution(11749822881713201089)
XLA Ops:
  0.6 0.0 copy-start.3
  0.6 0.9 copy-done.3
  1.5 1.0 shard_map.104
  2.6 17.2 %all-to-all-start = ((f32[32,8,128]{2,1,0:T(8,128)}), f32[32,8,128]{2,1,0:T(8,128)S(1)}, u32[]{:S(2)}, u32[]{:S(2)}) async-start(f32[32,8,128]{2,1,0:T(8,128)} %shard_map.104), calls=%async_computation | async-start | bytes 262144 | tf_op jit(solution)/shard_map/all_to_all | solution.py:599
  19.8 0.0 copy-start
  19.8 1.1 copy-done
  20.9 1.0 copy-done.5
  21.9 0.9 shard_map.105
  22.8 3.1 %collective-permute-start = (f32[64,128]{1,0:T(8,128)S(1)}, f32[64,128]{1,0:T(8,128)S(1)}, u32[]{:S(2)}, u32[]{:S(2)}) collective-permute-start(f32[64,128]{1,0:T(8,128)S(1)} %get-tuple-element.16.own_yhi_ref), channel_id=1, source_target_pairs={{0,1},{1,2},{2,3},{3,4},{4,5},{5,6},{6,7},{7,8},{8,9},{9,10},{10,1... | collective-permute-start | bytes 98312 | tf_op jit(solution)/shard_map/ppermute | solution.py:593
  25.9 6.1 %collective-permute-start.1 = (f32[64,128]{1,0:T(8,128)S(1)}, f32[64,128]{1,0:T(8,128)S(1)}, u32[]{:S(2)}, u32[]{:S(2)}) collective-permute-start(f32[64,128]{1,0:T(8,128)S(1)} %get-tuple-element.17.own_ylo_ref), channel_id=1, source_target_pairs={{0,15},{1,0},{2,1},{3,2},{4,3},{5,4},{6,5},{7,6},{8,7},{9,8},{10,9... | collective-permute-start | bytes 98312 | tf_op jit(solution)/shard_map/ppermute | solution.py:594
  32.0 0.0 collective-permute-done.after_ref.ylo_ref
  32.0 1.0 collective-permute-done.1.also_ref.yhi_ref
  33.0 0.0 all-to-all-done.in_ref
  33.0 1.4 %shard_map.106 = f32[512,128]{1,0:T(8,128)} custom-call(f32[32,8,128]{2,1,0:T(8,128)S(1)} %all-to-all-done.in_ref, f32[352,256]{1,0:T(8,128)S(1)} %copy-done.6, f32[64,128]{1,0:T(8,128)S(1)} %collective-permute-done.after_ref.ylo_ref, f32[64,128]{1,0:T(8,128)S(1)} %collective-permute-done.1.also_ref.yhi_ref), custom_call_target="tpu_custom_call" | custom-call | tf_op jit(solution)/shard_map/pallas_call | solution.py:520
  34.4 18.8 %all-to-all-start.1 = ((f32[512,1,128]{2,1,0:T(1,128)}), f32[512,1,128]{2,1,0:T(1,128)S(1)}, u32[]{:S(2)}, u32[]{:S(2)}) async-start(f32[512,1,128]{2,1,0:T(1,128)} %bitcast.1), calls=%async_computation.1 | async-start | bytes 524288 | tf_op jit(solution)/shard_map/all_to_all | solution.py:604
  53.2 0.1 shard_map.108
  53.3 3.5 %collective-permute-start.2 = (f32[32,128]{1,0:T(8,128)S(1)}, f32[32,128]{1,0:T(8,128)S(1)}, u32[]{:S(2)}, u32[]{:S(2)}) collective-permute-start(f32[32,128]{1,0:T(8,128)S(1)} %get-tuple-element.22), channel_id=1, source_target_pairs={{0,16},{16,32},{32,48},{48,64},{64,80},{80,96},{96,112},{112,128},... | collective-permute-start | bytes 49160 | tf_op jit(solution)/shard_map/ppermute | solution.py:593
  56.9 4.6 %collective-permute-start.3 = (f32[32,128]{1,0:T(8,128)S(1)}, f32[32,128]{1,0:T(8,128)S(1)}, u32[]{:S(2)}, u32[]{:S(2)}) collective-permute-start(f32[32,128]{1,0:T(8,128)S(1)} %get-tuple-element.23), channel_id=1, source_target_pairs={{0,496},{16,0},{32,16},{48,32},{64,48},{80,64},{96,80},{112,96},{1... | collective-permute-start | bytes 49160 | tf_op jit(solution)/shard_map/ppermute | solution.py:594
  61.5 1.6 %shard_map.107 = (f32[2,8,512]{2,1,0:T(8,128)S(1)}, f32[3,2,2,8,512]{4,3,2,1,0:T(8,128)S(1)}) custom-call(f32[7,4,1,16,128]{4,3,2,1,0:T(8,128)S(1)} %copy-done.9, f32[6,2,3,4,1,16,128]{6,5,4,3,2,1,0:T(8,128)S(1)} %copy-done.2), custom_call_target="tpu_custom_call" | custom-call | tf_op jit(solution)/shard_map/pallas_call | solution.py:520
  63.1 0.0 copy-start.8
  63.1 0.0 collective-permute-done.3.also_ref.xhi_ref
  63.1 7.3 %all-to-all-done.1 = f32[512,1,128]{2,1,0:T(1,128)S(1)} async-done(((f32[512,1,128]{2,1,0:T(1,128)}), f32[512,1,128]{2,1,0:T(1,128)S(1)}, u32[]{:S(2)}, u32[]{:S(2)}) %all-to-all-start.1) | async-done | bytes 262176 | tf_op jit(solution)/shard_map/all_to_all | solution.py:604
  70.4 1.1 shard_map.109.after_ref
  71.6 0.0 copy-start.1
  71.6 0.0 copy-start.4
  71.6 0.0 copy-start.10
  71.6 31.3 %all_to_all.20 = f32[512,1,128]{2,1,0:T(1,128)S(1)} all-to-all(f32[512,1,128]{2,1,0:T(1,128)S(1)} %bitcast.8), channel_id=1, replica_groups=mesh['bx'=32,'by'=16] {'by','bx'}, dimensions={0} | all-to-all | bytes 524288 | tf_op jit(solution)/shard_map/all_to_all | solution.py:604
  102.9 1.5 %shard_map.110 = f32[32,8,128]{2,1,0:T(8,128)} custom-call(f32[512,128]{1,0:T(8,128)S(1)} %bitcast.10, f32[320,256]{1,0:T(8,128)S(1)} %copy-done.8), custom_call_target="tpu_custom_call" | custom-call | tf_op jit(solution)/shard_map/pallas_call | solution.py:520
  104.3 4.6 %all-to-all-start.3 = ((f32[32,8,128]{2,1,0:T(8,128)}), f32[32,8,128]{2,1,0:T(8,128)S(1)}, u32[]{:S(2)}, u32[]{:S(2)}) async-start(f32[32,8,128]{2,1,0:T(8,128)} %shard_map.110), calls=%async_computation.3 | async-start | bytes 262144 | tf_op jit(solution)/shard_map/all_to_all | solution.py:599
  108.9 0.3 shard_map.111
  109.2 12.7 %all-to-all-done.3.in_ref = f32[32,8,128]{2,1,0:T(8,128)S(1)} async-done(((f32[32,8,128]{2,1,0:T(8,128)}), f32[32,8,128]{2,1,0:T(8,128)S(1)}, u32[]{:S(2)}, u32[]{:S(2)}) %all-to-all-start.3) | async-done | bytes 131104 | tf_op jit(solution)/shard_map/all_to_all | solution.py:599
  121.9 1.8 %shard_map.112 = (f32[3,4,64,128]{3,2,1,0:T(8,128)}, f32[6,4,64,128]{3,2,1,0:T(8,128)}) custom-call(f32[32,8,128]{2,1,0:T(8,128)S(1)} %all-to-all-done.3.in_ref, f32[3,4,64,128]{3,2,1,0:T(8,128)S(1)} %get-tuple-element.25.before_ref, f32[6,4,64,128]{3,2,1,0:T(8,128)S(1)} %copy-done.1, f32[4,64,128]{2,1,0:T(8,128)S(1)} %copy-done.10, ...), custom_call_target="tpu_custom_call" | custom-call | tf_op jit(solution)/shard_map/pallas_call | solution.py:520
  (14 shorter events, 0.0 us)
Async XLA Ops:
  0.6 0.9 copy-start.3
  1.5 31.5 %copy-start.6 = (f32[352,256]{1,0:T(8,128)S(1)}, f32[352,256]{1,0:T(8,128)}, u32[]{:S(2)}) copy-start(f32[352,256]{1,0:T(8,128)} %constant.6.clone.table_ref) | copy-start | bytes 1081348
  2.6 30.5 %all-to-all-start = ((f32[32,8,128]{2,1,0:T(8,128)}), f32[32,8,128]{2,1,0:T(8,128)S(1)}, u32[]{:S(2)}, u32[]{:S(2)}) async-start(f32[32,8,128]{2,1,0:T(8,128)} %shard_map.104), calls=%async_computation | async-start | bytes 262144 | tf_op jit(solution)/shard_map/all_to_all | solution.py:599
  19.8 1.1 copy-start
  20.9 1.0 copy-start.5
  21.9 39.6 %copy-start.2 = (f32[6,2,3,4,1,16,128]{6,5,4,3,2,1,0:T(8,128)S(1)}, f32[6,2,3,4,1,16,128]{6,5,4,3,2,1,0:T(8,128)}, u32[]{:S(2)}) copy-start(f32[6,2,3,4,1,16,128]{6,5,4,3,2,1,0:T(8,128)} %history_hbm.1) | copy-start | bytes 3538948
  21.9 39.6 %copy-start.9 = (f32[7,4,1,16,128]{4,3,2,1,0:T(8,128)S(1)}, f32[7,4,1,16,128]{4,3,2,1,0:T(8,128)}, u32[]{:S(2)}) copy-start(f32[7,4,1,16,128]{4,3,2,1,0:T(8,128)} %kernel_hbm.1) | copy-start | bytes 688132
  22.8 9.2 %collective-permute-start = (f32[64,128]{1,0:T(8,128)S(1)}, f32[64,128]{1,0:T(8,128)S(1)}, u32[]{:S(2)}, u32[]{:S(2)}) collective-permute-start(f32[64,128]{1,0:T(8,128)S(1)} %get-tuple-element.16.own_yhi_ref), channel_id=1, source_target_pairs={{0,1},{1,2},{2,3},{3,4},{4,5},{5,6},{6,7},{7,8},{8,9},{9,10},{10,1... | collective-permute-start | bytes 98312 | tf_op jit(solution)/shard_map/ppermute | solution.py:593
  25.9 7.1 %collective-permute-start.1 = (f32[64,128]{1,0:T(8,128)S(1)}, f32[64,128]{1,0:T(8,128)S(1)}, u32[]{:S(2)}, u32[]{:S(2)}) collective-permute-start(f32[64,128]{1,0:T(8,128)S(1)} %get-tuple-element.17.own_ylo_ref), channel_id=1, source_target_pairs={{0,15},{1,0},{2,1},{3,2},{4,3},{5,4},{6,5},{7,6},{8,7},{9,8},{10,9... | collective-permute-start | bytes 98312 | tf_op jit(solution)/shard_map/ppermute | solution.py:594
  34.4 36.0 %copy-start.7 = (f32[328,256]{1,0:T(8,128)S(1)}, f32[328,256]{1,0:T(8,128)}, u32[]{:S(2)}) copy-start(f32[328,256]{1,0:T(8,128)} %constant.7.clone.table_ref) | copy-start | bytes 1007620
  34.4 36.0 %all-to-all-start.1 = ((f32[512,1,128]{2,1,0:T(1,128)}), f32[512,1,128]{2,1,0:T(1,128)S(1)}, u32[]{:S(2)}, u32[]{:S(2)}) async-start(f32[512,1,128]{2,1,0:T(1,128)} %bitcast.1), calls=%async_computation.1 | async-start | bytes 524288 | tf_op jit(solution)/shard_map/all_to_all | solution.py:604
  53.3 9.8 %collective-permute-start.2 = (f32[32,128]{1,0:T(8,128)S(1)}, f32[32,128]{1,0:T(8,128)S(1)}, u32[]{:S(2)}, u32[]{:S(2)}) collective-permute-start(f32[32,128]{1,0:T(8,128)S(1)} %get-tuple-element.22), channel_id=1, source_target_pairs={{0,16},{16,32},{32,48},{48,64},{64,80},{80,96},{96,112},{112,128},... | collective-permute-start | bytes 49160 | tf_op jit(solution)/shard_map/ppermute | solution.py:593
  56.9 6.2 %collective-permute-start.3 = (f32[32,128]{1,0:T(8,128)S(1)}, f32[32,128]{1,0:T(8,128)S(1)}, u32[]{:S(2)}, u32[]{:S(2)}) collective-permute-start(f32[32,128]{1,0:T(8,128)S(1)} %get-tuple-element.23), channel_id=1, source_target_pairs={{0,496},{16,0},{32,16},{48,32},{64,48},{80,64},{96,80},{112,96},{1... | collective-permute-start | bytes 49160 | tf_op jit(solution)/shard_map/ppermute | solution.py:594
  63.1 39.8 %copy-start.8 = (f32[320,256]{1,0:T(8,128)S(1)}, f32[320,256]{1,0:T(8,128)}, u32[]{:S(2)}) copy-start(f32[320,256]{1,0:T(8,128)} %constant.8.clone.table_ref) | copy-start | bytes 983044
  71.6 50.3 %copy-start.1 = (f32[6,4,64,128]{3,2,1,0:T(8,128)S(1)}, f32[6,4,64,128]{3,2,1,0:T(8,128)}, u32[]{:S(2)}) copy-start(f32[6,4,64,128]{3,2,1,0:T(8,128)} %stress_ref.3) | copy-start | bytes 2359300
  71.6 50.3 %copy-start.4 = (f32[3,64,128]{2,1,0:T(8,128)S(1)}, f32[3,64,128]{2,1,0:T(8,128)}, u32[]{:S(2)}) copy-start(f32[3,64,128]{2,1,0:T(8,128)} %iv_ref.3) | copy-start | bytes 294916
  71.6 50.3 %copy-start.10 = (f32[4,64,128]{2,1,0:T(8,128)S(1)}, f32[4,64,128]{2,1,0:T(8,128)}, u32[]{:S(2)}) copy-start(f32[4,64,128]{2,1,0:T(8,128)} %cohesion_ref.1) | copy-start | bytes 393220
  104.3 17.5 %all-to-all-start.3 = ((f32[32,8,128]{2,1,0:T(8,128)}), f32[32,8,128]{2,1,0:T(8,128)S(1)}, u32[]{:S(2)}, u32[]{:S(2)}) async-start(f32[32,8,128]{2,1,0:T(8,128)} %shard_map.110), calls=%async_computation.3 | async-start | bytes 262144 | tf_op jit(solution)/shard_map/all_to_all | solution.py:599

commit v5 on v4

--- a/solution.py
+++ b/solution.py
@@ -13,6 +13,7 @@
 NF = 512
 SCALE = 1.0 / 2048.0
 VMEM = pl.BlockSpec(memory_space=pltpu.VMEM)
+LONG = pl.CostEstimate(flops=30_000_000_000, bytes_accessed=20_000_000, transcendentals=0)
 PARAMS = pltpu.CompilerParams(vmem_limit_bytes=16 * 1024 * 1024)
 
 
@@ -402,7 +403,7 @@
 
 def row_kernel(
     part_ref, xlo_ref, xhi_ref, ylo_ref, yhi_ref,
-    own_xlo_ref, own_xhi_ref, own_ylo_ref, own_yhi_ref, after_ref,
+    own_xlo_ref, own_xhi_ref, own_ylo_ref, own_yhi_ref,
     out_ref, vxlo_ref, vxhi_ref, vylo_ref, vyhi_ref,
 ):
     row, lane = row_of((64, 128)), lane_of((64, 128))
@@ -515,7 +516,7 @@
     return jax.ShapeDtypeStruct(shape, jnp.float32)
 
 
-def call(kernel, out_shape, arguments, after=(), scratch=()):
+def call(kernel, out_shape, arguments, after=(), scratch=(), cost=None):
     many = isinstance(out_shape, tuple)
     return pl.pallas_call(
         kernel,
@@ -524,6 +525,7 @@
         out_specs=(VMEM,) * len(out_shape) if many else VMEM,
         scratch_shapes=list(scratch),
         compiler_params=PARAMS,
+        cost_estimate=cost,
     )(*arguments, *after)
 
 
@@ -566,15 +568,15 @@
 
 
 def velocity_columns(edges, halo):
-    return call(column_kernel, (f32(32, 128),) * 2, (*edges, *halo))
-
-
-def velocity_rows(part, halo, own, after):
+    return call(column_kernel, (f32(32, 128),) * 2, (*edges, *halo), cost=LONG)
+
+
+def velocity_rows(part, halo, own):
     return call(
         row_kernel,
         (f32(3, 4, 64, 128), f32(16, 128), f32(16, 128), f32(64, 128), f32(64, 128)),
         (part, *halo, *own),
-        (after,),
+        cost=LONG,
     )
 
 
@@ -610,12 +612,13 @@
     part, *edges = velocity_part(velocity, stress)
     own_columns, own_rows = edges[:2], edges[2:]
     columns = exchange("by", *own_columns)
-    sent = strike_forward(arrived, columns)
-    rows = exchange("bx", *velocity_columns(own_rows, columns))
+    edges = velocity_columns(own_rows, columns)
+    sent = strike_forward(arrived, edges)
+    rows = exchange("bx", *edges)
+    before, *halo = velocity_rows(part, (*rows, *columns), (*own_rows, *own_columns))
     arrived = whole_swap(sent)
     weight, past = past_terms(kernel, history)
-    sent = dip(arrived, weight, past, rows)
-    before, *halo = velocity_rows(part, (*rows, *columns), (*own_rows, *own_columns), sent)
+    sent = dip(arrived, weight, past, halo[:2])
     arrived = whole_swap(sent)
     arrived = strike_swap(strike_inverse(arrived))
     return slab(arrived, before, stress, cohesion, interface_velocity, halo)

time: 124 us -> 124 us (level)
  blocking collectives: 31.3 us -> 43.3 us
  starting transfers between devices: 57.9 us -> 46.2 us
  waiting for transfers between devices: 21 us -> 22.4 us
    all_to_all x0 -> x1, blocking collectives: none -> 17.3 us  [strike_swap(): return lax.all_to_all(value, 'bx', split_axis=0, concat_axis=0, tiled=True)]
    all_to_all x1, waiting for transfers between devices: 7.31 us -> 16.9 us  [whole_swap(): lax.all_to_all(value, ('by', 'bx'), split_axis=0, concat_axis=0, tiled=True)]
    all_to_all x2 -> x1, starting transfers between devices: 21.8 us -> 14.4 us  [strike_swap(): return lax.all_to_all(value, 'bx', split_axis=0, concat_axis=0, tiled=True)]
    all_to_all x2 -> x1, waiting for transfers between devices: 12.7 us -> 5.48 us  [strike_swap(): return lax.all_to_all(value, 'bx', split_axis=0, concat_axis=0, tiled=True)]
    all_to_all x1, blocking collectives: 31.3 us -> 26 us  [whole_swap(): lax.all_to_all(value, ('by', 'bx'), split_axis=0, concat_axis=0, tiled=True)]
    all_to_all x1, starting transfers between devices: 18.8 us -> 13.6 us  [whole_swap(): lax.all_to_all(value, ('by', 'bx'), split_axis=0, concat_axis=0, tiled=True)]
    ppermute x2, starting transfers between devices: 6.64 us -> 8.25 us  [exchange(): lax.ppermute(high, axis, [(i, (i + 1) % count) for i in range(count)])]
    unnamed x22 -> x20, local copies, waits for them, and re-layouts: 3.05 us -> 2.17 us
  transfers between devices with their start and end apart: 7 -> 6, of which waited for: 3 -> 2; matrix products, arithmetic and copies ran while one was open for 0% -> 0% of each run, Pallas kernels for 2% -> 4%
where the time goes in v5:
time: 124 us
  starting transfers between devices  46.2 us (37%)
  blocking collectives  43.3 us (35%)
  waiting for transfers between devices  22.4 us (18%)
  Pallas kernels  9.04 us (7%)
  local copies, waits for them, and re-layouts  2.17 us (2%)
    all_to_all x1, blocking collectives, whole_swap(): lax.all_to_all(value, ('by', 'bx'), split_axis=0, concat_axis=0, tiled=True)  26 us
    all_to_all x1, blocking collectives, strike_swap(): return lax.all_to_all(value, 'bx', split_axis=0, concat_axis=0, tiled=True)  17.3 us
    all_to_all x1, waiting for transfers between devices, whole_swap(): lax.all_to_all(value, ('by', 'bx'), split_axis=0, concat_axis=0, tiled=True)  16.9 us
    all_to_all x1, starting transfers between devices, strike_swap(): return lax.all_to_all(value, 'bx', split_axis=0, concat_axis=0, tiled=True)  14.4 us
    all_to_all x1, starting transfers between devices, whole_swap(): lax.all_to_all(value, ('by', 'bx'), split_axis=0, concat_axis=0, tiled=True)  13.6 us
    ppermute x2, starting transfers between devices, exchange(): lax.ppermute(low, axis, [(i, (i - 1) % count) for i in range(count)])  10 us
    pallas_call x9, Pallas kernels, call(): pl.pallas_call(kernel, out_shape=out_shape, in_specs=[VMEM] * len(argumen...  9.04 us
    ppermute x2, starting transfers between devices, exchange(): lax.ppermute(high, axis, [(i, (i + 1) % count) for i in range(count)])  8.25 us
  transfers between devices with their start and end apart: 6, of which 2 were waited for; matrix products, arithmetic and copies ran while one was open for 0% of the time, Pallas kernels for 4%

profile of v5, /device:TPU:1, one launch (start us, length us, event | category | flops | bytes accessed | tf_op | source)
XLA Modules:
  0.0 123.9 jit_solution(15791700974940591363)
XLA Ops:
  0.6 0.0 copy-start
  0.6 1.1 copy-done
  1.8 1.0 copy-done.4
  2.8 0.9 shard_map.105
  3.7 4.8 %collective-permute-start = (f32[64,128]{1,0:T(8,128)S(1)}, f32[64,128]{1,0:T(8,128)S(1)}, u32[]{:S(2)}, u32[]{:S(2)}) collective-permute-start(f32[64,128]{1,0:T(8,128)S(1)} %get-tuple-element.18.own_yhi_ref), channel_id=1, source_target_pairs={{0,1},{1,2},{2,3},{3,4},{4,5},{5,6},{6,7},{7,8},{8,9},{9,10},{10,1... | collective-permute-start | bytes 98312 | tf_op jit(solution)/shard_map/ppermute | solution.py:595
  8.5 7.7 %collective-permute-start.1 = (f32[64,128]{1,0:T(8,128)S(1)}, f32[64,128]{1,0:T(8,128)S(1)}, u32[]{:S(2)}, u32[]{:S(2)}) collective-permute-start(f32[64,128]{1,0:T(8,128)S(1)} %get-tuple-element.19.own_ylo_ref), channel_id=1, source_target_pairs={{0,15},{1,0},{2,1},{3,2},{4,3},{5,4},{6,5},{7,6},{8,7},{9,8},{10,9... | collective-permute-start | bytes 98312 | tf_op jit(solution)/shard_map/ppermute | solution.py:596
  16.3 0.0 copy-done.3
  16.3 1.0 shard_map.104
  17.3 14.4 %all-to-all-start = ((f32[32,8,128]{2,1,0:T(8,128)}), f32[32,8,128]{2,1,0:T(8,128)S(1)}, u32[]{:S(2)}, u32[]{:S(2)}) async-start(f32[32,8,128]{2,1,0:T(8,128)} %shard_map.104), calls=%async_computation | async-start | bytes 262144 | tf_op jit(solution)/shard_map/all_to_all | solution.py:601
  31.7 0.0 collective-permute-done.ylo_ref
  31.7 0.0 collective-permute-done.1.yhi_ref
  31.7 0.0 copy-start.2
  31.8 0.0 copy-start.8
  31.8 0.1 shard_map.106
  31.9 0.0 copy-start.5
  31.9 2.3 %collective-permute-start.3 = (f32[32,128]{1,0:T(8,128)S(1)}, f32[32,128]{1,0:T(8,128)S(1)}, u32[]{:S(2)}, u32[]{:S(2)}) collective-permute-start(f32[32,128]{1,0:T(8,128)S(1)} %get-tuple-element.20.after_ref), channel_id=1, source_target_pairs={{0,496},{16,0},{32,16},{48,32},{64,48},{80,64},{96,80},{112,96},{1... | collective-permute-start | bytes 49160 | tf_op jit(solution)/shard_map/ppermute | solution.py:596
  34.2 3.4 %collective-permute-start.2 = (f32[32,128]{1,0:T(8,128)S(1)}, f32[32,128]{1,0:T(8,128)S(1)}, u32[]{:S(2)}, u32[]{:S(2)}) collective-permute-start(f32[32,128]{1,0:T(8,128)S(1)} %get-tuple-element.21.also_ref), channel_id=1, source_target_pairs={{0,16},{16,32},{32,48},{48,64},{64,80},{80,96},{96,112},{112,128},... | collective-permute-start | bytes 49160 | tf_op jit(solution)/shard_map/ppermute | solution.py:595
  37.6 1.6 %shard_map.108 = (f32[2,8,512]{2,1,0:T(8,128)S(1)}, f32[3,2,2,8,512]{4,3,2,1,0:T(8,128)S(1)}) custom-call(f32[7,4,1,16,128]{4,3,2,1,0:T(8,128)S(1)} %copy-done.8, f32[6,2,3,4,1,16,128]{6,5,4,3,2,1,0:T(8,128)S(1)} %copy-done.2), custom_call_target="tpu_custom_call" | custom-call | tf_op jit(solution)/shard_map/pallas_call | solution.py:521
  39.2 5.5 %all-to-all-done.in_ref = f32[32,8,128]{2,1,0:T(8,128)S(1)} async-done(((f32[32,8,128]{2,1,0:T(8,128)}), f32[32,8,128]{2,1,0:T(8,128)S(1)}, u32[]{:S(2)}, u32[]{:S(2)}) %all-to-all-start) | async-done | bytes 131104 | tf_op jit(solution)/shard_map/all_to_all | solution.py:601
  44.7 1.4 %shard_map.107 = f32[512,128]{1,0:T(8,128)} custom-call(f32[32,8,128]{2,1,0:T(8,128)S(1)} %all-to-all-done.in_ref, f32[352,256]{1,0:T(8,128)S(1)} %copy-done.5, f32[32,128]{1,0:T(8,128)S(1)} %get-tuple-element.20.after_ref, f32[32,128]{1,0:T(8,128)S(1)} %get-tuple-element.21.also_ref), custom_call_target="tpu_custom_call" | custom-call | tf_op jit(solution)/shard_map/pallas_call | solution.py:521
  46.1 13.6 %all-to-all-start.1 = ((f32[512,1,128]{2,1,0:T(1,128)}), f32[512,1,128]{2,1,0:T(1,128)S(1)}, u32[]{:S(2)}, u32[]{:S(2)}) async-start(f32[512,1,128]{2,1,0:T(1,128)} %bitcast.1), calls=%async_computation.1 | async-start | bytes 524288 | tf_op jit(solution)/shard_map/all_to_all | solution.py:606
  59.7 0.0 collective-permute-done.3.xhi_ref
  59.7 0.0 collective-permute-done.2.xlo_ref
  59.7 0.0 copy-start.6
  59.7 0.3 shard_map.109
  60.0 0.0 copy-start.7
  60.0 16.9 %all-to-all-done.1 = f32[512,1,128]{2,1,0:T(1,128)S(1)} async-done(((f32[512,1,128]{2,1,0:T(1,128)}), f32[512,1,128]{2,1,0:T(1,128)S(1)}, u32[]{:S(2)}, u32[]{:S(2)}) %all-to-all-start.1) | async-done | bytes 262176 | tf_op jit(solution)/shard_map/all_to_all | solution.py:606
  76.9 1.1 shard_map.110
  78.0 26.0 %all_to_all.20 = f32[512,1,128]{2,1,0:T(1,128)S(1)} all-to-all(f32[512,1,128]{2,1,0:T(1,128)S(1)} %bitcast.9), channel_id=1, replica_groups=mesh['bx'=32,'by'=16] {'by','bx'}, dimensions={0} | all-to-all | bytes 524288 | tf_op jit(solution)/shard_map/all_to_all | solution.py:606
  104.0 0.8 shard_map.111
  104.8 17.3 %all_to_all.21.in_ref = f32[32,8,128]{2,1,0:T(8,128)S(1)} all-to-all(f32[32,8,128]{2,1,0:T(8,128)S(1)} %shard_map.111), channel_id=1, replica_groups=mesh['bx'=32,'by'=16] {'bx'}, dimensions={0} | all-to-all | bytes 262144 | tf_op jit(solution)/shard_map/all_to_all | solution.py:601
  122.2 1.8 %shard_map.112 = (f32[3,4,64,128]{3,2,1,0:T(8,128)}, f32[6,4,64,128]{3,2,1,0:T(8,128)}) custom-call(f32[32,8,128]{2,1,0:T(8,128)S(1)} %all_to_all.21.in_ref, f32[3,4,64,128]{3,2,1,0:T(8,128)S(1)} %get-tuple-element.27.before_ref, f32[6,4,64,128]{3,2,1,0:T(8,128)S(1)} %copy-done.1, f32[4,64,128]{2,1,0:T(8,128)S(1)} %copy-done.9, f32[3,64,128]{2,1,0:T(8,128)S(1)} %copy-done.3, ...), custom_call_target="tpu_custom_call" | custom-call | tf_op jit(solution)/shard_map/pallas_call | solution.py:521
  (11 shorter events, 0.0 us)
Async XLA Ops:
  0.6 1.1 copy-start
  1.8 1.0 copy-start.4
  2.8 13.5 %copy-start.3 = (f32[3,64,128]{2,1,0:T(8,128)S(1)}, f32[3,64,128]{2,1,0:T(8,128)}, u32[]{:S(2)}) copy-start(f32[3,64,128]{2,1,0:T(8,128)} %iv_ref.3) | copy-start | bytes 294916
  3.7 28.0 %collective-permute-start = (f32[64,128]{1,0:T(8,128)S(1)}, f32[64,128]{1,0:T(8,128)S(1)}, u32[]{:S(2)}, u32[]{:S(2)}) collective-permute-start(f32[64,128]{1,0:T(8,128)S(1)} %get-tuple-element.18.own_yhi_ref), channel_id=1, source_target_pairs={{0,1},{1,2},{2,3},{3,4},{4,5},{5,6},{6,7},{7,8},{8,9},{9,10},{10,1... | collective-permute-start | bytes 98312 | tf_op jit(solution)/shard_map/ppermute | solution.py:595
  8.5 23.2 %collective-permute-start.1 = (f32[64,128]{1,0:T(8,128)S(1)}, f32[64,128]{1,0:T(8,128)S(1)}, u32[]{:S(2)}, u32[]{:S(2)}) collective-permute-start(f32[64,128]{1,0:T(8,128)S(1)} %get-tuple-element.19.own_ylo_ref), channel_id=1, source_target_pairs={{0,15},{1,0},{2,1},{3,2},{4,3},{5,4},{6,5},{7,6},{8,7},{9,8},{10,9... | collective-permute-start | bytes 98312 | tf_op jit(solution)/shard_map/ppermute | solution.py:596
  17.3 27.4 %all-to-all-start = ((f32[32,8,128]{2,1,0:T(8,128)}), f32[32,8,128]{2,1,0:T(8,128)S(1)}, u32[]{:S(2)}, u32[]{:S(2)}) async-start(f32[32,8,128]{2,1,0:T(8,128)} %shard_map.104), calls=%async_computation | async-start | bytes 262144 | tf_op jit(solution)/shard_map/all_to_all | solution.py:601
  31.7 5.9 %copy-start.2 = (f32[6,2,3,4,1,16,128]{6,5,4,3,2,1,0:T(8,128)S(1)}, f32[6,2,3,4,1,16,128]{6,5,4,3,2,1,0:T(8,128)}, u32[]{:S(2)}) copy-start(f32[6,2,3,4,1,16,128]{6,5,4,3,2,1,0:T(8,128)} %history_hbm.1) | copy-start | bytes 3538948
  31.8 5.9 %copy-start.8 = (f32[7,4,1,16,128]{4,3,2,1,0:T(8,128)S(1)}, f32[7,4,1,16,128]{4,3,2,1,0:T(8,128)}, u32[]{:S(2)}) copy-start(f32[7,4,1,16,128]{4,3,2,1,0:T(8,128)} %kernel_hbm.1) | copy-start | bytes 688132
  31.9 12.8 %copy-start.5 = (f32[352,256]{1,0:T(8,128)S(1)}, f32[352,256]{1,0:T(8,128)}, u32[]{:S(2)}) copy-start(f32[352,256]{1,0:T(8,128)} %constant.6.clone.table_ref) | copy-start | bytes 1081348
  31.9 27.8 %collective-permute-start.3 = (f32[32,128]{1,0:T(8,128)S(1)}, f32[32,128]{1,0:T(8,128)S(1)}, u32[]{:S(2)}, u32[]{:S(2)}) collective-permute-start(f32[32,128]{1,0:T(8,128)S(1)} %get-tuple-element.20.after_ref), channel_id=1, source_target_pairs={{0,496},{16,0},{32,16},{48,32},{64,48},{80,64},{96,80},{112,96},{1... | collective-permute-start | bytes 49160 | tf_op jit(solution)/shard_map/ppermute | solution.py:596
  34.2 25.5 %collective-permute-start.2 = (f32[32,128]{1,0:T(8,128)S(1)}, f32[32,128]{1,0:T(8,128)S(1)}, u32[]{:S(2)}, u32[]{:S(2)}) collective-permute-start(f32[32,128]{1,0:T(8,128)S(1)} %get-tuple-element.21.also_ref), channel_id=1, source_target_pairs={{0,16},{16,32},{32,48},{48,64},{64,80},{80,96},{96,112},{112,128},... | collective-permute-start | bytes 49160 | tf_op jit(solution)/shard_map/ppermute | solution.py:595
  46.1 30.8 %all-to-all-start.1 = ((f32[512,1,128]{2,1,0:T(1,128)}), f32[512,1,128]{2,1,0:T(1,128)S(1)}, u32[]{:S(2)}, u32[]{:S(2)}) async-start(f32[512,1,128]{2,1,0:T(1,128)} %bitcast.1), calls=%async_computation.1 | async-start | bytes 524288 | tf_op jit(solution)/shard_map/all_to_all | solution.py:606
  59.7 17.2 %copy-start.6 = (f32[328,256]{1,0:T(8,128)S(1)}, f32[328,256]{1,0:T(8,128)}, u32[]{:S(2)}) copy-start(f32[328,256]{1,0:T(8,128)} %constant.7.clone.table_ref) | copy-start | bytes 1007620
  60.0 44.0 %copy-start.7 = (f32[320,256]{1,0:T(8,128)S(1)}, f32[320,256]{1,0:T(8,128)}, u32[]{:S(2)}) copy-start(f32[320,256]{1,0:T(8,128)} %constant.8.clone.table_ref) | copy-start | bytes 983044
  76.9 45.3 %copy-start.1 = (f32[6,4,64,128]{3,2,1,0:T(8,128)S(1)}, f32[6,4,64,128]{3,2,1,0:T(8,128)}, u32[]{:S(2)}) copy-start(f32[6,4,64,128]{3,2,1,0:T(8,128)} %stress_ref.3) | copy-start | bytes 2359300
  76.9 45.3 %copy-start.9 = (f32[4,64,128]{2,1,0:T(8,128)S(1)}, f32[4,64,128]{2,1,0:T(8,128)}, u32[]{:S(2)}) copy-start(f32[4,64,128]{2,1,0:T(8,128)} %cohesion_ref.1) | copy-start | bytes 393220

commit v6 on v4

--- a/solution.py
+++ b/solution.py
@@ -162,7 +162,7 @@
     out_ref[:, 7, :] = zero
 
 
-def strike_forward_kernel(in_ref, table_ref, after_ref, also_ref, out_ref):
+def strike_forward_kernel(in_ref, table_ref, out_ref):
     value = jnp.concatenate([in_ref[:, m, :] for m in range(6)], axis=1)
     value = stacked_dot(table_ref[288:352, 0:32], value)
     cos, sin = table_ref[256:288, 0:128], table_ref[256:288, 128:256]
@@ -182,7 +182,7 @@
             out_ref[32 * (8 * t + b) : 32 * (8 * t + b + 1), :] = parts[b]
 
 
-def strike_inverse_kernel(in_ref, table_ref, out_ref):
+def strike_inverse_kernel(in_ref, table_ref, after_ref, also_ref, out_ref):
     columns = []
     for t in range(2):
         columns.append(
@@ -362,7 +362,9 @@
     return total
 
 
-def part_kernel(velocity_ref, stress_ref, part_ref, ylo_ref, yhi_ref, xlo_ref, xhi_ref):
+def part_kernel(
+    velocity_ref, stress_ref, after_ref, part_ref, ylo_ref, yhi_ref, xlo_ref, xhi_ref
+):
     row, lane = row_of((64, 128)), lane_of((64, 128))
     for n in range(3):
         for z in range(4):
@@ -385,7 +387,7 @@
         ref[...] = jnp.concatenate(rows + [pad], axis=0)
 
 
-def column_kernel(low_ref, high_ref, ylo_ref, yhi_ref, out_low_ref, out_high_ref):
+def column_kernel(low_ref, high_ref, ylo_ref, yhi_ref, after_ref, out_low_ref, out_high_ref):
     lane, row = lane_of((32, 128)), row_of((32, 128))
     for at, ref, out_ref in ((0, low_ref, out_low_ref), (63, high_ref, out_high_ref)):
         low = jnp.broadcast_to(ylo_ref[at : at + 1, :], (32, 128))
@@ -532,13 +534,13 @@
     return call(scatter_kernel, f32(32, 8, 128), (iv,), scratch=scratch)
 
 
-def strike_forward(arrived, after):
-    arguments = (arrived, strike_tables(False))
-    return call(strike_forward_kernel, f32(512, 128), arguments, after)
-
-
-def strike_inverse(arrived):
-    return call(strike_inverse_kernel, f32(32, 8, 128), (arrived, strike_tables(True)))
+def strike_forward(arrived):
+    return call(strike_forward_kernel, f32(512, 128), (arrived, strike_tables(False)))
+
+
+def strike_inverse(arrived, after):
+    arguments = (arrived, strike_tables(True))
+    return call(strike_inverse_kernel, f32(32, 8, 128), arguments, after)
 
 
 def dip(arrived, weight, past, after):
@@ -560,13 +562,14 @@
     )
 
 
-def velocity_part(velocity, stress):
+def velocity_part(velocity, stress, after):
     columns, rows = (f32(64, 128),) * 2, (f32(32, 128),) * 2
-    return call(part_kernel, (f32(3, 4, 64, 128), *columns, *rows), (velocity, stress))
-
-
-def velocity_columns(edges, halo):
-    return call(column_kernel, (f32(32, 128),) * 2, (*edges, *halo))
+    outs = (f32(3, 4, 64, 128), *columns, *rows)
+    return call(part_kernel, outs, (velocity, stress), (after,))
+
+
+def velocity_columns(edges, halo, after):
+    return call(column_kernel, (f32(32, 128),) * 2, (*edges, *halo), (after,))
 
 
 def velocity_rows(part, halo, own, after):
@@ -607,17 +610,18 @@
 
 def local(interface_velocity, history, kernel, velocity, stress, cohesion):
     arrived = strike_swap(scatter(interface_velocity))
-    part, *edges = velocity_part(velocity, stress)
+    sent = strike_forward(arrived)
+    arrived = whole_swap(sent)
+    part, *edges = velocity_part(velocity, stress, sent)
     own_columns, own_rows = edges[:2], edges[2:]
     columns = exchange("by", *own_columns)
-    sent = strike_forward(arrived, columns)
-    rows = exchange("bx", *velocity_columns(own_rows, columns))
+    weight, past = past_terms(kernel, history)
+    sent = dip(arrived, weight, past, columns)
     arrived = whole_swap(sent)
-    weight, past = past_terms(kernel, history)
-    sent = dip(arrived, weight, past, rows)
+    rows = exchange("bx", *velocity_columns(own_rows, columns, sent))
+    sent = strike_inverse(arrived, rows)
+    arrived = strike_swap(sent)
     before, *halo = velocity_rows(part, (*rows, *columns), (*own_rows, *own_columns), sent)
-    arrived = whole_swap(sent)
-    arrived = strike_swap(strike_inverse(arrived))
     return slab(arrived, before, stress, cohesion, interface_velocity, halo)
 
 

time: 124 us -> 124 us (level)
  starting transfers between devices: 57.9 us -> 54.6 us
  waiting for transfers between devices: 21 us -> 24 us
  blocking collectives: 31.3 us -> 30 us
  local copies, waits for them, and re-layouts: 3.05 us -> 4.31 us
    all_to_all x2 -> x1, starting transfers between devices: 21.8 us -> 9.44 us  [strike_swap(): return lax.all_to_all(value, 'bx', split_axis=0, concat_axis=0, tiled=True)]
    all_to_all x1 -> x2, starting transfers between devices: 18.8 us -> 26.4 us  [whole_swap(): lax.all_to_all(value, ('by', 'bx'), split_axis=0, concat_axis=0, tiled=True)]
    all_to_all x1 -> x2, waiting for transfers between devices: 7.31 us -> 10.5 us  [whole_swap(): lax.all_to_all(value, ('by', 'bx'), split_axis=0, concat_axis=0, tiled=True)]
    all_to_all x1, blocking collectives: 31.3 us -> 30 us  [strike_swap(): return lax.all_to_all(value, 'bx', split_axis=0, concat_axis=0, tiled=True)]
    unnamed x22 -> x40, local copies, waits for them, and re-layouts: 3.05 us -> 4.31 us
    all_to_all x2 -> x1, waiting for transfers between devices: 12.7 us -> 12.7 us  [strike_swap(): return lax.all_to_all(value, 'bx', split_axis=0, concat_axis=0, tiled=True)]
  transfers between devices with their start and end apart: 7 -> 7, of which waited for: 3 -> 4; matrix products, arithmetic and copies ran while one was open for 0% -> 0% of each run, Pallas kernels for 2% -> 2%
where the time goes in v6:
time: 124 us; the launch traced here: 123 us
  starting transfers between devices  54.6 us (44%)
  blocking collectives  30 us (24%)
  waiting for transfers between devices  24 us (19%)
  Pallas kernels  9.68 us (8%)
  local copies, waits for them, and re-layouts  4.31 us (3%)
    all_to_all x1, blocking collectives, strike_swap(): return lax.all_to_all(value, 'bx', split_axis=0, concat_axis=0, tiled=True)  30 us
    all_to_all x2, starting transfers between devices, whole_swap(): lax.all_to_all(value, ('by', 'bx'), split_axis=0, concat_axis=0, tiled=True)  26.4 us
    all_to_all x1, waiting for transfers between devices, strike_swap(): return lax.all_to_all(value, 'bx', split_axis=0, concat_axis=0, tiled=True)  12.7 us
    ppermute x2, starting transfers between devices, exchange(): lax.ppermute(low, axis, [(i, (i - 1) % count) for i in range(count)])  11.5 us
    all_to_all x2, waiting for transfers between devices, whole_swap(): lax.all_to_all(value, ('by', 'bx'), split_axis=0, concat_axis=0, tiled=True)  10.5 us
    pallas_call x9, Pallas kernels, call(): pl.pallas_call(kernel, out_shape=out_shape, in_specs=[VMEM] * len(argumen...  9.68 us
    all_to_all x1, starting transfers between devices, strike_swap(): return lax.all_to_all(value, 'bx', split_axis=0, concat_axis=0, tiled=True)  9.44 us
    ppermute x2, starting transfers between devices, exchange(): lax.ppermute(high, axis, [(i, (i + 1) % count) for i in range(count)])  7.23 us
  transfers between devices with their start and end apart: 7, of which 4 were waited for; matrix products, arithmetic and copies ran while one was open for 0% of the time, Pallas kernels for 2%

profile of v6, /device:TPU:1, one launch (start us, length us, event | category | flops | bytes accessed | tf_op | source)
XLA Modules:
  0.0 123.4 jit_solution(8767741497888313046)
XLA Ops:
  0.6 0.0 copy-start.2
  0.7 1.0 copy-done.2
  1.6 0.4 shard_map.104
  2.0 30.0 %all_to_all.20.in_ref = f32[32,8,128]{2,1,0:T(8,128)S(1)} all-to-all(f32[32,8,128]{2,1,0:T(8,128)S(1)} %shard_map.104), channel_id=1, replica_groups=mesh['bx'=32,'by'=16] {'bx'}, dimensions={0} | all-to-all | bytes 262144 | tf_op jit(solution)/shard_map/all_to_all | solution.py:602
  32.0 1.0 copy-done.5
  33.0 1.4 %shard_map.105.after_ref = f32[512,128]{1,0:T(8,128)} custom-call(f32[32,8,128]{2,1,0:T(8,128)S(1)} %all_to_all.20.in_ref, f32[352,256]{1,0:T(8,128)S(1)} %copy-done.5), custom_call_target="tpu_custom_call" | custom-call | tf_op jit(solution)/shard_map/pallas_call | solution.py:522
  34.3 11.4 %all-to-all-start.1 = ((f32[512,1,128]{2,1,0:T(1,128)}), f32[512,1,128]{2,1,0:T(1,128)S(1)}, u32[]{:S(2)}, u32[]{:S(2)}) async-start(f32[512,1,128]{2,1,0:T(1,128)} %bitcast.1), calls=%async_computation.1 | async-start | bytes 524288 | tf_op jit(solution)/shard_map/all_to_all | solution.py:607
  45.7 0.0 copy-start.6
  45.7 0.9 shard_map.107
  46.7 3.7 %collective-permute-start = (f32[64,128]{1,0:T(8,128)S(1)}, f32[64,128]{1,0:T(8,128)S(1)}, u32[]{:S(2)}, u32[]{:S(2)}) collective-permute-start(f32[64,128]{1,0:T(8,128)S(1)} %get-tuple-element.18.own_yhi_ref), channel_id=1, source_target_pairs={{0,1},{1,2},{2,3},{3,4},{4,5},{5,6},{6,7},{7,8},{8,9},{9,10},{10,1... | collective-permute-start | bytes 98312 | tf_op jit(solution)/shard_map/ppermute | solution.py:596
  50.4 7.0 %collective-permute-start.1 = (f32[64,128]{1,0:T(8,128)S(1)}, f32[64,128]{1,0:T(8,128)S(1)}, u32[]{:S(2)}, u32[]{:S(2)}) collective-permute-start(f32[64,128]{1,0:T(8,128)S(1)} %get-tuple-element.19.own_ylo_ref), channel_id=1, source_target_pairs={{0,15},{1,0},{2,1},{3,2},{4,3},{5,4},{6,5},{7,6},{8,7},{9,8},{10,9... | collective-permute-start | bytes 98312 | tf_op jit(solution)/shard_map/ppermute | solution.py:597
  57.4 0.0 copy-start.8
  57.4 0.9 copy-done.8
  58.3 1.5 %shard_map.106 = (f32[2,8,512]{2,1,0:T(8,128)S(1)}, f32[3,2,2,8,512]{4,3,2,1,0:T(8,128)S(1)}) custom-call(f32[7,4,1,16,128]{4,3,2,1,0:T(8,128)S(1)} %copy-done.8, f32[6,2,3,4,1,16,128]{6,5,4,3,2,1,0:T(8,128)S(1)} %copy-done.1), custom_call_target="tpu_custom_call" | custom-call | tf_op jit(solution)/shard_map/pallas_call | solution.py:522
  59.9 0.0 copy-start.18
  59.9 0.6 copy-done.18
  60.5 2.4 %all-to-all-done.1 = f32[512,1,128]{2,1,0:T(1,128)S(1)} async-done(((f32[512,1,128]{2,1,0:T(1,128)}), f32[512,1,128]{2,1,0:T(1,128)S(1)}, u32[]{:S(2)}, u32[]{:S(2)}) %all-to-all-start.1) | async-done | bytes 262176 | tf_op jit(solution)/shard_map/all_to_all | solution.py:607
  62.9 0.8 copy-done.19
  63.7 1.8 %shard_map.108.after_ref = f32[512,128]{1,0:T(8,128)} custom-call(f32[512,128]{1,0:T(8,128)S(1)} %bitcast.9, f32[2,8,512]{2,1,0:T(8,128)S(1)} %copy-done.19, f32[3,2,2,8,512]{4,3,2,1,0:T(8,128)S(1)} %get-tuple-element.17.past_ref, f32[328,256]{1,0:T(8,128)S(1)} %copy-done.6, f32[64,128]{1,0:T(8,128)S(1)} %collective-permute-done.after_ref.ylo_ref, ...), custom_call_target="tpu_custom_call" | custom-call | tf_op jit(solution)/shard_map/pallas_call | solution.py:522
  65.5 15.0 %all-to-all-start.2 = ((f32[512,1,128]{2,1,0:T(1,128)}), f32[512,1,128]{2,1,0:T(1,128)S(1)}, u32[]{:S(2)}, u32[]{:S(2)}) async-start(f32[512,1,128]{2,1,0:T(1,128)} %bitcast.4), calls=%async_computation.2 | async-start | bytes 524288 | tf_op jit(solution)/shard_map/all_to_all | solution.py:607
  80.6 0.0 copy-start.3
  80.6 0.0 copy-start.9
  80.6 0.1 shard_map.109
  80.7 3.5 %collective-permute-start.2 = (f32[32,128]{1,0:T(8,128)S(1)}, f32[32,128]{1,0:T(8,128)S(1)}, u32[]{:S(2)}, u32[]{:S(2)}) collective-permute-start(f32[32,128]{1,0:T(8,128)S(1)} %get-tuple-element.22), channel_id=1, source_target_pairs={{0,16},{16,32},{32,48},{48,64},{64,80},{80,96},{96,112},{112,128},... | collective-permute-start | bytes 49160 | tf_op jit(solution)/shard_map/ppermute | solution.py:596
  84.3 4.6 %collective-permute-start.3 = (f32[32,128]{1,0:T(8,128)S(1)}, f32[32,128]{1,0:T(8,128)S(1)}, u32[]{:S(2)}, u32[]{:S(2)}) collective-permute-start(f32[32,128]{1,0:T(8,128)S(1)} %get-tuple-element.23), channel_id=1, source_target_pairs={{0,496},{16,0},{32,16},{48,32},{64,48},{80,64},{96,80},{112,96},{1... | collective-permute-start | bytes 49160 | tf_op jit(solution)/shard_map/ppermute | solution.py:597
  88.9 0.8 collective-permute-done.3.also_ref.xhi_ref
  89.7 8.1 %all-to-all-done.2 = f32[512,1,128]{2,1,0:T(1,128)S(1)} async-done(((f32[512,1,128]{2,1,0:T(1,128)}), f32[512,1,128]{2,1,0:T(1,128)S(1)}, u32[]{:S(2)}, u32[]{:S(2)}) %all-to-all-start.2) | async-done | bytes 262176 | tf_op jit(solution)/shard_map/all_to_all | solution.py:607
  97.8 1.5 %shard_map.110.after_ref = f32[32,8,128]{2,1,0:T(8,128)} custom-call(f32[512,128]{1,0:T(8,128)S(1)} %bitcast.8, f32[320,256]{1,0:T(8,128)S(1)} %copy-done.7, f32[32,128]{1,0:T(8,128)S(1)} %collective-permute-done.2.after_ref.xlo_ref, f32[32,128]{1,0:T(8,128)S(1)} %collective-permute-done.3.also_ref.xhi_ref), custom_call_target="tpu_custom_call" | custom-call | tf_op jit(solution)/shard_map/pallas_call | solution.py:522
  99.2 9.4 %all-to-all-start.3 = ((f32[32,8,128]{2,1,0:T(8,128)}), f32[32,8,128]{2,1,0:T(8,128)S(1)}, u32[]{:S(2)}, u32[]{:S(2)}) async-start(f32[32,8,128]{2,1,0:T(8,128)} %shard_map.110.after_ref), calls=%async_computation.3 | async-start | bytes 262144 | tf_op jit(solution)/shard_map/all_to_all | solution.py:602
  108.7 0.3 shard_map.111
  109.0 12.7 %all-to-all-done.3.in_ref = f32[32,8,128]{2,1,0:T(8,128)S(1)} async-done(((f32[32,8,128]{2,1,0:T(8,128)}), f32[32,8,128]{2,1,0:T(8,128)S(1)}, u32[]{:S(2)}, u32[]{:S(2)}) %all-to-all-start.3) | async-done | bytes 131104 | tf_op jit(solution)/shard_map/all_to_all | solution.py:602
  121.7 1.8 %shard_map.112 = (f32[3,4,64,128]{3,2,1,0:T(8,128)}, f32[6,4,64,128]{3,2,1,0:T(8,128)}) custom-call(f32[32,8,128]{2,1,0:T(8,128)S(1)} %all-to-all-done.3.in_ref, f32[3,4,64,128]{3,2,1,0:T(8,128)S(1)} %get-tuple-element.25.before_ref, f32[6,4,64,128]{3,2,1,0:T(8,128)S(1)} %copy-done, f32[4,64,128]{2,1,0:T(8,128)S(1)} %copy-done.9, ...), custom_call_target="tpu_custom_call" | custom-call | tf_op jit(solution)/shard_map/pallas_call | solution.py:522
  (32 shorter events, 0.1 us)
Async XLA Ops:
  0.6 45.1 %copy-start = (f32[6,4,64,128]{3,2,1,0:T(8,128)S(1)}, f32[6,4,64,128]{3,2,1,0:T(8,128)}, u32[]{:S(2)}) copy-start(f32[6,4,64,128]{3,2,1,0:T(8,128)} %stress_ref.3) | copy-start | bytes 2359300
  0.6 1.0 copy-start.2
  1.6 44.1 %copy-start.4 = (f32[3,4,64,128]{3,2,1,0:T(8,128)S(1)}, f32[3,4,64,128]{3,2,1,0:T(8,128)}, u32[]{:S(2)}) copy-start(f32[3,4,64,128]{3,2,1,0:T(8,128)} %velocity_ref.1) | copy-start | bytes 1179652
  32.0 1.0 copy-start.5
  33.0 24.4 %copy-start.1 = (f32[6,2,3,4,1,16,128]{6,5,4,3,2,1,0:T(8,128)S(1)}, f32[6,2,3,4,1,16,128]{6,5,4,3,2,1,0:T(8,128)}, u32[]{:S(2)}) copy-start(f32[6,2,3,4,1,16,128]{6,5,4,3,2,1,0:T(8,128)} %history_hbm.1) | copy-start | bytes 3538948
  34.3 28.6 %all-to-all-start.1 = ((f32[512,1,128]{2,1,0:T(1,128)}), f32[512,1,128]{2,1,0:T(1,128)S(1)}, u32[]{:S(2)}, u32[]{:S(2)}) async-start(f32[512,1,128]{2,1,0:T(1,128)} %bitcast.1), calls=%async_computation.1 | async-start | bytes 524288 | tf_op jit(solution)/shard_map/all_to_all | solution.py:607
  45.7 17.2 %copy-start.6 = (f32[328,256]{1,0:T(8,128)S(1)}, f32[328,256]{1,0:T(8,128)}, u32[]{:S(2)}) copy-start(f32[328,256]{1,0:T(8,128)} %constant.7.clone.table_ref) | copy-start | bytes 1007620
  46.7 13.8 %copy-start.10 = (f32[32,128]{1,0:T(8,128)}, f32[32,128]{1,0:T(8,128)S(1)}, u32[]{:S(2)}) copy-start(f32[32,128]{1,0:T(8,128)S(1)} %get-tuple-element.20.low_ref.own_xlo_ref) | copy-start | bytes 49156
  46.7 13.8 %copy-start.12 = (f32[32,128]{1,0:T(8,128)}, f32[32,128]{1,0:T(8,128)S(1)}, u32[]{:S(2)}) copy-start(f32[32,128]{1,0:T(8,128)S(1)} %get-tuple-element.21.high_ref.own_xhi_ref) | copy-start | bytes 49156
  46.7 13.8 %copy-start.14 = (f32[64,128]{1,0:T(8,128)}, f32[64,128]{1,0:T(8,128)S(1)}, u32[]{:S(2)}) copy-start(f32[64,128]{1,0:T(8,128)S(1)} %get-tuple-element.19.own_ylo_ref) | copy-start | bytes 98308
  46.7 13.8 %copy-start.16 = (f32[64,128]{1,0:T(8,128)}, f32[64,128]{1,0:T(8,128)S(1)}, u32[]{:S(2)}) copy-start(f32[64,128]{1,0:T(8,128)S(1)} %get-tuple-element.18.own_yhi_ref) | copy-start | bytes 98308
  46.7 13.8 %collective-permute-start = (f32[64,128]{1,0:T(8,128)S(1)}, f32[64,128]{1,0:T(8,128)S(1)}, u32[]{:S(2)}, u32[]{:S(2)}) collective-permute-start(f32[64,128]{1,0:T(8,128)S(1)} %get-tuple-element.18.own_yhi_ref), channel_id=1, source_target_pairs={{0,1},{1,2},{2,3},{3,4},{4,5},{5,6},{6,7},{7,8},{8,9},{9,10},{10,1... | collective-permute-start | bytes 98312 | tf_op jit(solution)/shard_map/ppermute | solution.py:596
  50.4 10.1 %collective-permute-start.1 = (f32[64,128]{1,0:T(8,128)S(1)}, f32[64,128]{1,0:T(8,128)S(1)}, u32[]{:S(2)}, u32[]{:S(2)}) collective-permute-start(f32[64,128]{1,0:T(8,128)S(1)} %get-tuple-element.19.own_ylo_ref), channel_id=1, source_target_pairs={{0,15},{1,0},{2,1},{3,2},{4,3},{5,4},{6,5},{7,6},{8,7},{9,8},{10,9... | collective-permute-start | bytes 98312 | tf_op jit(solution)/shard_map/ppermute | solution.py:597
  57.4 0.9 copy-start.8
  59.9 0.6 copy-start.18
  60.5 37.3 %copy-start.7 = (f32[320,256]{1,0:T(8,128)S(1)}, f32[320,256]{1,0:T(8,128)}, u32[]{:S(2)}) copy-start(f32[320,256]{1,0:T(8,128)} %constant.8.clone.table_ref) | copy-start | bytes 983044
  60.5 20.1 %copy-start.11 = (f32[32,128]{1,0:T(8,128)S(1)}, f32[32,128]{1,0:T(8,128)}, u32[]{:S(2)}) copy-start(f32[32,128]{1,0:T(8,128)} %copy-done.10) | copy-start | bytes 49156
  60.5 20.1 %copy-start.13 = (f32[32,128]{1,0:T(8,128)S(1)}, f32[32,128]{1,0:T(8,128)}, u32[]{:S(2)}) copy-start(f32[32,128]{1,0:T(8,128)} %copy-done.12) | copy-start | bytes 49156
  62.9 0.8 copy-start.19
  65.5 43.2 %copy-start.15 = (f32[64,128]{1,0:T(8,128)S(1)}, f32[64,128]{1,0:T(8,128)}, u32[]{:S(2)}) copy-start(f32[64,128]{1,0:T(8,128)} %copy-done.14) | copy-start | bytes 98308
  65.5 43.2 %copy-start.17 = (f32[64,128]{1,0:T(8,128)S(1)}, f32[64,128]{1,0:T(8,128)}, u32[]{:S(2)}) copy-start(f32[64,128]{1,0:T(8,128)} %copy-done.16) | copy-start | bytes 98308
  65.5 32.2 %all-to-all-start.2 = ((f32[512,1,128]{2,1,0:T(1,128)}), f32[512,1,128]{2,1,0:T(1,128)S(1)}, u32[]{:S(2)}, u32[]{:S(2)}) async-start(f32[512,1,128]{2,1,0:T(1,128)} %bitcast.4), calls=%async_computation.2 | async-start | bytes 524288 | tf_op jit(solution)/shard_map/all_to_all | solution.py:607
  80.6 41.1 %copy-start.3 = (f32[3,64,128]{2,1,0:T(8,128)S(1)}, f32[3,64,128]{2,1,0:T(8,128)}, u32[]{:S(2)}) copy-start(f32[3,64,128]{2,1,0:T(8,128)} %iv_ref.3) | copy-start | bytes 294916
  80.6 41.1 %copy-start.9 = (f32[4,64,128]{2,1,0:T(8,128)S(1)}, f32[4,64,128]{2,1,0:T(8,128)}, u32[]{:S(2)}) copy-start(f32[4,64,128]{2,1,0:T(8,128)} %cohesion_ref.1) | copy-start | bytes 393220
  80.7 8.1 %collective-permute-start.2 = (f32[32,128]{1,0:T(8,128)S(1)}, f32[32,128]{1,0:T(8,128)S(1)}, u32[]{:S(2)}, u32[]{:S(2)}) collective-permute-start(f32[32,128]{1,0:T(8,128)S(1)} %get-tuple-element.22), channel_id=1, source_target_pairs={{0,16},{16,32},{32,48},{48,64},{64,80},{80,96},{96,112},{112,128},... | collective-permute-start | bytes 49160 | tf_op jit(solution)/shard_map/ppermute | solution.py:596
  84.3 5.4 %collective-permute-start.3 = (f32[32,128]{1,0:T(8,128)S(1)}, f32[32,128]{1,0:T(8,128)S(1)}, u32[]{:S(2)}, u32[]{:S(2)}) collective-permute-start(f32[32,128]{1,0:T(8,128)S(1)} %get-tuple-element.23), channel_id=1, source_target_pairs={{0,496},{16,0},{32,16},{48,32},{64,48},{80,64},{96,80},{112,96},{1... | collective-permute-start | bytes 49160 | tf_op jit(solution)/shard_map/ppermute | solution.py:597
  99.2 22.4 %all-to-all-start.3 = ((f32[32,8,128]{2,1,0:T(8,128)}), f32[32,8,128]{2,1,0:T(8,128)S(1)}, u32[]{:S(2)}, u32[]{:S(2)}) async-start(f32[32,8,128]{2,1,0:T(8,128)} %shard_map.110.after_ref), calls=%async_computation.3 | async-start | bytes 262144 | tf_op jit(solution)/shard_map/all_to_all | solution.py:602

commit v7 on v6

--- a/solution.py
+++ b/solution.py
@@ -162,7 +162,7 @@
     out_ref[:, 7, :] = zero
 
 
-def strike_forward_kernel(in_ref, table_ref, out_ref):
+def strike_forward_kernel(in_ref, table_ref, after_ref, also_ref, out_ref):
     value = jnp.concatenate([in_ref[:, m, :] for m in range(6)], axis=1)
     value = stacked_dot(table_ref[288:352, 0:32], value)
     cos, sin = table_ref[256:288, 0:128], table_ref[256:288, 128:256]
@@ -534,8 +534,9 @@
     return call(scatter_kernel, f32(32, 8, 128), (iv,), scratch=scratch)
 
 
-def strike_forward(arrived):
-    return call(strike_forward_kernel, f32(512, 128), (arrived, strike_tables(False)))
+def strike_forward(arrived, after):
+    arguments = (arrived, strike_tables(False))
+    return call(strike_forward_kernel, f32(512, 128), arguments, after)
 
 
 def strike_inverse(arrived, after):
@@ -610,12 +611,12 @@
 
 def local(interface_velocity, history, kernel, velocity, stress, cohesion):
     arrived = strike_swap(scatter(interface_velocity))
-    sent = strike_forward(arrived)
+    weight, past = past_terms(kernel, history)
+    sent = strike_forward(arrived, (weight, past))
     arrived = whole_swap(sent)
     part, *edges = velocity_part(velocity, stress, sent)
     own_columns, own_rows = edges[:2], edges[2:]
     columns = exchange("by", *own_columns)
-    weight, past = past_terms(kernel, history)
     sent = dip(arrived, weight, past, columns)
     arrived = whole_swap(sent)
     rows = exchange("bx", *velocity_columns(own_rows, columns, sent))

time: 124 us -> 123 us (level)
  blocking collectives: 30 us -> 0 us
  starting transfers between devices: 54.6 us -> 72 us
  waiting for transfers between devices: 24 us -> 36.3 us
    all_to_all x1 -> x0, blocking collectives: 30 us -> none  [strike_swap(): return lax.all_to_all(value, 'bx', split_axis=0, concat_axis=0, tiled=True)]
    all_to_all x1 -> x2, starting transfers between devices: 9.44 us -> 26.6 us  [strike_swap(): return lax.all_to_all(value, 'bx', split_axis=0, concat_axis=0, tiled=True)]
    all_to_all x1 -> x2, waiting for transfers between devices: 12.7 us -> 21.9 us  [strike_swap(): return lax.all_to_all(value, 'bx', split_axis=0, concat_axis=0, tiled=True)]
    all_to_all x2, waiting for transfers between devices: 10.5 us -> 12.6 us  [whole_swap(): lax.all_to_all(value, ('by', 'bx'), split_axis=0, concat_axis=0, tiled=True)]
    unnamed x40 -> x20, local copies, waits for them, and re-layouts: 4.31 us -> 3.13 us
  transfers between devices with their start and end apart: 7 -> 8, of which waited for: 4 -> 7; matrix products, arithmetic and copies ran while one was open for 0% -> 0% of each run, Pallas kernels for 2% -> 2%
where the time goes in v7:
time: 123 us
  starting transfers between devices  72 us (59%)
  waiting for transfers between devices  36.3 us (30%)
  Pallas kernels  10.4 us (8%)
  local copies, waits for them, and re-layouts  3.13 us (3%)
    all_to_all x2, starting transfers between devices, strike_swap(): return lax.all_to_all(value, 'bx', split_axis=0, concat_axis=0, tiled=True)  26.6 us
    all_to_all x2, starting transfers between devices, whole_swap(): lax.all_to_all(value, ('by', 'bx'), split_axis=0, concat_axis=0, tiled=True)  26.5 us
    all_to_all x2, waiting for transfers between devices, strike_swap(): return lax.all_to_all(value, 'bx', split_axis=0, concat_axis=0, tiled=True)  21.9 us
    all_to_all x2, waiting for transfers between devices, whole_swap(): lax.all_to_all(value, ('by', 'bx'), split_axis=0, concat_axis=0, tiled=True)  12.6 us
    ppermute x2, starting transfers between devices, exchange(): lax.ppermute(low, axis, [(i, (i - 1) % count) for i in range(count)])  11.5 us
    pallas_call x9, Pallas kernels, call(): pl.pallas_call(kernel, out_shape=out_shape, in_specs=[VMEM] * len(argumen...  10.4 us
    ppermute x2, starting transfers between devices, exchange(): lax.ppermute(high, axis, [(i, (i + 1) % count) for i in range(count)])  7.36 us
    unnamed x20, local copies, waits for them, and re-layouts  3.13 us
  transfers between devices with their start and end apart: 8, of which 7 were waited for; matrix products, arithmetic and copies ran while one was open for 0% of the time, Pallas kernels for 2%

profile of v7, /device:TPU:1, one launch (start us, length us, event | category | flops | bytes accessed | tf_op | source)
XLA Modules:
  0.0 122.5 jit_solution(15443837619998890596)
XLA Ops:
  0.6 0.0 copy-start.2
  0.6 0.9 copy-done.2
  1.5 1.0 shard_map.104
  2.6 17.2 %all-to-all-start = ((f32[32,8,128]{2,1,0:T(8,128)}), f32[32,8,128]{2,1,0:T(8,128)S(1)}, u32[]{:S(2)}, u32[]{:S(2)}) async-start(f32[32,8,128]{2,1,0:T(8,128)} %shard_map.104), calls=%async_computation | async-start | bytes 262144 | tf_op jit(solution)/shard_map/all_to_all | solution.py:603
  19.8 0.0 copy-start.1
  19.8 1.3 %copy-done.1 = f32[6,2,3,4,1,16,128]{6,5,4,3,2,1,0:T(8,128)S(1)} copy-done((f32[6,2,3,4,1,16,128]{6,5,4,3,2,1,0:T(8,128)S(1)}, f32[6,2,3,4,1,16,128]{6,5,4,3,2,1,0:T(8,128)}, u32[]{:S(2)}) %copy-start.1) | copy-done | bytes 1179672
  21.1 0.9 copy-done.8
  22.0 1.6 %shard_map.105 = (f32[2,8,512]{2,1,0:T(8,128)S(1)}, f32[3,2,2,8,512]{4,3,2,1,0:T(8,128)S(1)}) custom-call(f32[7,4,1,16,128]{4,3,2,1,0:T(8,128)S(1)} %copy-done.8, f32[6,2,3,4,1,16,128]{6,5,4,3,2,1,0:T(8,128)S(1)} %copy-done.1), custom_call_target="tpu_custom_call" | custom-call | tf_op jit(solution)/shard_map/pallas_call | solution.py:522
  23.6 9.2 %all-to-all-done.in_ref = f32[32,8,128]{2,1,0:T(8,128)S(1)} async-done(((f32[32,8,128]{2,1,0:T(8,128)}), f32[32,8,128]{2,1,0:T(8,128)S(1)}, u32[]{:S(2)}, u32[]{:S(2)}) %all-to-all-start) | async-done | bytes 131104 | tf_op jit(solution)/shard_map/all_to_all | solution.py:603
  32.8 1.4 %shard_map.106.after_ref = f32[512,128]{1,0:T(8,128)} custom-call(f32[32,8,128]{2,1,0:T(8,128)S(1)} %all-to-all-done.in_ref, f32[352,256]{1,0:T(8,128)S(1)} %copy-done.5, f32[2,8,512]{2,1,0:T(8,128)S(1)} %get-tuple-element.16.after_ref.weight_ref, f32[3,2,2,8,512]{4,3,2,1,0:T(8,128)S(1)} %get-tuple-element.17.also_ref.past_ref), custom_call_target="tpu_custom_call" | custom-call | tf_op jit(solution)/shard_map/pallas_call | solution.py:522
  34.1 11.4 %all-to-all-start.1 = ((f32[512,1,128]{2,1,0:T(1,128)}), f32[512,1,128]{2,1,0:T(1,128)S(1)}, u32[]{:S(2)}, u32[]{:S(2)}) async-start(f32[512,1,128]{2,1,0:T(1,128)} %bitcast.1), calls=%async_computation.1 | async-start | bytes 524288 | tf_op jit(solution)/shard_map/all_to_all | solution.py:608
  45.5 0.9 shard_map.107
  46.4 0.0 copy-start.7
  46.5 3.8 %collective-permute-start = (f32[64,128]{1,0:T(8,128)S(1)}, f32[64,128]{1,0:T(8,128)S(1)}, u32[]{:S(2)}, u32[]{:S(2)}) collective-permute-start(f32[64,128]{1,0:T(8,128)S(1)} %get-tuple-element.18.own_yhi_ref), channel_id=1, source_target_pairs={{0,1},{1,2},{2,3},{3,4},{4,5},{5,6},{6,7},{7,8},{8,9},{9,10},{10,1... | collective-permute-start | bytes 98312 | tf_op jit(solution)/shard_map/ppermute | solution.py:597
  50.3 7.0 %collective-permute-start.1 = (f32[64,128]{1,0:T(8,128)S(1)}, f32[64,128]{1,0:T(8,128)S(1)}, u32[]{:S(2)}, u32[]{:S(2)}) collective-permute-start(f32[64,128]{1,0:T(8,128)S(1)} %get-tuple-element.19.own_ylo_ref), channel_id=1, source_target_pairs={{0,15},{1,0},{2,1},{3,2},{4,3},{5,4},{6,5},{7,6},{8,7},{9,8},{10,9... | collective-permute-start | bytes 98312 | tf_op jit(solution)/shard_map/ppermute | solution.py:598
  57.2 0.5 collective-permute-done.after_ref.ylo_ref
  57.8 0.5 collective-permute-done.1.also_ref.yhi_ref
  58.3 4.5 %all-to-all-done.1 = f32[512,1,128]{2,1,0:T(1,128)S(1)} async-done(((f32[512,1,128]{2,1,0:T(1,128)}), f32[512,1,128]{2,1,0:T(1,128)S(1)}, u32[]{:S(2)}, u32[]{:S(2)}) %all-to-all-start.1) | async-done | bytes 262176 | tf_op jit(solution)/shard_map/all_to_all | solution.py:608
  62.7 1.8 %shard_map.108.after_ref = f32[512,128]{1,0:T(8,128)} custom-call(f32[512,128]{1,0:T(8,128)S(1)} %bitcast.9, f32[2,8,512]{2,1,0:T(8,128)S(1)} %get-tuple-element.16.after_ref.weight_ref, f32[3,2,2,8,512]{4,3,2,1,0:T(8,128)S(1)} %get-tuple-element.17.also_ref.past_ref, f32[328,256]{1,0:T(8,128)S(1)} %copy-done.6, ...), custom_call_target="tpu_custom_call" | custom-call | tf_op jit(solution)/shard_map/pallas_call | solution.py:522
  64.6 15.1 %all-to-all-start.2 = ((f32[512,1,128]{2,1,0:T(1,128)}), f32[512,1,128]{2,1,0:T(1,128)S(1)}, u32[]{:S(2)}, u32[]{:S(2)}) async-start(f32[512,1,128]{2,1,0:T(1,128)} %bitcast.4), calls=%async_computation.2 | async-start | bytes 524288 | tf_op jit(solution)/shard_map/all_to_all | solution.py:608
  79.7 0.0 copy-start.3
  79.7 0.0 copy-start.9
  79.7 0.1 shard_map.109
  79.8 3.5 %collective-permute-start.2 = (f32[32,128]{1,0:T(8,128)S(1)}, f32[32,128]{1,0:T(8,128)S(1)}, u32[]{:S(2)}, u32[]{:S(2)}) collective-permute-start(f32[32,128]{1,0:T(8,128)S(1)} %get-tuple-element.22), channel_id=1, source_target_pairs={{0,16},{16,32},{32,48},{48,64},{64,80},{80,96},{96,112},{112,128},... | collective-permute-start | bytes 49160 | tf_op jit(solution)/shard_map/ppermute | solution.py:597
  83.4 4.6 %collective-permute-start.3 = (f32[32,128]{1,0:T(8,128)S(1)}, f32[32,128]{1,0:T(8,128)S(1)}, u32[]{:S(2)}, u32[]{:S(2)}) collective-permute-start(f32[32,128]{1,0:T(8,128)S(1)} %get-tuple-element.23), channel_id=1, source_target_pairs={{0,496},{16,0},{32,16},{48,32},{64,48},{80,64},{96,80},{112,96},{1... | collective-permute-start | bytes 49160 | tf_op jit(solution)/shard_map/ppermute | solution.py:598
  88.0 0.8 collective-permute-done.3.also_ref.xhi_ref
  88.8 8.1 %all-to-all-done.2 = f32[512,1,128]{2,1,0:T(1,128)S(1)} async-done(((f32[512,1,128]{2,1,0:T(1,128)}), f32[512,1,128]{2,1,0:T(1,128)S(1)}, u32[]{:S(2)}, u32[]{:S(2)}) %all-to-all-start.2) | async-done | bytes 262176 | tf_op jit(solution)/shard_map/all_to_all | solution.py:608
  96.9 1.5 %shard_map.110.after_ref = f32[32,8,128]{2,1,0:T(8,128)} custom-call(f32[512,128]{1,0:T(8,128)S(1)} %bitcast.8, f32[320,256]{1,0:T(8,128)S(1)} %copy-done.7, f32[32,128]{1,0:T(8,128)S(1)} %collective-permute-done.2.after_ref.xlo_ref, f32[32,128]{1,0:T(8,128)S(1)} %collective-permute-done.3.also_ref.xhi_ref), custom_call_target="tpu_custom_call" | custom-call | tf_op jit(solution)/shard_map/pallas_call | solution.py:522
  98.3 9.4 %all-to-all-start.3 = ((f32[32,8,128]{2,1,0:T(8,128)}), f32[32,8,128]{2,1,0:T(8,128)S(1)}, u32[]{:S(2)}, u32[]{:S(2)}) async-start(f32[32,8,128]{2,1,0:T(8,128)} %shard_map.110.after_ref), calls=%async_computation.3 | async-start | bytes 262144 | tf_op jit(solution)/shard_map/all_to_all | solution.py:603
  107.8 0.3 shard_map.111
  108.1 12.7 %all-to-all-done.3.in_ref = f32[32,8,128]{2,1,0:T(8,128)S(1)} async-done(((f32[32,8,128]{2,1,0:T(8,128)}), f32[32,8,128]{2,1,0:T(8,128)S(1)}, u32[]{:S(2)}, u32[]{:S(2)}) %all-to-all-start.3) | async-done | bytes 131104 | tf_op jit(solution)/shard_map/all_to_all | solution.py:603
  120.7 1.8 %shard_map.112 = (f32[3,4,64,128]{3,2,1,0:T(8,128)}, f32[6,4,64,128]{3,2,1,0:T(8,128)}) custom-call(f32[32,8,128]{2,1,0:T(8,128)S(1)} %all-to-all-done.3.in_ref, f32[3,4,64,128]{3,2,1,0:T(8,128)S(1)} %get-tuple-element.25.before_ref, f32[6,4,64,128]{3,2,1,0:T(8,128)S(1)} %copy-done, f32[4,64,128]{2,1,0:T(8,128)S(1)} %copy-done.9, ...), custom_call_target="tpu_custom_call" | custom-call | tf_op jit(solution)/shard_map/pallas_call | solution.py:522
  (13 shorter events, 0.0 us)
Async XLA Ops:
  0.6 0.9 copy-start.2
  1.5 31.2 %copy-start.5 = (f32[352,256]{1,0:T(8,128)S(1)}, f32[352,256]{1,0:T(8,128)}, u32[]{:S(2)}) copy-start(f32[352,256]{1,0:T(8,128)} %constant.6.clone.table_ref) | copy-start | bytes 1081348
  2.6 30.2 %all-to-all-start = ((f32[32,8,128]{2,1,0:T(8,128)}), f32[32,8,128]{2,1,0:T(8,128)S(1)}, u32[]{:S(2)}, u32[]{:S(2)}) async-start(f32[32,8,128]{2,1,0:T(8,128)} %shard_map.104), calls=%async_computation | async-start | bytes 262144 | tf_op jit(solution)/shard_map/all_to_all | solution.py:603
  19.8 1.3 %copy-start.1 = (f32[6,2,3,4,1,16,128]{6,5,4,3,2,1,0:T(8,128)S(1)}, f32[6,2,3,4,1,16,128]{6,5,4,3,2,1,0:T(8,128)}, u32[]{:S(2)}) copy-start(f32[6,2,3,4,1,16,128]{6,5,4,3,2,1,0:T(8,128)} %history_hbm.1) | copy-start | bytes 3538948
  21.1 0.9 copy-start.8
  22.0 23.5 %copy-start = (f32[6,4,64,128]{3,2,1,0:T(8,128)S(1)}, f32[6,4,64,128]{3,2,1,0:T(8,128)}, u32[]{:S(2)}) copy-start(f32[6,4,64,128]{3,2,1,0:T(8,128)} %stress_ref.3) | copy-start | bytes 2359300
  22.0 23.5 %copy-start.4 = (f32[3,4,64,128]{3,2,1,0:T(8,128)S(1)}, f32[3,4,64,128]{3,2,1,0:T(8,128)}, u32[]{:S(2)}) copy-start(f32[3,4,64,128]{3,2,1,0:T(8,128)} %velocity_ref.1) | copy-start | bytes 1179652
  34.1 28.6 %copy-start.6 = (f32[328,256]{1,0:T(8,128)S(1)}, f32[328,256]{1,0:T(8,128)}, u32[]{:S(2)}) copy-start(f32[328,256]{1,0:T(8,128)} %constant.7.clone.table_ref) | copy-start | bytes 1007620
  34.1 28.6 %all-to-all-start.1 = ((f32[512,1,128]{2,1,0:T(1,128)}), f32[512,1,128]{2,1,0:T(1,128)S(1)}, u32[]{:S(2)}, u32[]{:S(2)}) async-start(f32[512,1,128]{2,1,0:T(1,128)} %bitcast.1), calls=%async_computation.1 | async-start | bytes 524288 | tf_op jit(solution)/shard_map/all_to_all | solution.py:608
  46.4 50.4 %copy-start.7 = (f32[320,256]{1,0:T(8,128)S(1)}, f32[320,256]{1,0:T(8,128)}, u32[]{:S(2)}) copy-start(f32[320,256]{1,0:T(8,128)} %constant.8.clone.table_ref) | copy-start | bytes 983044
  46.5 11.3 %collective-permute-start = (f32[64,128]{1,0:T(8,128)S(1)}, f32[64,128]{1,0:T(8,128)S(1)}, u32[]{:S(2)}, u32[]{:S(2)}) collective-permute-start(f32[64,128]{1,0:T(8,128)S(1)} %get-tuple-element.18.own_yhi_ref), channel_id=1, source_target_pairs={{0,1},{1,2},{2,3},{3,4},{4,5},{5,6},{6,7},{7,8},{8,9},{9,10},{10,1... | collective-permute-start | bytes 98312 | tf_op jit(solution)/shard_map/ppermute | solution.py:597
  50.3 8.0 %collective-permute-start.1 = (f32[64,128]{1,0:T(8,128)S(1)}, f32[64,128]{1,0:T(8,128)S(1)}, u32[]{:S(2)}, u32[]{:S(2)}) collective-permute-start(f32[64,128]{1,0:T(8,128)S(1)} %get-tuple-element.19.own_ylo_ref), channel_id=1, source_target_pairs={{0,15},{1,0},{2,1},{3,2},{4,3},{5,4},{6,5},{7,6},{8,7},{9,8},{10,9... | collective-permute-start | bytes 98312 | tf_op jit(solution)/shard_map/ppermute | solution.py:598
  64.6 32.3 %all-to-all-start.2 = ((f32[512,1,128]{2,1,0:T(1,128)}), f32[512,1,128]{2,1,0:T(1,128)S(1)}, u32[]{:S(2)}, u32[]{:S(2)}) async-start(f32[512,1,128]{2,1,0:T(1,128)} %bitcast.4), calls=%async_computation.2 | async-start | bytes 524288 | tf_op jit(solution)/shard_map/all_to_all | solution.py:608
  79.7 41.1 %copy-start.3 = (f32[3,64,128]{2,1,0:T(8,128)S(1)}, f32[3,64,128]{2,1,0:T(8,128)}, u32[]{:S(2)}) copy-start(f32[3,64,128]{2,1,0:T(8,128)} %iv_ref.3) | copy-start | bytes 294916
  79.7 41.1 %copy-start.9 = (f32[4,64,128]{2,1,0:T(8,128)S(1)}, f32[4,64,128]{2,1,0:T(8,128)}, u32[]{:S(2)}) copy-start(f32[4,64,128]{2,1,0:T(8,128)} %cohesion_ref.1) | copy-start | bytes 393220
  79.8 8.1 %collective-permute-start.2 = (f32[32,128]{1,0:T(8,128)S(1)}, f32[32,128]{1,0:T(8,128)S(1)}, u32[]{:S(2)}, u32[]{:S(2)}) collective-permute-start(f32[32,128]{1,0:T(8,128)S(1)} %get-tuple-element.22), channel_id=1, source_target_pairs={{0,16},{16,32},{32,48},{48,64},{64,80},{80,96},{96,112},{112,128},... | collective-permute-start | bytes 49160 | tf_op jit(solution)/shard_map/ppermute | solution.py:597
  83.4 5.4 %collective-permute-start.3 = (f32[32,128]{1,0:T(8,128)S(1)}, f32[32,128]{1,0:T(8,128)S(1)}, u32[]{:S(2)}, u32[]{:S(2)}) collective-permute-start(f32[32,128]{1,0:T(8,128)S(1)} %get-tuple-element.23), channel_id=1, source_target_pairs={{0,496},{16,0},{32,16},{48,32},{64,48},{80,64},{96,80},{112,96},{1... | collective-permute-start | bytes 49160 | tf_op jit(solution)/shard_map/ppermute | solution.py:598
  98.3 22.4 %all-to-all-start.3 = ((f32[32,8,128]{2,1,0:T(8,128)}), f32[32,8,128]{2,1,0:T(8,128)S(1)}, u32[]{:S(2)}, u32[]{:S(2)}) async-start(f32[32,8,128]{2,1,0:T(8,128)} %shard_map.110.after_ref), calls=%async_computation.3 | async-start | bytes 262144 | tf_op jit(solution)/shard_map/all_to_all | solution.py:603

commit v8 on v7

--- a/solution.py
+++ b/solution.py
@@ -182,7 +182,7 @@
             out_ref[32 * (8 * t + b) : 32 * (8 * t + b + 1), :] = parts[b]
 
 
-def strike_inverse_kernel(in_ref, table_ref, after_ref, also_ref, out_ref):
+def strike_inverse_kernel(in_ref, table_ref, out_ref):
     columns = []
     for t in range(2):
         columns.append(
@@ -539,9 +539,8 @@
     return call(strike_forward_kernel, f32(512, 128), arguments, after)
 
 
-def strike_inverse(arrived, after):
-    arguments = (arrived, strike_tables(True))
-    return call(strike_inverse_kernel, f32(32, 8, 128), arguments, after)
+def strike_inverse(arrived):
+    return call(strike_inverse_kernel, f32(32, 8, 128), (arrived, strike_tables(True)))
 
 
 def dip(arrived, weight, past, after):
@@ -619,9 +618,9 @@
     columns = exchange("by", *own_columns)
     sent = dip(arrived, weight, past, columns)
     arrived = whole_swap(sent)
+    sent = strike_inverse(arrived)
+    arrived = strike_swap(sent)
     rows = exchange("bx", *velocity_columns(own_rows, columns, sent))
-    sent = strike_inverse(arrived, rows)
-    arrived = strike_swap(sent)
     before, *halo = velocity_rows(part, (*rows, *columns), (*own_rows, *own_columns), sent)
     return slab(arrived, before, stress, cohesion, interface_velocity, halo)
 

time: 123 us -> 122 us (level)
  the two profiles are of different devices: /device:TPU:1 before, /device:TPU:57 now
where the time goes in v8:
time: 122 us; the launch traced here: 121 us
  starting transfers between devices  55.9 us (46%)
  blocking collectives  32.2 us (26%)
  waiting for transfers between devices  19.6 us (16%)
  Pallas kernels  9.64 us (8%)
  local copies, waits for them, and re-layouts  3.13 us (3%)
    all_to_all x1, blocking collectives, whole_swap(): lax.all_to_all(value, ('by', 'bx'), split_axis=0, concat_axis=0, tiled=True)  32.2 us
    all_to_all x2, starting transfers between devices, strike_swap(): return lax.all_to_all(value, 'bx', split_axis=0, concat_axis=0, tiled=True)  22.6 us
    all_to_all x1, starting transfers between devices, whole_swap(): lax.all_to_all(value, ('by', 'bx'), split_axis=0, concat_axis=0, tiled=True)  13.4 us
    ppermute x2, starting transfers between devices, exchange(): lax.ppermute(high, axis, [(i, (i + 1) % count) for i in range(count)])  11 us
    ppermute x2, waiting for transfers between devices, exchange(): lax.ppermute(low, axis, [(i, (i - 1) % count) for i in range(count)])  9.68 us
    pallas_call x9, Pallas kernels, call(): pl.pallas_call(kernel, out_shape=out_shape, in_specs=[VMEM] * len(argumen...  9.64 us
    ppermute x2, starting transfers between devices, exchange(): lax.ppermute(low, axis, [(i, (i - 1) % count) for i in range(count)])  8.88 us
    all_to_all x2, waiting for transfers between devices, strike_swap(): return lax.all_to_all(value, 'bx', split_axis=0, concat_axis=0, tiled=True)  7.5 us
  transfers between devices with their start and end apart: 7, of which 5 were waited for; matrix products, arithmetic and copies ran while one was open for 0% of the time, Pallas kernels for 2%

profile of v8, /device:TPU:57, one launch (start us, length us, event | category | flops | bytes accessed | tf_op | source)
XLA Modules:
  0.0 121.2 jit_solution(4412960138266116069)
XLA Ops:
  0.6 0.0 copy-start.2
  0.6 0.9 copy-done.2
  1.5 1.0 shard_map.104
  2.6 15.8 %all-to-all-start = ((f32[32,8,128]{2,1,0:T(8,128)}), f32[32,8,128]{2,1,0:T(8,128)S(1)}, u32[]{:S(2)}, u32[]{:S(2)}) async-start(f32[32,8,128]{2,1,0:T(8,128)} %shard_map.104), calls=%async_computation | async-start | bytes 262144 | tf_op jit(solution)/shard_map/all_to_all | solution.py:602
  18.4 0.0 copy-start.1
  18.4 1.3 %copy-done.1 = f32[6,2,3,4,1,16,128]{6,5,4,3,2,1,0:T(8,128)S(1)} copy-done((f32[6,2,3,4,1,16,128]{6,5,4,3,2,1,0:T(8,128)S(1)}, f32[6,2,3,4,1,16,128]{6,5,4,3,2,1,0:T(8,128)}, u32[]{:S(2)}) %copy-start.1) | copy-done | bytes 1179672
  19.6 0.9 copy-done.8
  20.6 1.6 %shard_map.105 = (f32[2,8,512]{2,1,0:T(8,128)S(1)}, f32[3,2,2,8,512]{4,3,2,1,0:T(8,128)S(1)}) custom-call(f32[7,4,1,16,128]{4,3,2,1,0:T(8,128)S(1)} %copy-done.8, f32[6,2,3,4,1,16,128]{6,5,4,3,2,1,0:T(8,128)S(1)} %copy-done.1), custom_call_target="tpu_custom_call" | custom-call | tf_op jit(solution)/shard_map/pallas_call | solution.py:522
  22.1 7.5 %all-to-all-done.in_ref = f32[32,8,128]{2,1,0:T(8,128)S(1)} async-done(((f32[32,8,128]{2,1,0:T(8,128)}), f32[32,8,128]{2,1,0:T(8,128)S(1)}, u32[]{:S(2)}, u32[]{:S(2)}) %all-to-all-start) | async-done | bytes 131104 | tf_op jit(solution)/shard_map/all_to_all | solution.py:602
  29.6 1.4 %shard_map.106.after_ref = f32[512,128]{1,0:T(8,128)} custom-call(f32[32,8,128]{2,1,0:T(8,128)S(1)} %all-to-all-done.in_ref, f32[352,256]{1,0:T(8,128)S(1)} %copy-done.5, f32[2,8,512]{2,1,0:T(8,128)S(1)} %get-tuple-element.16.after_ref.weight_ref, f32[3,2,2,8,512]{4,3,2,1,0:T(8,128)S(1)} %get-tuple-element.17.also_ref.past_ref), custom_call_target="tpu_custom_call" | custom-call | tf_op jit(solution)/shard_map/pallas_call | solution.py:522
  31.0 13.4 %all-to-all-start.1 = ((f32[512,1,128]{2,1,0:T(1,128)}), f32[512,1,128]{2,1,0:T(1,128)S(1)}, u32[]{:S(2)}, u32[]{:S(2)}) async-start(f32[512,1,128]{2,1,0:T(1,128)} %bitcast.1), calls=%async_computation.1 | async-start | bytes 524288 | tf_op jit(solution)/shard_map/all_to_all | solution.py:607
  44.4 0.9 shard_map.107
  45.3 0.0 copy-start.7
  45.4 3.8 %collective-permute-start = (f32[64,128]{1,0:T(8,128)S(1)}, f32[64,128]{1,0:T(8,128)S(1)}, u32[]{:S(2)}, u32[]{:S(2)}) collective-permute-start(f32[64,128]{1,0:T(8,128)S(1)} %get-tuple-element.18.own_yhi_ref), channel_id=1, source_target_pairs={{0,1},{1,2},{2,3},{3,4},{4,5},{5,6},{6,7},{7,8},{8,9},{9,10},{10,1... | collective-permute-start | bytes 98312 | tf_op jit(solution)/shard_map/ppermute | solution.py:596
  49.1 7.0 %collective-permute-start.1 = (f32[64,128]{1,0:T(8,128)S(1)}, f32[64,128]{1,0:T(8,128)S(1)}, u32[]{:S(2)}, u32[]{:S(2)}) collective-permute-start(f32[64,128]{1,0:T(8,128)S(1)} %get-tuple-element.19.own_ylo_ref), channel_id=1, source_target_pairs={{0,15},{1,0},{2,1},{3,2},{4,3},{5,4},{6,5},{7,6},{8,7},{9,8},{10,9... | collective-permute-start | bytes 98312 | tf_op jit(solution)/shard_map/ppermute | solution.py:597
  56.1 0.5 collective-permute-done.after_ref.ylo_ref
  56.6 0.5 collective-permute-done.1.also_ref.yhi_ref
  57.1 1.9 %all-to-all-done.1 = f32[512,1,128]{2,1,0:T(1,128)S(1)} async-done(((f32[512,1,128]{2,1,0:T(1,128)}), f32[512,1,128]{2,1,0:T(1,128)S(1)}, u32[]{:S(2)}, u32[]{:S(2)}) %all-to-all-start.1) | async-done | bytes 262176 | tf_op jit(solution)/shard_map/all_to_all | solution.py:607
  59.0 1.1 shard_map.108
  60.2 0.0 copy-start.3
  60.2 0.0 copy-start.9
  60.2 32.2 %all_to_all.20 = f32[512,1,128]{2,1,0:T(1,128)S(1)} all-to-all(f32[512,1,128]{2,1,0:T(1,128)S(1)} %bitcast.9), channel_id=1, replica_groups=mesh['bx'=32,'by'=16] {'by','bx'}, dimensions={0} | all-to-all | bytes 524288 | tf_op jit(solution)/shard_map/all_to_all | solution.py:607
  92.4 1.5 %shard_map.109.after_ref = f32[32,8,128]{2,1,0:T(8,128)} custom-call(f32[512,128]{1,0:T(8,128)S(1)} %bitcast.10, f32[320,256]{1,0:T(8,128)S(1)} %copy-done.7), custom_call_target="tpu_custom_call" | custom-call | tf_op jit(solution)/shard_map/pallas_call | solution.py:522
  93.8 6.9 %all-to-all-start.3 = ((f32[32,8,128]{2,1,0:T(8,128)}), f32[32,8,128]{2,1,0:T(8,128)S(1)}, u32[]{:S(2)}, u32[]{:S(2)}) async-start(f32[32,8,128]{2,1,0:T(8,128)} %shard_map.109.after_ref), calls=%async_computation.3 | async-start | bytes 262144 | tf_op jit(solution)/shard_map/all_to_all | solution.py:602
  100.7 0.1 shard_map.110
  100.8 7.2 %collective-permute-start.2 = (f32[32,128]{1,0:T(8,128)S(1)}, f32[32,128]{1,0:T(8,128)S(1)}, u32[]{:S(2)}, u32[]{:S(2)}) collective-permute-start(f32[32,128]{1,0:T(8,128)S(1)} %get-tuple-element.23), channel_id=1, source_target_pairs={{0,16},{16,32},{32,48},{48,64},{64,80},{80,96},{96,112},{112,128},... | collective-permute-start | bytes 49160 | tf_op jit(solution)/shard_map/ppermute | solution.py:596
  108.1 1.9 %collective-permute-start.3 = (f32[32,128]{1,0:T(8,128)S(1)}, f32[32,128]{1,0:T(8,128)S(1)}, u32[]{:S(2)}, u32[]{:S(2)}) collective-permute-start(f32[32,128]{1,0:T(8,128)S(1)} %get-tuple-element.24), channel_id=1, source_target_pairs={{0,496},{16,0},{32,16},{48,32},{64,48},{80,64},{96,80},{112,96},{1... | collective-permute-start | bytes 49160 | tf_op jit(solution)/shard_map/ppermute | solution.py:597
  110.0 0.0 collective-permute-done.2.xlo_ref
  110.0 9.1 %collective-permute-done.3.xhi_ref = f32[32,128]{1,0:T(8,128)S(1)} collective-permute-done((f32[32,128]{1,0:T(8,128)S(1)}, f32[32,128]{1,0:T(8,128)S(1)}, u32[]{:S(2)}, u32[]{:S(2)}) %collective-permute-start.3) | collective-permute-done | bytes 16416 | tf_op jit(solution)/shard_map/ppermute | solution.py:597
  119.1 0.3 shard_map.111
  119.4 0.0 all-to-all-done.3.in_ref
  119.4 1.8 %shard_map.112 = (f32[3,4,64,128]{3,2,1,0:T(8,128)}, f32[6,4,64,128]{3,2,1,0:T(8,128)}) custom-call(f32[32,8,128]{2,1,0:T(8,128)S(1)} %all-to-all-done.3.in_ref, f32[3,4,64,128]{3,2,1,0:T(8,128)S(1)} %get-tuple-element.25.before_ref, f32[6,4,64,128]{3,2,1,0:T(8,128)S(1)} %copy-done, f32[4,64,128]{2,1,0:T(8,128)S(1)} %copy-done.9, ...), custom_call_target="tpu_custom_call" | custom-call | tf_op jit(solution)/shard_map/pallas_call | solution.py:522
  (12 shorter events, 0.0 us)
Async XLA Ops:
  0.6 0.9 copy-start.2
  1.5 28.1 %copy-start.5 = (f32[352,256]{1,0:T(8,128)S(1)}, f32[352,256]{1,0:T(8,128)}, u32[]{:S(2)}) copy-start(f32[352,256]{1,0:T(8,128)} %constant.6.clone.table_ref) | copy-start | bytes 1081348
  2.6 27.1 %all-to-all-start = ((f32[32,8,128]{2,1,0:T(8,128)}), f32[32,8,128]{2,1,0:T(8,128)S(1)}, u32[]{:S(2)}, u32[]{:S(2)}) async-start(f32[32,8,128]{2,1,0:T(8,128)} %shard_map.104), calls=%async_computation | async-start | bytes 262144 | tf_op jit(solution)/shard_map/all_to_all | solution.py:602
  18.4 1.3 %copy-start.1 = (f32[6,2,3,4,1,16,128]{6,5,4,3,2,1,0:T(8,128)S(1)}, f32[6,2,3,4,1,16,128]{6,5,4,3,2,1,0:T(8,128)}, u32[]{:S(2)}) copy-start(f32[6,2,3,4,1,16,128]{6,5,4,3,2,1,0:T(8,128)} %history_hbm.1) | copy-start | bytes 3538948
  19.6 0.9 copy-start.8
  20.6 23.8 %copy-start = (f32[6,4,64,128]{3,2,1,0:T(8,128)S(1)}, f32[6,4,64,128]{3,2,1,0:T(8,128)}, u32[]{:S(2)}) copy-start(f32[6,4,64,128]{3,2,1,0:T(8,128)} %stress_ref.3) | copy-start | bytes 2359300
  20.6 23.8 %copy-start.4 = (f32[3,4,64,128]{3,2,1,0:T(8,128)S(1)}, f32[3,4,64,128]{3,2,1,0:T(8,128)}, u32[]{:S(2)}) copy-start(f32[3,4,64,128]{3,2,1,0:T(8,128)} %velocity_ref.1) | copy-start | bytes 1179652
  31.0 28.0 %copy-start.6 = (f32[328,256]{1,0:T(8,128)S(1)}, f32[328,256]{1,0:T(8,128)}, u32[]{:S(2)}) copy-start(f32[328,256]{1,0:T(8,128)} %constant.7.clone.table_ref) | copy-start | bytes 1007620
  31.0 28.0 %all-to-all-start.1 = ((f32[512,1,128]{2,1,0:T(1,128)}), f32[512,1,128]{2,1,0:T(1,128)S(1)}, u32[]{:S(2)}, u32[]{:S(2)}) async-start(f32[512,1,128]{2,1,0:T(1,128)} %bitcast.1), calls=%async_computation.1 | async-start | bytes 524288 | tf_op jit(solution)/shard_map/all_to_all | solution.py:607
  45.3 47.0 %copy-start.7 = (f32[320,256]{1,0:T(8,128)S(1)}, f32[320,256]{1,0:T(8,128)}, u32[]{:S(2)}) copy-start(f32[320,256]{1,0:T(8,128)} %constant.8.clone.table_ref) | copy-start | bytes 983044
  45.4 11.2 %collective-permute-start = (f32[64,128]{1,0:T(8,128)S(1)}, f32[64,128]{1,0:T(8,128)S(1)}, u32[]{:S(2)}, u32[]{:S(2)}) collective-permute-start(f32[64,128]{1,0:T(8,128)S(1)} %get-tuple-element.18.own_yhi_ref), channel_id=1, source_target_pairs={{0,1},{1,2},{2,3},{3,4},{4,5},{5,6},{6,7},{7,8},{8,9},{9,10},{10,1... | collective-permute-start | bytes 98312 | tf_op jit(solution)/shard_map/ppermute | solution.py:596
  49.1 8.0 %collective-permute-start.1 = (f32[64,128]{1,0:T(8,128)S(1)}, f32[64,128]{1,0:T(8,128)S(1)}, u32[]{:S(2)}, u32[]{:S(2)}) collective-permute-start(f32[64,128]{1,0:T(8,128)S(1)} %get-tuple-element.19.own_ylo_ref), channel_id=1, source_target_pairs={{0,15},{1,0},{2,1},{3,2},{4,3},{5,4},{6,5},{7,6},{8,7},{9,8},{10,9... | collective-permute-start | bytes 98312 | tf_op jit(solution)/shard_map/ppermute | solution.py:597
  60.2 59.3 %copy-start.3 = (f32[3,64,128]{2,1,0:T(8,128)S(1)}, f32[3,64,128]{2,1,0:T(8,128)}, u32[]{:S(2)}) copy-start(f32[3,64,128]{2,1,0:T(8,128)} %iv_ref.3) | copy-start | bytes 294916
  60.2 59.3 %copy-start.9 = (f32[4,64,128]{2,1,0:T(8,128)S(1)}, f32[4,64,128]{2,1,0:T(8,128)}, u32[]{:S(2)}) copy-start(f32[4,64,128]{2,1,0:T(8,128)} %cohesion_ref.1) | copy-start | bytes 393220
  93.8 25.6 %all-to-all-start.3 = ((f32[32,8,128]{2,1,0:T(8,128)}), f32[32,8,128]{2,1,0:T(8,128)S(1)}, u32[]{:S(2)}, u32[]{:S(2)}) async-start(f32[32,8,128]{2,1,0:T(8,128)} %shard_map.109.after_ref), calls=%async_computation.3 | async-start | bytes 262144 | tf_op jit(solution)/shard_map/all_to_all | solution.py:602
  100.8 9.2 %collective-permute-start.2 = (f32[32,128]{1,0:T(8,128)S(1)}, f32[32,128]{1,0:T(8,128)S(1)}, u32[]{:S(2)}, u32[]{:S(2)}) collective-permute-start(f32[32,128]{1,0:T(8,128)S(1)} %get-tuple-element.23), channel_id=1, source_target_pairs={{0,16},{16,32},{32,48},{48,64},{64,80},{80,96},{96,112},{112,128},... | collective-permute-start | bytes 49160 | tf_op jit(solution)/shard_map/ppermute | solution.py:596
  108.1 11.1 %collective-permute-start.3 = (f32[32,128]{1,0:T(8,128)S(1)}, f32[32,128]{1,0:T(8,128)S(1)}, u32[]{:S(2)}, u32[]{:S(2)}) collective-permute-start(f32[32,128]{1,0:T(8,128)S(1)} %get-tuple-element.24), channel_id=1, source_target_pairs={{0,496},{16,0},{32,16},{48,32},{64,48},{80,64},{96,80},{112,96},{1... | collective-permute-start | bytes 49160 | tf_op jit(solution)/shard_map/ppermute | solution.py:597
